TPU v7x, 32 devices: a whole 2x2x4 slice. The times are simulated.
32 devices in a mesh: leaf: 8 (over z, y), level: 4 (over x, core).
Axes of the slice: x: 2, y: 2, z: 4, core: 2. Of those that a mesh axis runs over, the one named last changes fastest.
Arguments:
- points_x: bfloat16 [256, 16384], P(None, ('leaf', 'level')), may hold values from -6 to 6
- leaf_basis: bfloat16 [32, 512, 256], P(('leaf', 'level')), may hold values from -0.25 to 0.25
- near_tiles: bfloat16 [32, 4, 512, 512], P(('leaf', 'level')), may hold values from -0.25 to 0.25
- near_cols: int32 [32, 4], P(('leaf', 'level')), may hold values from 0 to 11, as said below
- near_count: int32 [32], P(('leaf', 'level')), may hold values from 3 to 4, as said below
- transfer: bfloat16 [2, 256, 256], replicated, may hold values from -0.3125 to 0.3125
- coupling: bfloat16 [6, 2, 256, 256], replicated, may hold values from -0.375 to 0.375
- couple_mask: int32 [6, 8, 2], replicated, may hold values 0 or 1
Outputs:
- kernel_product: bfloat16 [256, 16384], P(None, ('leaf', 'level'))
Inputs may be any that keep to these rules, and one draw needn't show every extreme that they name: Slots 0, 1 and 2 of leaf L name L itself, L - 1 and L + 1 (near_cols 4 + L mod 4, one less, one more); slot 3 names any leaf of the previous, own or next group; some leaf's slot 3 names 0 and some names 11. The live slots of a leaf are its first near_count slots; in every draw some leaf has 3 and some has 4 live slots.
All inputs are finite; a program needn't handle non-finite values.
Results may differ from a plain program's by a relative error of at most 0.015.
Values may be sent and summed in bfloat16 or wider, within the bound.
No kernel may reach another device: no remote copies, remote signals or barrier semaphores. Data moves between devices by JAX's collectives and lax.ppermute only.
A program may use at most 64 MiB of HBM per device.

v0:
```python
from functools import partial

import jax
import jax.numpy as jnp
from jax import lax
from jax.experimental import pallas as pl
from jax.experimental.pallas import tpu as pltpu
from jax.sharding import PartitionSpec as P

VMEM_LIMIT = 32 * 1024 * 1024
F32 = jnp.float32
BF16 = jnp.bfloat16
GROUP = 4
SLOT = 3
TAIL = 16


def dot(a, b):
    return jnp.dot(a, b, preferred_element_type=F32)


def dot_t(a, b):
    return lax.dot_general(a, b, (((1,), (1,)), ((), ())), preferred_element_type=F32)


def call(kernel, name, inputs, scalars, outputs, scratch=(), inputs_in=pltpu.VMEM):
    shapes = [jax.ShapeDtypeStruct(shape, dtype) for shape, dtype in outputs]
    return pl.pallas_call(
        kernel,
        out_shape=shapes,
        in_specs=[pl.BlockSpec(memory_space=inputs_in)] * len(inputs)
        + [pl.BlockSpec(memory_space=pltpu.SMEM)] * len(scalars),
        out_specs=[pl.BlockSpec(memory_space=pltpu.VMEM)] * len(outputs),
        scratch_shapes=list(scratch),
        compiler_params=pltpu.CompilerParams(vmem_limit_bytes=VMEM_LIMIT),
        cost_estimate=pl.CostEstimate(flops=0, bytes_accessed=0, transcendentals=0),
        name=name,
    )(*(pltpu.with_memory_space_constraint(a, inputs_in) for a in inputs), *scalars)


def up_kernel(
    bits, x_hbm, basis_hbm, transfer_hbm, coupling_hbm, cols_hbm,
    keep_ref, send_ref, w_ref, x_ref, transfer_ref, coupling_ref, basis_ref, z_ref, cols_ref, sems
):
    pos = lax.axis_index("level")
    chip, core = pos >> 1, pos & 1
    pairs = (
        (basis_hbm.at[0], basis_ref), (transfer_hbm, transfer_ref), (x_hbm, x_ref),
        (coupling_hbm.at[:2], coupling_ref), (cols_hbm, cols_ref),
    )
    copies = [pltpu.make_async_copy(a, b, sems.at[i]) for i, (a, b) in enumerate(pairs)]
    for copy in copies:
        copy.start()
    copies[0].wait()
    copies[1].wait()
    w = basis_ref[...]
    for bit in range(bits):
        w = dot(w, transfer_ref[pos >> bit & 1]).astype(BF16)
    w_ref[...] = w
    copies[2].wait()
    z = dot(x_ref[...], w).astype(BF16)
    rows = z_ref.shape[1]
    for part in range(GROUP):
        z_ref[part] = z[part * rows : (part + 1) * rows]
    copies[4].wait()
    lanes = lax.broadcasted_iota(jnp.int32, (TAIL, z.shape[1]), 1)
    first = lanes < z.shape[1] // 2
    tail = jnp.where(first == (chip == 0), cols_ref[0, SLOT], 0).astype(F32).astype(BF16)
    for at, half in enumerate((chip, 1 - chip)):
        low = at * (rows + TAIL)
        keep_ref[low : low + rows] = z_ref[2 * core + half]
        send_ref[low : low + rows] = z_ref[2 * (1 - core) + half]
        keep_ref[low + rows : low + rows + TAIL] = tail
        send_ref[low + rows : low + rows + TAIL] = jnp.zeros_like(tail)
    copies[3].wait()


def push_kernel(
    turns, pairs, clusters, own_ref, mate_ref, coupling_ref, transfer_ref, mask_ref, *refs
):
    *push_refs, pair_ref, both_ref = refs
    leaf_pos = lax.axis_index("leaf")
    pair, side = leaf_pos >> 1, leaf_pos & 1
    rows = both_ref.shape[1]
    both_ref[side] = own_ref[:rows]
    both_ref[1 - side] = mate_ref[:rows]
    total = dot(both_ref[0], transfer_ref[0]) + dot(both_ref[1], transfer_ref[1])
    pair_ref[...] = total.astype(BF16)

    def term(lev, coef, gap, source, target):
        pick = abs(gap) - 2
        matrix = coupling_ref[lev, pick]
        switch = mask_ref[lev, pick, source if gap > 0 else target].astype(F32)
        return switch * (dot_t(coef, matrix) if gap > 0 else dot(coef, matrix))

    def fill(push_ref, distance, to_side):
        target_pair = pair + distance
        total = None
        if abs(distance) in (2, 3) and clusters[1]:
            coupled = term(1, pair_ref[...], distance, pair, target_pair).astype(BF16)
            total = dot_t(coupled, transfer_ref[to_side])
        for from_side in (0, 1):
            gap = 2 * distance + to_side - from_side
            if abs(gap) in (2, 3) and clusters[0]:
                more = term(
                    0, both_ref[from_side], gap, 2 * pair + from_side, 2 * target_pair + to_side
                )
                total = more if total is None else total + more
        if total is None:
            total = jnp.zeros(pair_ref.shape, F32)
        push_ref[:rows] = total.astype(BF16)

    for turn, push_ref in zip(turns, push_refs):
        push_ref[rows:] = mate_ref[rows:]
        for distance in reached(turn, pairs):
            if pairs == 4:
                inside = (pair ^ turn) == pair + distance
            else:
                inside = jnp.logical_and(pair + distance >= 0, pair + distance < pairs)
            for to_side in (0, 1):
                @pl.when(jnp.logical_and(inside, side == to_side))
                def _(push_ref=push_ref, distance=distance, to_side=to_side):
                    fill(push_ref, distance, to_side)


def reached(turn, pairs):
    return sorted({(i ^ turn) - i for i in range(pairs)}) if pairs == 4 else [turn]


def named_place(rows, ref):
    half = ref.shape[1] // 2
    cols = [jnp.max(ref[rows:, at : at + half].astype(F32)) for at in (0, half)]
    col = jnp.where(lax.axis_index("level") >> 1 == 0, cols[0], cols[1]).astype(jnp.int32)
    return lax.rem(col, GROUP)


def pick_block(place, blocks, out_ref):
    turn = place ^ lax.axis_index("level")
    for at, block in enumerate(blocks):
        @pl.when(turn == at)
        def _(block=block):
            out_ref[...] = block[...]


def pick_even_kernel(rows, named_ref, *refs):
    *blocks, out_ref = refs
    pick_block(named_place(rows, named_ref), blocks, out_ref)


def pick_odd_kernel(rows, pairs, named_refs_count, *refs):
    named_refs, blocks, out_ref = refs[:named_refs_count], refs[named_refs_count:-1], refs[-1]
    leaf_pos = lax.axis_index("leaf")
    pair, side = leaf_pos >> 1, leaf_pos & 1
    places = [named_place(rows, ref) for ref in named_refs]
    if pairs == 4:
        inner = jnp.logical_or(
            jnp.logical_and(pair == 1, side == 1), jnp.logical_and(pair == 2, side == 0)
        )
    else:
        inner = side == 1
    pick_block(jnp.where(inner, places[1], places[0]), blocks, out_ref)


def near_kernel(
    x_ref, mate_ref, across_ref, corner_ref, edge_ref, tiles_ref, w_ref, field0, field1, field2,
    field3, cols_ref, count_ref, acc_ref, field_ref
):
    pos = lax.axis_index("level")
    for turn, part_ref in enumerate((field0, field1, field2, field3)):
        field_ref[part_of(pos ^ turn)] = part_ref[...]
    field = jnp.concatenate([field_ref[part] for part in range(GROUP)], axis=0)
    odd = pos & 1
    inner = jnp.logical_or(pos == 1, pos == 2)
    acc = dot(x_ref[...], tiles_ref[0, 0]) + dot(mate_ref[...], tiles_ref[0, 2 - odd])
    beside = jnp.where(inner, corner_ref[...], edge_ref[...])
    acc = acc + dot(beside, tiles_ref[0, 1 + odd])
    acc_ref[...] = acc + dot_t(field, w_ref[...])
    col = cols_ref[0, SLOT]
    turn = lax.rem(col, GROUP) ^ pos
    here = jnp.logical_and(count_ref[0] > SLOT, col // GROUP == 1)
    for at, block in enumerate((x_ref, mate_ref, across_ref, corner_ref)):
        @pl.when(jnp.logical_and(here, turn == at))
        def _(block=block):
            acc_ref[...] += dot(block[...], tiles_ref[0, SLOT])


def finish_kernel(acc_ref, even_ref, odd_ref, tiles_ref, cols_ref, count_ref, out_ref):
    side = lax.axis_index("leaf") & 1
    group = cols_ref[0, SLOT] // GROUP
    live = jnp.logical_and(count_ref[0] > SLOT, group != 1)
    from_even = (group == 0) == (side == 1)

    @pl.when(jnp.logical_not(live))
    def _():
        out_ref[...] = acc_ref[...].astype(BF16)

    for here, block in ((from_even, even_ref), (jnp.logical_not(from_even), odd_ref)):
        @pl.when(jnp.logical_and(live, here))
        def _(block=block):
            out_ref[...] = (acc_ref[...] + dot(block[...], tiles_ref[0, SLOT])).astype(BF16)


def part_of(pos):
    return 2 * (pos & 1) + (pos >> 1)


def turned(value, turn):
    return lax.ppermute(value, "level", [(i, i ^ turn) for i in range(GROUP)])


def shifted(value, steps):
    count = lax.axis_size("leaf")
    route = [(i, i + steps) for i in range(count) if 0 <= i + steps < count]
    return lax.ppermute(value, "leaf", route)


def swapped(value, distance):
    count = lax.axis_size("leaf")
    return lax.ppermute(value, "leaf", [(i, i ^ 1 << distance) for i in range(count)])


def neighbours(value, odd):
    count = lax.axis_size("leaf")
    route = [(i, i + 1) for i in range(odd, count - 1, 2)]
    return lax.ppermute(value, "leaf", route + [(b, a) for a, b in route])


def upper_field(coef, coupling, transfer, couple_mask):
    leaf_count = lax.axis_size("leaf")
    leaf_pos = lax.axis_index("leaf")
    couplings = []
    levels = range(2, min(coupling.shape[0], leaf_count.bit_length()))
    for lev in levels:
        other = swapped(coef, lev - 1)
        is_upper = (leaf_pos >> lev - 1 & 1) == 1
        total = dot(jnp.where(is_upper, other, coef), transfer[0])
        total = total + dot(jnp.where(is_upper, coef, other), transfer[1])
        coef = total.astype(BF16)
        cluster = leaf_pos >> lev
        coupled = jnp.zeros(coef.shape, F32)
        for pick, offset in enumerate((2, 3)):
            if offset < leaf_count >> lev:
                matrix = coupling[lev, pick]
                ahead = shifted(coef, -(offset << lev))
                behind = shifted(coef, offset << lev)
                ahead_mask = couple_mask[lev, cluster, pick].astype(F32)
                behind_mask = couple_mask[lev, jnp.maximum(cluster - offset, 0), pick].astype(F32)
                coupled = coupled + ahead_mask * dot(ahead, matrix)
                coupled = coupled + behind_mask * dot_t(behind, matrix)
        couplings.append(coupled)
    field = jnp.zeros(coef.shape, F32)
    for lev, coupled in zip(reversed(levels), reversed(couplings)):
        if lev + 1 in levels:
            field = dot_t(field.astype(BF16), transfer[leaf_pos >> lev & 1])
        field = field + coupled
    for lev in (1, 0):
        field = dot_t(field.astype(BF16), transfer[leaf_pos >> lev & 1])
    return field


def per_device(
    points_x, leaf_basis, near_tiles, near_cols, near_count, transfer, coupling, couple_mask
):
    assert lax.axis_size("level") == GROUP
    leaf_count = lax.axis_size("leaf")
    vectors, points = points_x.shape
    rank = leaf_basis.shape[2]
    rows = vectors // GROUP
    bits = GROUP.bit_length() - 1
    block = ((vectors, points), BF16)
    part = ((rows, rank), BF16)
    tailed = ((rows + TAIL, rank), BF16)
    doubled = ((2 * (rows + TAIL), rank), BF16)

    keep, send, w, own_x, transfer_in, coupling_in = call(
        partial(up_kernel, bits), "up",
        [points_x, leaf_basis, transfer, coupling, near_cols], [],
        [doubled, doubled, ((points, rank), BF16), block, (transfer.shape, BF16),
         ((2,) + coupling.shape[1:], BF16)],
        [pltpu.VMEM((points, rank), BF16), pltpu.VMEM((GROUP, rows, rank), BF16),
         pltpu.SMEM(near_cols.shape, jnp.int32), pltpu.SemaphoreType.DMA((5,))],
        pltpu.HBM,
    )
    chip_sum = (keep.astype(F32) + turned(send, 1).astype(F32)).astype(BF16)
    came_half = turned(chip_sum[rows + TAIL :], 2)
    coef = (chip_sum[: rows + TAIL].astype(F32) + came_half.astype(F32)).astype(BF16)
    sent, coef = lax.optimization_barrier((points_x, coef))
    joints = [(GROUP * g - 1, GROUP * g) for g in range(1, leaf_count)]
    edge = lax.ppermute(sent, ("leaf", "level"), joints + [(b, a) for a, b in joints])
    beside = swapped(coef, 0)

    across = turned(points_x, 2)
    mate = turned(points_x, 1)
    across, beside = lax.optimization_barrier((across, beside))
    corner = turned(across, 1)

    active = min(coupling.shape[0], leaf_count.bit_length())
    pairs = leaf_count // 2
    turns = [1, 2, 3] if pairs == 4 else [1, 2, 3, -1, -2, -3]
    clusters = [lev < active and (leaf_count >> lev) > 2 for lev in (0, 1)]
    *pushes, pair_coef = call(
        partial(push_kernel, turns, pairs, clusters), "push",
        [coef, beside, coupling_in, transfer_in], [couple_mask.transpose(0, 2, 1)],
        [tailed] * len(turns) + [part], [pltpu.VMEM((2, rows, rank), BF16)],
    )
    edge, mate, corner, pushes = lax.optimization_barrier((edge, mate, corner, pushes))
    held = [own_x, mate, across, corner]
    came = {}
    for turn, push in zip(turns, pushes):
        if pairs == 4:
            came[turn] = lax.ppermute(
                push, "leaf", [(i, i ^ 2 * turn) for i in range(leaf_count)]
            )
        else:
            came[turn] = shifted(push, 2 * turn)
    field = came[1][:rows].astype(F32)
    for turn in turns[1:]:
        field = field + came[turn][:rows].astype(F32)
    if active > 2 and (leaf_count >> 2) > 2:
        field = field + upper_field(pair_coef, coupling, transfer, couple_mask)
    field = field.astype(BF16)

    (to_even,) = call(partial(pick_even_kernel, rows), "pick_even", [beside] + held, [], [block])
    from_even = neighbours(to_even, 0)
    named = [came[1], came[3 if pairs == 4 else -1]]
    (to_odd,) = call(
        partial(pick_odd_kernel, rows, pairs, len(named)), "pick_odd", named + held, [], [block]
    )
    field, to_odd = lax.optimization_barrier((field, to_odd))
    fields = [field] + [turned(field, turn) for turn in range(1, GROUP)]
    from_odd = neighbours(to_odd, 1)
    (acc,) = call(
        near_kernel, "near", held + [edge, near_tiles, w] + fields, [near_cols, near_count],
        [((vectors, points), F32)], [pltpu.VMEM((GROUP, rows, rank), BF16)],
    )
    (out,) = call(
        finish_kernel, "finish", [acc, from_even, from_odd, near_tiles], [near_cols, near_count],
        [block],
    )
    return out


def solution(mesh):
    in_specs = (
        P(None, ("leaf", "level")),
        P(("leaf", "level"), None, None),
        P(("leaf", "level"), None, None, None),
        P(("leaf", "level"), None),
        P(("leaf", "level")),
        P(),
        P(),
        P(),
    )
    out_specs = P(None, ("leaf", "level"))
    return jax.shard_map(
        per_device, mesh=mesh, in_specs=in_specs, out_specs=out_specs, check_vma=False
    )
```

profile of v0, /device:TPU:7, one launch (start us, length us, event | category | flops | bytes accessed | tf_op | source)
XLA Modules:
  0.0 38.4 jit_solution(4713064922021101856)
XLA Ops:
  0.0 1.9 %up.1 = (bf16[160,256]{1,0:T(8,128)(2,1)S(1)}, bf16[160,256]{1,0:T(8,128)(2,1)S(1)}, bf16[512,256]{1,0:T(8,128)(2,1)S(1)}, bf16[256,512]{1,0:T(8,128)(2,1)S(1)},...) custom-call(bf16[256,512]{1,0:T(8,128)(2,1)} %x_hbm.1, bf16[1,512,256]{2,1,0:T(8,128)(2,1)} %basis_hbm.1, ...), custom_call_target="tpu_custom_call" | custom-call | tf_op jit(solution)/shard_map/up/pallas_call | solution.py:28
  1.9 0.7 %collective-permute-start = (bf16[160,256]{1,0:T(8,128)(2,1)S(1)}, bf16[160,256]{1,0:T(8,128)(2,1)S(1)}, u32[]{:S(2)}, u32[]{:S(2)}) collective-permute-start(bf16[160,256]{1,0:T(8,128)(2,1)S(1)} %get-tuple-element.28), channel_id=1, source_target_pairs={{0,1},{1,0},{2,3},{3,2},{4,5},{5,4},{6,7},{7,6},{8,9},{9,8},{10,11... | collective-permute-start | bytes 245768 | tf_op jit(solution)/shard_map/ppermute | solution.py:208
  2.6 0.9 %collective-permute-done = bf16[160,256]{1,0:T(8,128)(2,1)S(1)} collective-permute-done((bf16[160,256]{1,0:T(8,128)(2,1)S(1)}, bf16[160,256]{1,0:T(8,128)(2,1)S(1)}, u32[]{:S(2)}, u32[]{:S(2)}) %collective-permute-start) | collective-permute-done | bytes 81952 | tf_op jit(solution)/shard_map/ppermute | solution.py:208
  3.6 0.3 collective-permute-start.1
  3.9 1.2 %collective-permute-start.4 = (bf16[256,512]{1,0:T(8,128)(2,1)S(1)}, bf16[256,512]{1,0:T(8,128)(2,1)S(1)}, u32[]{:S(2)}, u32[]{:S(2)}) collective-permute-start(bf16[256,512]{1,0:T(8,128)(2,1)S(1)} %copy-done.3), channel_id=1, source_target_pairs={{0,2},{1,3},{2,0},{3,1},{4,6},{5,7},{6,4},{7,5},{8,10},{9,11},{10,... | collective-permute-start | bytes 786440 | tf_op jit(solution)/shard_map/ppermute | solution.py:208
  5.1 1.4 %collective-permute-done.1 = bf16[80,256]{1,0:T(8,128)(2,1)S(1)} collective-permute-done((bf16[80,256]{1,0:T(8,128)(2,1)S(1)}, bf16[80,256]{1,0:T(8,128)(2,1)S(1)}, u32[]{:S(2)}, u32[]{:S(2)}) %collective-permute-start.1) | collective-permute-done | bytes 40992 | tf_op jit(solution)/shard_map/ppermute | solution.py:208
  6.5 0.3 collective-permute-start.5
  6.8 2.2 %collective-permute-start.3 = (bf16[256,512]{1,0:T(8,128)(2,1)S(1)}, bf16[256,512]{1,0:T(8,128)(2,1)S(1)}, u32[]{:S(2)}, u32[]{:S(2)}) collective-permute-start(bf16[256,512]{1,0:T(8,128)(2,1)S(1)} %copy-done.3), channel_id=1, source_target_pairs={{0,1},{1,0},{2,3},{3,2},{4,5},{5,4},{6,7},{7,6},{8,9},{9,8},{10,11... | collective-permute-start | bytes 786440 | tf_op jit(solution)/shard_map/ppermute | solution.py:208
  9.0 3.7 %collective-permute-start.2 = (bf16[256,512]{1,0:T(8,128)(2,1)S(1)}, bf16[256,512]{1,0:T(8,128)(2,1)S(1)}, u32[]{:S(2)}, u32[]{:S(2)}) collective-permute-start(bf16[256,512]{1,0:T(8,128)(2,1)S(1)} %copy-done.3), channel_id=1, source_target_pairs={{3,4},{7,8},{11,12},{15,16},{19,20},{23,24},{27,28},{4,3},{8,7},{1... | collective-permute-start | bytes 786440 | tf_op jit(solution)/shard_map/ppermute | solution.py:289
  12.7 0.0 collective-permute-done.5.mate_ref.named_ref
  12.7 0.0 collective-permute-done.4.refs_4_.across_ref.refs_2_
  12.7 0.5 %collective-permute-start.6 = (bf16[256,512]{1,0:T(8,128)(2,1)S(1)}, bf16[256,512]{1,0:T(8,128)(2,1)S(1)}, u32[]{:S(2)}, u32[]{:S(2)}) collective-permute-start(bf16[256,512]{1,0:T(8,128)(2,1)S(1)} %collective-permute-done.4.refs_4_.across_ref.refs_2_), channel_id=1, source_target_pairs={{0,1},{1,0},{2,3},{3,2},{4,5},{5,4},{6,7},{7,6},{8,9},{9,8},{10,11... | collective-permute-start | bytes 786440 | tf_op jit(solution)/shard_map/ppermute | solution.py:208
  13.2 2.3 %push.1 = (bf16[80,256]{1,0:T(8,128)(2,1)S(1)}, bf16[80,256]{1,0:T(8,128)(2,1)S(1)}, bf16[80,256]{1,0:T(8,128)(2,1)S(1)}, bf16[64,256]{1,0:T(8,128)(2,1)}) custom-call(bf16[80,256]{1,0:T(8,128)(2,1)S(1)} %add_convert_fusion.1.own_ref, bf16[80,256]{1,0:T(8,128)(2,1)S(1)} %collective-permute-done.5.mate_ref.named_ref, ...), custom_call_target="tpu_custom_call" | custom-call | tf_op jit(solution)/shard_map/push/pallas_call | solution.py:28
  15.6 0.0 collective-permute-done.3.refs_3_.mate_ref.refs_1_
  15.6 3.0 %collective-permute-done.2.edge_ref = bf16[256,512]{1,0:T(8,128)(2,1)S(1)} collective-permute-done((bf16[256,512]{1,0:T(8,128)(2,1)S(1)}, bf16[256,512]{1,0:T(8,128)(2,1)S(1)}, u32[]{:S(2)}, u32[]{:S(2)}) %collective-permute-start.2) | collective-permute-done | bytes 262176 | tf_op jit(solution)/shard_map/ppermute | solution.py:289
  18.6 0.0 collective-permute-done.6.refs_5_.corner_ref.refs_3_
  18.6 1.2 %collective-permute-start.7 = (bf16[80,256]{1,0:T(8,128)(2,1)S(1)}, bf16[80,256]{1,0:T(8,128)(2,1)S(1)}, u32[]{:S(2)}, u32[]{:S(2)}) collective-permute-start(bf16[80,256]{1,0:T(8,128)(2,1)S(1)} %get-tuple-element.42), channel_id=1, source_target_pairs={{0,8},{4,12},{8,0},{12,4},{16,24},{20,28},{24,16},{28,20},{1,9},{5... | collective-permute-start | bytes 122888 | tf_op jit(solution)/shard_map/ppermute | solution.py:311
  19.8 2.5 %collective-permute-start.9 = (bf16[80,256]{1,0:T(8,128)(2,1)S(1)}, bf16[80,256]{1,0:T(8,128)(2,1)S(1)}, u32[]{:S(2)}, u32[]{:S(2)}) collective-permute-start(bf16[80,256]{1,0:T(8,128)(2,1)S(1)} %get-tuple-element.44), channel_id=1, source_target_pairs={{0,24},{4,28},{8,16},{12,20},{16,8},{20,12},{24,0},{28,4},{1,25},{... | collective-permute-start | bytes 122888 | tf_op jit(solution)/shard_map/ppermute | solution.py:311
  22.2 0.0 collective-permute-start.8
  22.2 0.2 pick_even.1
  22.4 0.3 collective-permute-start.13
  22.7 1.9 %collective-permute-done.9.refs_1_ = bf16[80,256]{1,0:T(8,128)(2,1)S(1)} collective-permute-done((bf16[80,256]{1,0:T(8,128)(2,1)S(1)}, bf16[80,256]{1,0:T(8,128)(2,1)S(1)}, u32[]{:S(2)}, u32[]{:S(2)}) %collective-permute-start.9) | collective-permute-done | bytes 40992 | tf_op jit(solution)/shard_map/ppermute | solution.py:311
  24.6 0.2 pick_odd.1
  24.8 1.2 %collective-permute-done.8 = bf16[80,256]{1,0:T(8,128)(2,1)S(1)} collective-permute-done((bf16[80,256]{1,0:T(8,128)(2,1)S(1)}, bf16[80,256]{1,0:T(8,128)(2,1)S(1)}, u32[]{:S(2)}, u32[]{:S(2)}) %collective-permute-start.8) | collective-permute-done | bytes 40992 | tf_op jit(solution)/shard_map/ppermute | solution.py:311
  26.0 2.2 %collective-permute-start.14 = (bf16[256,512]{1,0:T(8,128)(2,1)S(1)}, bf16[256,512]{1,0:T(8,128)(2,1)S(1)}, u32[]{:S(2)}, u32[]{:S(2)}) collective-permute-start(bf16[256,512]{1,0:T(8,128)(2,1)S(1)} %pick_odd.1), channel_id=1, source_target_pairs={{4,8},{12,16},{20,24},{8,4},{16,12},{24,20},{5,9},{13,17},{21,25},... | collective-permute-start | bytes 786440 | tf_op jit(solution)/shard_map/ppermute | solution.py:225
  28.2 2.8 %collective-permute-start.12 = (bf16[64,256]{1,0:T(8,128)(2,1)S(1)}, bf16[64,256]{1,0:T(8,128)(2,1)S(1)}, u32[]{:S(2)}, u32[]{:S(2)}) collective-permute-start(bf16[64,256]{1,0:T(8,128)(2,1)S(1)} %add_convert_fusion.2.field0), channel_id=1, source_target_pairs={{0,3},{1,2},{2,1},{3,0},{4,7},{5,6},{6,5},{7,4},{8,11},{9,10},{10,... | collective-permute-start | bytes 98312 | tf_op jit(solution)/shard_map/ppermute | solution.py:208
  31.0 0.5 %collective-permute-start.10 = (bf16[64,256]{1,0:T(8,128)(2,1)S(1)}, bf16[64,256]{1,0:T(8,128)(2,1)S(1)}, u32[]{:S(2)}, u32[]{:S(2)}) collective-permute-start(bf16[64,256]{1,0:T(8,128)(2,1)S(1)} %add_convert_fusion.2.field0), channel_id=1, source_target_pairs={{0,1},{1,0},{2,3},{3,2},{4,5},{5,4},{6,7},{7,6},{8,9},{9,8},{10,11... | collective-permute-start | bytes 98312 | tf_op jit(solution)/shard_map/ppermute | solution.py:208
  32.1 0.8 %collective-permute-done.12.field3 = bf16[64,256]{1,0:T(8,128)(2,1)S(1)} collective-permute-done((bf16[64,256]{1,0:T(8,128)(2,1)S(1)}, bf16[64,256]{1,0:T(8,128)(2,1)S(1)}, u32[]{:S(2)}, u32[]{:S(2)}) %collective-permute-start.12) | collective-permute-done | bytes 32800 | tf_op jit(solution)/shard_map/ppermute | solution.py:208
  32.9 1.2 %collective-permute-done.11.field2 = bf16[64,256]{1,0:T(8,128)(2,1)S(1)} collective-permute-done((bf16[64,256]{1,0:T(8,128)(2,1)S(1)}, bf16[64,256]{1,0:T(8,128)(2,1)S(1)}, u32[]{:S(2)}, u32[]{:S(2)}) %collective-permute-start.11) | collective-permute-done | bytes 32800 | tf_op jit(solution)/shard_map/ppermute | solution.py:208
  34.1 1.2 %near.1.acc_ref = f32[256,512]{1,0:T(8,128)S(1)} custom-call(bf16[256,512]{1,0:T(8,128)(2,1)S(1)} %get-tuple-element.26.refs_2_.x_ref.refs_0_, bf16[256,512]{1,0:T(8,128)(2,1)S(1)} %collective-permute-done.3.refs_3_.mate_ref.refs_1_, bf16[256,512]{1,0:T(8,128)(2,1)S(1)} %collective-permute-done.4.refs_4_.across_ref.refs_2_, ...), custom_call_target="tpu_custom_call" | custom-call | tf_op jit(solution)/shard_map/near/pallas_call | solution.py:28
  35.3 1.6 %collective-permute-done.14.odd_ref = bf16[256,512]{1,0:T(8,128)(2,1)S(1)} collective-permute-done((bf16[256,512]{1,0:T(8,128)(2,1)S(1)}, bf16[256,512]{1,0:T(8,128)(2,1)S(1)}, u32[]{:S(2)}, u32[]{:S(2)}) %collective-permute-start.14) | collective-permute-done | bytes 262176 | tf_op jit(solution)/shard_map/ppermute | solution.py:225
  36.9 1.6 %finish.1 = bf16[256,512]{1,0:T(8,128)(2,1)} custom-call(f32[256,512]{1,0:T(8,128)S(1)} %near.1.acc_ref, bf16[256,512]{1,0:T(8,128)(2,1)S(1)} %collective-permute-done.13.even_ref, bf16[256,512]{1,0:T(8,128)(2,1)S(1)} %collective-permute-done.14.odd_ref, bf16[1,4,512,512]{3,2,1,0:T(8,128)(2,1)S(1)} %copy-done, s32[1,4]{1,0:T(1,128)S(1)} %copy-done.2, ...), custom_call_target="tpu_custom_call" | custom-call | tf_op jit(solution)/shard_map/finish/pallas_call | solution.py:28
  (16 shorter events, 0.1 us)
Async XLA Ops:
  0.0 3.9 %copy-start.3 = (bf16[256,512]{1,0:T(8,128)(2,1)S(1)}, bf16[256,512]{1,0:T(8,128)(2,1)}, u32[]{:S(2)}) copy-start(bf16[256,512]{1,0:T(8,128)(2,1)} %x_hbm.1) | copy-start | bytes 786436
  0.0 13.2 %copy-start.1 = (s32[6,8,2]{1,2,0:T(2,128)S(1)}, s32[6,8,2]{1,2,0:T(2,128)}, u32[]{:S(2)}) copy-start(s32[6,8,2]{1,2,0:T(2,128)} %param.15) | copy-start | bytes 1156
  1.9 1.7 %collective-permute-start = (bf16[160,256]{1,0:T(8,128)(2,1)S(1)}, bf16[160,256]{1,0:T(8,128)(2,1)S(1)}, u32[]{:S(2)}, u32[]{:S(2)}) collective-permute-start(bf16[160,256]{1,0:T(8,128)(2,1)S(1)} %get-tuple-element.28), channel_id=1, source_target_pairs={{0,1},{1,0},{2,3},{3,2},{4,5},{5,4},{6,7},{7,6},{8,9},{9,8},{10,11... | collective-permute-start | bytes 245768 | tf_op jit(solution)/shard_map/ppermute | solution.py:208
  3.5 30.6 %copy-start = (bf16[1,4,512,512]{3,2,1,0:T(8,128)(2,1)S(1)}, bf16[1,4,512,512]{3,2,1,0:T(8,128)(2,1)}, u32[]{:S(2)}) copy-start(bf16[1,4,512,512]{3,2,1,0:T(8,128)(2,1)} %tiles_ref.3) | copy-start | bytes 6291460
  3.5 30.6 %copy-start.2 = (s32[1,4]{1,0:T(1,128)S(1)}, s32[1,4]{1,0:T(1,128)}, u32[]{:S(2)}) copy-start(s32[1,4]{1,0:T(1,128)} %cols_ref.3) | copy-start | bytes 52
  3.6 2.9 %collective-permute-start.1 = (bf16[80,256]{1,0:T(8,128)(2,1)S(1)}, bf16[80,256]{1,0:T(8,128)(2,1)S(1)}, u32[]{:S(2)}, u32[]{:S(2)}) collective-permute-start(bf16[80,256]{1,0:T(8,128)(2,1)S(1)} %slice.21), channel_id=1, source_target_pairs={{0,2},{1,3},{2,0},{3,1},{4,6},{5,7},{6,4},{7,5},{8,10},{9,11},{10,... | collective-permute-start | bytes 122888 | tf_op jit(solution)/shard_map/ppermute | solution.py:208
  3.9 8.8 %collective-permute-start.4 = (bf16[256,512]{1,0:T(8,128)(2,1)S(1)}, bf16[256,512]{1,0:T(8,128)(2,1)S(1)}, u32[]{:S(2)}, u32[]{:S(2)}) collective-permute-start(bf16[256,512]{1,0:T(8,128)(2,1)S(1)} %copy-done.3), channel_id=1, source_target_pairs={{0,2},{1,3},{2,0},{3,1},{4,6},{5,7},{6,4},{7,5},{8,10},{9,11},{10,... | collective-permute-start | bytes 786440 | tf_op jit(solution)/shard_map/ppermute | solution.py:208
  6.5 6.2 %collective-permute-start.5 = (bf16[80,256]{1,0:T(8,128)(2,1)S(1)}, bf16[80,256]{1,0:T(8,128)(2,1)S(1)}, u32[]{:S(2)}, u32[]{:S(2)}) collective-permute-start(bf16[80,256]{1,0:T(8,128)(2,1)S(1)} %add_convert_fusion.1.own_ref), channel_id=1, source_target_pairs={{0,4},{4,0},{8,12},{12,8},{16,20},{20,16},{24,28},{28,24},{1,5},{5... | collective-permute-start | bytes 122888 | tf_op jit(solution)/shard_map/ppermute | solution.py:219
  6.8 8.8 %collective-permute-start.3 = (bf16[256,512]{1,0:T(8,128)(2,1)S(1)}, bf16[256,512]{1,0:T(8,128)(2,1)S(1)}, u32[]{:S(2)}, u32[]{:S(2)}) collective-permute-start(bf16[256,512]{1,0:T(8,128)(2,1)S(1)} %copy-done.3), channel_id=1, source_target_pairs={{0,1},{1,0},{2,3},{3,2},{4,5},{5,4},{6,7},{7,6},{8,9},{9,8},{10,11... | collective-permute-start | bytes 786440 | tf_op jit(solution)/shard_map/ppermute | solution.py:208
  9.0 9.6 %collective-permute-start.2 = (bf16[256,512]{1,0:T(8,128)(2,1)S(1)}, bf16[256,512]{1,0:T(8,128)(2,1)S(1)}, u32[]{:S(2)}, u32[]{:S(2)}) collective-permute-start(bf16[256,512]{1,0:T(8,128)(2,1)S(1)} %copy-done.3), channel_id=1, source_target_pairs={{3,4},{7,8},{11,12},{15,16},{19,20},{23,24},{27,28},{4,3},{8,7},{1... | collective-permute-start | bytes 786440 | tf_op jit(solution)/shard_map/ppermute | solution.py:289
  12.7 5.9 %collective-permute-start.6 = (bf16[256,512]{1,0:T(8,128)(2,1)S(1)}, bf16[256,512]{1,0:T(8,128)(2,1)S(1)}, u32[]{:S(2)}, u32[]{:S(2)}) collective-permute-start(bf16[256,512]{1,0:T(8,128)(2,1)S(1)} %collective-permute-done.4.refs_4_.across_ref.refs_2_), channel_id=1, source_target_pairs={{0,1},{1,0},{2,3},{3,2},{4,5},{5,4},{6,7},{7,6},{8,9},{9,8},{10,11... | collective-permute-start | bytes 786440 | tf_op jit(solution)/shard_map/ppermute | solution.py:208
  18.6 4.1 %collective-permute-start.7 = (bf16[80,256]{1,0:T(8,128)(2,1)S(1)}, bf16[80,256]{1,0:T(8,128)(2,1)S(1)}, u32[]{:S(2)}, u32[]{:S(2)}) collective-permute-start(bf16[80,256]{1,0:T(8,128)(2,1)S(1)} %get-tuple-element.42), channel_id=1, source_target_pairs={{0,8},{4,12},{8,0},{12,4},{16,24},{20,28},{24,16},{28,20},{1,9},{5... | collective-permute-start | bytes 122888 | tf_op jit(solution)/shard_map/ppermute | solution.py:311
  19.8 4.8 %collective-permute-start.9 = (bf16[80,256]{1,0:T(8,128)(2,1)S(1)}, bf16[80,256]{1,0:T(8,128)(2,1)S(1)}, u32[]{:S(2)}, u32[]{:S(2)}) collective-permute-start(bf16[80,256]{1,0:T(8,128)(2,1)S(1)} %get-tuple-element.44), channel_id=1, source_target_pairs={{0,24},{4,28},{8,16},{12,20},{16,8},{20,12},{24,0},{28,4},{1,25},{... | collective-permute-start | bytes 122888 | tf_op jit(solution)/shard_map/ppermute | solution.py:311
  22.2 3.8 %collective-permute-start.8 = (bf16[80,256]{1,0:T(8,128)(2,1)S(1)}, bf16[80,256]{1,0:T(8,128)(2,1)S(1)}, u32[]{:S(2)}, u32[]{:S(2)}) collective-permute-start(bf16[80,256]{1,0:T(8,128)(2,1)S(1)} %get-tuple-element.43), channel_id=1, source_target_pairs={{0,16},{4,20},{8,24},{12,28},{16,0},{20,4},{24,8},{28,12},{1,17},{... | collective-permute-start | bytes 122888 | tf_op jit(solution)/shard_map/ppermute | solution.py:311
  22.4 12.9 %collective-permute-start.13 = (bf16[256,512]{1,0:T(8,128)(2,1)S(1)}, bf16[256,512]{1,0:T(8,128)(2,1)S(1)}, u32[]{:S(2)}, u32[]{:S(2)}) collective-permute-start(bf16[256,512]{1,0:T(8,128)(2,1)S(1)} %pick_even.1), channel_id=1, source_target_pairs={{0,4},{8,12},{16,20},{24,28},{4,0},{12,8},{20,16},{28,24},{1,5},{9... | collective-permute-start | bytes 786440 | tf_op jit(solution)/shard_map/ppermute | solution.py:225
  26.0 10.9 %collective-permute-start.14 = (bf16[256,512]{1,0:T(8,128)(2,1)S(1)}, bf16[256,512]{1,0:T(8,128)(2,1)S(1)}, u32[]{:S(2)}, u32[]{:S(2)}) collective-permute-start(bf16[256,512]{1,0:T(8,128)(2,1)S(1)} %pick_odd.1), channel_id=1, source_target_pairs={{4,8},{12,16},{20,24},{8,4},{16,12},{24,20},{5,9},{13,17},{21,25},... | collective-permute-start | bytes 786440 | tf_op jit(solution)/shard_map/ppermute | solution.py:225
  28.2 4.7 %collective-permute-start.12 = (bf16[64,256]{1,0:T(8,128)(2,1)S(1)}, bf16[64,256]{1,0:T(8,128)(2,1)S(1)}, u32[]{:S(2)}, u32[]{:S(2)}) collective-permute-start(bf16[64,256]{1,0:T(8,128)(2,1)S(1)} %add_convert_fusion.2.field0), channel_id=1, source_target_pairs={{0,3},{1,2},{2,1},{3,0},{4,7},{5,6},{6,5},{7,4},{8,11},{9,10},{10,... | collective-permute-start | bytes 98312 | tf_op jit(solution)/shard_map/ppermute | solution.py:208
  31.0 3.1 %collective-permute-start.11 = (bf16[64,256]{1,0:T(8,128)(2,1)S(1)}, bf16[64,256]{1,0:T(8,128)(2,1)S(1)}, u32[]{:S(2)}, u32[]{:S(2)}) collective-permute-start(bf16[64,256]{1,0:T(8,128)(2,1)S(1)} %add_convert_fusion.2.field0), channel_id=1, source_target_pairs={{0,2},{1,3},{2,0},{3,1},{4,6},{5,7},{6,4},{7,5},{8,10},{9,11},{10,... | collective-permute-start | bytes 98312 | tf_op jit(solution)/shard_map/ppermute | solution.py:208
  31.0 3.1 %collective-permute-start.10 = (bf16[64,256]{1,0:T(8,128)(2,1)S(1)}, bf16[64,256]{1,0:T(8,128)(2,1)S(1)}, u32[]{:S(2)}, u32[]{:S(2)}) collective-permute-start(bf16[64,256]{1,0:T(8,128)(2,1)S(1)} %add_convert_fusion.2.field0), channel_id=1, source_target_pairs={{0,1},{1,0},{2,3},{3,2},{4,5},{5,4},{6,7},{7,6},{8,9},{9,8},{10,11... | collective-permute-start | bytes 98312 | tf_op jit(solution)/shard_map/ppermute | solution.py:208
where the time goes:
time: 38.5 us; the launch traced here: 38.4 us
  starting transfers between devices  18.3 us (48%)
  waiting for transfers between devices  12 us (31%)
  Pallas kernels  7.25 us (19%)
  between operations  0.76 us (2%)
    ppermute x8, starting transfers between devices, turned(): return lax.ppermute(value, 'level', [(i, i ^ turn) for i in range(GROUP)])  8.24 us
    pallas_call x6, Pallas kernels, call(): pl.pallas_call(kernel, out_shape=shapes, in_specs=[pl.BlockSpec(memory_sp...  7.25 us
    ppermute x8, waiting for transfers between devices, turned(): return lax.ppermute(value, 'level', [(i, i ^ turn) for i in range(GROUP)])  4.25 us
    ppermute x1, starting transfers between devices, per_device(): lax.ppermute(sent, ('leaf', 'level'), joints + [(b, a) for a, b in joints])  3.73 us
    ppermute x3, starting transfers between devices, per_device(): lax.ppermute(push, 'leaf', [(i, i ^ 2 * turn) for i in range(leaf_count)])  3.63 us
    ppermute x3, waiting for transfers between devices, per_device(): lax.ppermute(push, 'leaf', [(i, i ^ 2 * turn) for i in range(leaf_count)])  3.16 us
    ppermute x1, waiting for transfers between devices, per_device(): lax.ppermute(sent, ('leaf', 'level'), joints + [(b, a) for a, b in joints])  3.04 us
    ppermute x2, starting transfers between devices, neighbours(): return lax.ppermute(value, 'leaf', route + [(b, a) for a, b in route])  2.44 us
  transfers between devices with their start and end apart: 15, of which 8 were waited for; matrix products, arithmetic and copies ran while one was open for 0% of the time, Pallas kernels for 10%

commit v1 on v0

--- a/solution.py
+++ b/solution.py
@@ -291,19 +291,19 @@
 
     across = turned(points_x, 2)
     mate = turned(points_x, 1)
-    across, beside = lax.optimization_barrier((across, beside))
-    corner = turned(across, 1)
 
     active = min(coupling.shape[0], leaf_count.bit_length())
     pairs = leaf_count // 2
-    turns = [1, 2, 3] if pairs == 4 else [1, 2, 3, -1, -2, -3]
+    turns = [1, 3, 2] if pairs == 4 else [1, 2, 3, -1, -2, -3]
     clusters = [lev < active and (leaf_count >> lev) > 2 for lev in (0, 1)]
     *pushes, pair_coef = call(
         partial(push_kernel, turns, pairs, clusters), "push",
         [coef, beside, coupling_in, transfer_in], [couple_mask.transpose(0, 2, 1)],
         [tailed] * len(turns) + [part], [pltpu.VMEM((2, rows, rank), BF16)],
     )
-    edge, mate, corner, pushes = lax.optimization_barrier((edge, mate, corner, pushes))
+    across, pushes = lax.optimization_barrier((across, pushes))
+    corner = turned(across, 1)
+    edge, mate, corner, pushes[0] = lax.optimization_barrier((edge, mate, corner, pushes[0]))
     held = [own_x, mate, across, corner]
     came = {}
     for turn, push in zip(turns, pushes):
@@ -313,6 +313,7 @@
             )
         else:
             came[turn] = shifted(push, 2 * turn)
+    came = dict(zip(came, lax.optimization_barrier(list(came.values()))))
     field = came[1][:rows].astype(F32)
     for turn in turns[1:]:
         field = field + came[turn][:rows].astype(F32)

time: 38.5 us -> 35.7 us (0.927)
  the two profiles are of different devices: /device:TPU:7 before, /device:TPU:6 now
where the time goes in v1:
time: 35.7 us; the launch traced here: 35.6 us
  waiting for transfers between devices  15.1 us (42%)
  starting transfers between devices  12.7 us (36%)
  Pallas kernels  6.96 us (19%)
  between operations  0.77 us (2%)
    pallas_call x6, Pallas kernels, call(): pl.pallas_call(kernel, out_shape=shapes, in_specs=[pl.BlockSpec(memory_sp...  6.96 us
    ppermute x8, waiting for transfers between devices, turned(): return lax.ppermute(value, 'level', [(i, i ^ turn) for i in range(GROUP)])  5.89 us
    ppermute x8, starting transfers between devices, turned(): return lax.ppermute(value, 'level', [(i, i ^ turn) for i in range(GROUP)])  4.85 us
    ppermute x3, starting transfers between devices, per_device(): lax.ppermute(push, 'leaf', [(i, i ^ 2 * turn) for i in range(leaf_count)])  4.45 us
    ppermute x3, waiting for transfers between devices, per_device(): lax.ppermute(push, 'leaf', [(i, i ^ 2 * turn) for i in range(leaf_count)])  3.45 us
    ppermute x2, waiting for transfers between devices, neighbours(): return lax.ppermute(value, 'leaf', route + [(b, a) for a, b in route])  2.93 us
    ppermute x1, waiting for transfers between devices, swapped(): lax.ppermute(value, 'leaf', [(i, i ^ 1 << distance) for i in range(count)])  2.82 us
    ppermute x2, starting transfers between devices, neighbours(): return lax.ppermute(value, 'leaf', route + [(b, a) for a, b in route])  2.13 us
  transfers between devices with their start and end apart: 15, of which 9 were waited for; matrix products, arithmetic and copies ran while one was open for 0% of the time, Pallas kernels for 11%

profile of v1, /device:TPU:6, one launch (start us, length us, event | category | flops | bytes accessed | tf_op | source)
XLA Modules:
  0.0 35.6 jit_solution(3468712031069636153)
XLA Ops:
  0.0 1.8 %up.1 = (bf16[160,256]{1,0:T(8,128)(2,1)S(1)}, bf16[160,256]{1,0:T(8,128)(2,1)S(1)}, bf16[512,256]{1,0:T(8,128)(2,1)S(1)}, bf16[256,512]{1,0:T(8,128)(2,1)S(1)},...) custom-call(bf16[256,512]{1,0:T(8,128)(2,1)} %x_hbm.1, bf16[1,512,256]{2,1,0:T(8,128)(2,1)} %basis_hbm.1, ...), custom_call_target="tpu_custom_call" | custom-call | tf_op jit(solution)/shard_map/up/pallas_call | solution.py:28
  1.9 0.1 collective-permute-start
  1.9 1.3 %collective-permute-done = bf16[160,256]{1,0:T(8,128)(2,1)S(1)} collective-permute-done((bf16[160,256]{1,0:T(8,128)(2,1)S(1)}, bf16[160,256]{1,0:T(8,128)(2,1)S(1)}, u32[]{:S(2)}, u32[]{:S(2)}) %collective-permute-start) | collective-permute-done | bytes 81952 | tf_op jit(solution)/shard_map/ppermute | solution.py:208
  3.2 0.6 %collective-permute-start.1 = (bf16[80,256]{1,0:T(8,128)(2,1)S(1)}, bf16[80,256]{1,0:T(8,128)(2,1)S(1)}, u32[]{:S(2)}, u32[]{:S(2)}) collective-permute-start(bf16[80,256]{1,0:T(8,128)(2,1)S(1)} %slice.21), channel_id=1, source_target_pairs={{0,2},{1,3},{2,0},{3,1},{4,6},{5,7},{6,4},{7,5},{8,10},{9,11},{10,... | collective-permute-start | bytes 122888 | tf_op jit(solution)/shard_map/ppermute | solution.py:208
  3.8 1.5 %collective-permute-start.4 = (bf16[256,512]{1,0:T(8,128)(2,1)S(1)}, bf16[256,512]{1,0:T(8,128)(2,1)S(1)}, u32[]{:S(2)}, u32[]{:S(2)}) collective-permute-start(bf16[256,512]{1,0:T(8,128)(2,1)S(1)} %copy-done.3), channel_id=1, source_target_pairs={{0,2},{1,3},{2,0},{3,1},{4,6},{5,7},{6,4},{7,5},{8,10},{9,11},{10,... | collective-permute-start | bytes 786440 | tf_op jit(solution)/shard_map/ppermute | solution.py:208
  5.3 2.4 %collective-permute-done.1 = bf16[80,256]{1,0:T(8,128)(2,1)S(1)} collective-permute-done((bf16[80,256]{1,0:T(8,128)(2,1)S(1)}, bf16[80,256]{1,0:T(8,128)(2,1)S(1)}, u32[]{:S(2)}, u32[]{:S(2)}) %collective-permute-start.1) | collective-permute-done | bytes 40992 | tf_op jit(solution)/shard_map/ppermute | solution.py:208
  7.7 0.6 %collective-permute-start.5 = (bf16[80,256]{1,0:T(8,128)(2,1)S(1)}, bf16[80,256]{1,0:T(8,128)(2,1)S(1)}, u32[]{:S(2)}, u32[]{:S(2)}) collective-permute-start(bf16[80,256]{1,0:T(8,128)(2,1)S(1)} %add_convert_fusion.1.own_ref), channel_id=1, source_target_pairs={{0,4},{4,0},{8,12},{12,8},{16,20},{20,16},{24,28},{28,24},{1,5},{5... | collective-permute-start | bytes 122888 | tf_op jit(solution)/shard_map/ppermute | solution.py:219
  8.3 0.0 collective-permute-start.3
  8.3 0.7 %collective-permute-start.2 = (bf16[256,512]{1,0:T(8,128)(2,1)S(1)}, bf16[256,512]{1,0:T(8,128)(2,1)S(1)}, u32[]{:S(2)}, u32[]{:S(2)}) collective-permute-start(bf16[256,512]{1,0:T(8,128)(2,1)S(1)} %copy-done.3), channel_id=1, source_target_pairs={{3,4},{7,8},{11,12},{15,16},{19,20},{23,24},{27,28},{4,3},{8,7},{1... | collective-permute-start | bytes 786440 | tf_op jit(solution)/shard_map/ppermute | solution.py:289
  9.0 2.8 %collective-permute-done.5.mate_ref.named_ref = bf16[80,256]{1,0:T(8,128)(2,1)S(1)} collective-permute-done((bf16[80,256]{1,0:T(8,128)(2,1)S(1)}, bf16[80,256]{1,0:T(8,128)(2,1)S(1)}, u32[]{:S(2)}, u32[]{:S(2)}) %collective-permute-start.5) | collective-permute-done | bytes 40992 | tf_op jit(solution)/shard_map/ppermute | solution.py:219
  11.8 2.3 %push.1 = (bf16[80,256]{1,0:T(8,128)(2,1)S(1)}, bf16[80,256]{1,0:T(8,128)(2,1)S(1)}, bf16[80,256]{1,0:T(8,128)(2,1)S(1)}, bf16[64,256]{1,0:T(8,128)(2,1)}) custom-call(bf16[80,256]{1,0:T(8,128)(2,1)S(1)} %add_convert_fusion.1.own_ref, bf16[80,256]{1,0:T(8,128)(2,1)S(1)} %collective-permute-done.5.mate_ref.named_ref, ...), custom_call_target="tpu_custom_call" | custom-call | tf_op jit(solution)/shard_map/push/pallas_call | solution.py:28
  14.1 0.0 collective-permute-done.4.refs_4_.across_ref.refs_2_
  14.1 0.8 %collective-permute-start.6 = (bf16[256,512]{1,0:T(8,128)(2,1)S(1)}, bf16[256,512]{1,0:T(8,128)(2,1)S(1)}, u32[]{:S(2)}, u32[]{:S(2)}) collective-permute-start(bf16[256,512]{1,0:T(8,128)(2,1)S(1)} %collective-permute-done.4.refs_4_.across_ref.refs_2_), channel_id=1, source_target_pairs={{0,1},{1,0},{2,3},{3,2},{4,5},{5,4},{6,7},{7,6},{8,9},{9,8},{10,11... | collective-permute-start | bytes 786440 | tf_op jit(solution)/shard_map/ppermute | solution.py:208
  14.9 2.7 %collective-permute-start.8 = (bf16[80,256]{1,0:T(8,128)(2,1)S(1)}, bf16[80,256]{1,0:T(8,128)(2,1)S(1)}, u32[]{:S(2)}, u32[]{:S(2)}) collective-permute-start(bf16[80,256]{1,0:T(8,128)(2,1)S(1)} %get-tuple-element.46), channel_id=1, source_target_pairs={{0,24},{4,28},{8,16},{12,20},{16,8},{20,12},{24,0},{28,4},{1,25},{... | collective-permute-start | bytes 122888 | tf_op jit(solution)/shard_map/ppermute | solution.py:311
  17.6 0.1 collective-permute-start.9
  17.7 0.0 collective-permute-done.3.refs_3_.mate_ref.refs_1_
  17.7 1.6 %collective-permute-start.7 = (bf16[80,256]{1,0:T(8,128)(2,1)S(1)}, bf16[80,256]{1,0:T(8,128)(2,1)S(1)}, u32[]{:S(2)}, u32[]{:S(2)}) collective-permute-start(bf16[80,256]{1,0:T(8,128)(2,1)S(1)} %get-tuple-element.45), channel_id=1, source_target_pairs={{0,8},{4,12},{8,0},{12,4},{16,24},{20,28},{24,16},{28,20},{1,9},{5... | collective-permute-start | bytes 122888 | tf_op jit(solution)/shard_map/ppermute | solution.py:311
  19.3 0.2 pick_even.1
  19.5 0.1 collective-permute-start.13
  19.6 1.3 %collective-permute-done.8.refs_1_ = bf16[80,256]{1,0:T(8,128)(2,1)S(1)} collective-permute-done((bf16[80,256]{1,0:T(8,128)(2,1)S(1)}, bf16[80,256]{1,0:T(8,128)(2,1)S(1)}, u32[]{:S(2)}, u32[]{:S(2)}) %collective-permute-start.8) | collective-permute-done | bytes 40992 | tf_op jit(solution)/shard_map/ppermute | solution.py:311
  20.9 1.8 %collective-permute-done.9 = bf16[80,256]{1,0:T(8,128)(2,1)S(1)} collective-permute-done((bf16[80,256]{1,0:T(8,128)(2,1)S(1)}, bf16[80,256]{1,0:T(8,128)(2,1)S(1)}, u32[]{:S(2)}, u32[]{:S(2)}) %collective-permute-start.9) | collective-permute-done | bytes 40992 | tf_op jit(solution)/shard_map/ppermute | solution.py:311
  22.7 0.4 %collective-permute-done.7.refs_0_ = bf16[80,256]{1,0:T(8,128)(2,1)S(1)} collective-permute-done((bf16[80,256]{1,0:T(8,128)(2,1)S(1)}, bf16[80,256]{1,0:T(8,128)(2,1)S(1)}, u32[]{:S(2)}, u32[]{:S(2)}) %collective-permute-start.7) | collective-permute-done | bytes 40992 | tf_op jit(solution)/shard_map/ppermute | solution.py:311
  23.0 0.2 pick_odd.1
  23.2 2.1 %collective-permute-start.14 = (bf16[256,512]{1,0:T(8,128)(2,1)S(1)}, bf16[256,512]{1,0:T(8,128)(2,1)S(1)}, u32[]{:S(2)}, u32[]{:S(2)}) collective-permute-start(bf16[256,512]{1,0:T(8,128)(2,1)S(1)} %pick_odd.1), channel_id=1, source_target_pairs={{4,8},{12,16},{20,24},{8,4},{16,12},{24,20},{5,9},{13,17},{21,25},... | collective-permute-start | bytes 786440 | tf_op jit(solution)/shard_map/ppermute | solution.py:225
  25.3 0.6 %collective-permute-start.12 = (bf16[64,256]{1,0:T(8,128)(2,1)S(1)}, bf16[64,256]{1,0:T(8,128)(2,1)S(1)}, u32[]{:S(2)}, u32[]{:S(2)}) collective-permute-start(bf16[64,256]{1,0:T(8,128)(2,1)S(1)} %add_convert_fusion.2.field0), channel_id=1, source_target_pairs={{0,3},{1,2},{2,1},{3,0},{4,7},{5,6},{6,5},{7,4},{8,11},{9,10},{10,... | collective-permute-start | bytes 98312 | tf_op jit(solution)/shard_map/ppermute | solution.py:208
  25.9 1.0 %collective-permute-start.11 = (bf16[64,256]{1,0:T(8,128)(2,1)S(1)}, bf16[64,256]{1,0:T(8,128)(2,1)S(1)}, u32[]{:S(2)}, u32[]{:S(2)}) collective-permute-start(bf16[64,256]{1,0:T(8,128)(2,1)S(1)} %add_convert_fusion.2.field0), channel_id=1, source_target_pairs={{0,2},{1,3},{2,0},{3,1},{4,6},{5,7},{6,4},{7,5},{8,10},{9,11},{10,... | collective-permute-start | bytes 98312 | tf_op jit(solution)/shard_map/ppermute | solution.py:208
  27.0 0.3 collective-permute-start.10
  27.9 1.1 %collective-permute-done.12.field3 = bf16[64,256]{1,0:T(8,128)(2,1)S(1)} collective-permute-done((bf16[64,256]{1,0:T(8,128)(2,1)S(1)}, bf16[64,256]{1,0:T(8,128)(2,1)S(1)}, u32[]{:S(2)}, u32[]{:S(2)}) %collective-permute-start.12) | collective-permute-done | bytes 32800 | tf_op jit(solution)/shard_map/ppermute | solution.py:208
  29.0 1.1 %collective-permute-done.11.field2 = bf16[64,256]{1,0:T(8,128)(2,1)S(1)} collective-permute-done((bf16[64,256]{1,0:T(8,128)(2,1)S(1)}, bf16[64,256]{1,0:T(8,128)(2,1)S(1)}, u32[]{:S(2)}, u32[]{:S(2)}) %collective-permute-start.11) | collective-permute-done | bytes 32800 | tf_op jit(solution)/shard_map/ppermute | solution.py:208
  30.1 1.2 %near.1.acc_ref = f32[256,512]{1,0:T(8,128)S(1)} custom-call(bf16[256,512]{1,0:T(8,128)(2,1)S(1)} %get-tuple-element.29.refs_2_.x_ref.refs_0_, bf16[256,512]{1,0:T(8,128)(2,1)S(1)} %collective-permute-done.3.refs_3_.mate_ref.refs_1_, bf16[256,512]{1,0:T(8,128)(2,1)S(1)} %collective-permute-done.4.refs_4_.across_ref.refs_2_, ...), custom_call_target="tpu_custom_call" | custom-call | tf_op jit(solution)/shard_map/near/pallas_call | solution.py:28
  31.3 2.9 %collective-permute-done.14.odd_ref = bf16[256,512]{1,0:T(8,128)(2,1)S(1)} collective-permute-done((bf16[256,512]{1,0:T(8,128)(2,1)S(1)}, bf16[256,512]{1,0:T(8,128)(2,1)S(1)}, u32[]{:S(2)}, u32[]{:S(2)}) %collective-permute-start.14) | collective-permute-done | bytes 262176 | tf_op jit(solution)/shard_map/ppermute | solution.py:225
  34.3 1.3 %finish.1 = bf16[256,512]{1,0:T(8,128)(2,1)} custom-call(f32[256,512]{1,0:T(8,128)S(1)} %near.1.acc_ref, bf16[256,512]{1,0:T(8,128)(2,1)S(1)} %collective-permute-done.13.even_ref, bf16[256,512]{1,0:T(8,128)(2,1)S(1)} %collective-permute-done.14.odd_ref, bf16[1,4,512,512]{3,2,1,0:T(8,128)(2,1)S(1)} %copy-done, s32[1,4]{1,0:T(1,128)S(1)} %copy-done.2, ...), custom_call_target="tpu_custom_call" | custom-call | tf_op jit(solution)/shard_map/finish/pallas_call | solution.py:28
  (16 shorter events, 0.1 us)
Async XLA Ops:
  0.0 3.8 %copy-start.3 = (bf16[256,512]{1,0:T(8,128)(2,1)S(1)}, bf16[256,512]{1,0:T(8,128)(2,1)}, u32[]{:S(2)}) copy-start(bf16[256,512]{1,0:T(8,128)(2,1)} %x_hbm.1) | copy-start | bytes 786436
  0.0 11.8 %copy-start.1 = (s32[6,8,2]{1,2,0:T(2,128)S(1)}, s32[6,8,2]{1,2,0:T(2,128)}, u32[]{:S(2)}) copy-start(s32[6,8,2]{1,2,0:T(2,128)} %param.15) | copy-start | bytes 1156
  1.9 1.3 %collective-permute-start = (bf16[160,256]{1,0:T(8,128)(2,1)S(1)}, bf16[160,256]{1,0:T(8,128)(2,1)S(1)}, u32[]{:S(2)}, u32[]{:S(2)}) collective-permute-start(bf16[160,256]{1,0:T(8,128)(2,1)S(1)} %get-tuple-element.31), channel_id=1, source_target_pairs={{0,1},{1,0},{2,3},{3,2},{4,5},{5,4},{6,7},{7,6},{8,9},{9,8},{10,11... | collective-permute-start | bytes 245768 | tf_op jit(solution)/shard_map/ppermute | solution.py:208
  3.2 26.9 %copy-start = (bf16[1,4,512,512]{3,2,1,0:T(8,128)(2,1)S(1)}, bf16[1,4,512,512]{3,2,1,0:T(8,128)(2,1)}, u32[]{:S(2)}) copy-start(bf16[1,4,512,512]{3,2,1,0:T(8,128)(2,1)} %tiles_ref.3) | copy-start | bytes 6291460
  3.2 26.9 %copy-start.2 = (s32[1,4]{1,0:T(1,128)S(1)}, s32[1,4]{1,0:T(1,128)}, u32[]{:S(2)}) copy-start(s32[1,4]{1,0:T(1,128)} %cols_ref.3) | copy-start | bytes 52
  3.2 4.5 %collective-permute-start.1 = (bf16[80,256]{1,0:T(8,128)(2,1)S(1)}, bf16[80,256]{1,0:T(8,128)(2,1)S(1)}, u32[]{:S(2)}, u32[]{:S(2)}) collective-permute-start(bf16[80,256]{1,0:T(8,128)(2,1)S(1)} %slice.21), channel_id=1, source_target_pairs={{0,2},{1,3},{2,0},{3,1},{4,6},{5,7},{6,4},{7,5},{8,10},{9,11},{10,... | collective-permute-start | bytes 122888 | tf_op jit(solution)/shard_map/ppermute | solution.py:208
  3.8 10.3 %collective-permute-start.4 = (bf16[256,512]{1,0:T(8,128)(2,1)S(1)}, bf16[256,512]{1,0:T(8,128)(2,1)S(1)}, u32[]{:S(2)}, u32[]{:S(2)}) collective-permute-start(bf16[256,512]{1,0:T(8,128)(2,1)S(1)} %copy-done.3), channel_id=1, source_target_pairs={{0,2},{1,3},{2,0},{3,1},{4,6},{5,7},{6,4},{7,5},{8,10},{9,11},{10,... | collective-permute-start | bytes 786440 | tf_op jit(solution)/shard_map/ppermute | solution.py:208
  7.7 4.1 %collective-permute-start.5 = (bf16[80,256]{1,0:T(8,128)(2,1)S(1)}, bf16[80,256]{1,0:T(8,128)(2,1)S(1)}, u32[]{:S(2)}, u32[]{:S(2)}) collective-permute-start(bf16[80,256]{1,0:T(8,128)(2,1)S(1)} %add_convert_fusion.1.own_ref), channel_id=1, source_target_pairs={{0,4},{4,0},{8,12},{12,8},{16,20},{20,16},{24,28},{28,24},{1,5},{5... | collective-permute-start | bytes 122888 | tf_op jit(solution)/shard_map/ppermute | solution.py:219
  8.3 9.4 %collective-permute-start.3 = (bf16[256,512]{1,0:T(8,128)(2,1)S(1)}, bf16[256,512]{1,0:T(8,128)(2,1)S(1)}, u32[]{:S(2)}, u32[]{:S(2)}) collective-permute-start(bf16[256,512]{1,0:T(8,128)(2,1)S(1)} %copy-done.3), channel_id=1, source_target_pairs={{0,1},{1,0},{2,3},{3,2},{4,5},{5,4},{6,7},{7,6},{8,9},{9,8},{10,11... | collective-permute-start | bytes 786440 | tf_op jit(solution)/shard_map/ppermute | solution.py:208
  8.3 9.4 %collective-permute-start.2 = (bf16[256,512]{1,0:T(8,128)(2,1)S(1)}, bf16[256,512]{1,0:T(8,128)(2,1)S(1)}, u32[]{:S(2)}, u32[]{:S(2)}) collective-permute-start(bf16[256,512]{1,0:T(8,128)(2,1)S(1)} %copy-done.3), channel_id=1, source_target_pairs={{3,4},{7,8},{11,12},{15,16},{19,20},{23,24},{27,28},{4,3},{8,7},{1... | collective-permute-start | bytes 786440 | tf_op jit(solution)/shard_map/ppermute | solution.py:289
  14.1 3.6 %collective-permute-start.6 = (bf16[256,512]{1,0:T(8,128)(2,1)S(1)}, bf16[256,512]{1,0:T(8,128)(2,1)S(1)}, u32[]{:S(2)}, u32[]{:S(2)}) collective-permute-start(bf16[256,512]{1,0:T(8,128)(2,1)S(1)} %collective-permute-done.4.refs_4_.across_ref.refs_2_), channel_id=1, source_target_pairs={{0,1},{1,0},{2,3},{3,2},{4,5},{5,4},{6,7},{7,6},{8,9},{9,8},{10,11... | collective-permute-start | bytes 786440 | tf_op jit(solution)/shard_map/ppermute | solution.py:208
  14.9 6.0 %collective-permute-start.8 = (bf16[80,256]{1,0:T(8,128)(2,1)S(1)}, bf16[80,256]{1,0:T(8,128)(2,1)S(1)}, u32[]{:S(2)}, u32[]{:S(2)}) collective-permute-start(bf16[80,256]{1,0:T(8,128)(2,1)S(1)} %get-tuple-element.46), channel_id=1, source_target_pairs={{0,24},{4,28},{8,16},{12,20},{16,8},{20,12},{24,0},{28,4},{1,25},{... | collective-permute-start | bytes 122888 | tf_op jit(solution)/shard_map/ppermute | solution.py:311
  17.6 5.1 %collective-permute-start.9 = (bf16[80,256]{1,0:T(8,128)(2,1)S(1)}, bf16[80,256]{1,0:T(8,128)(2,1)S(1)}, u32[]{:S(2)}, u32[]{:S(2)}) collective-permute-start(bf16[80,256]{1,0:T(8,128)(2,1)S(1)} %get-tuple-element.47), channel_id=1, source_target_pairs={{0,16},{4,20},{8,24},{12,28},{16,0},{20,4},{24,8},{28,12},{1,17},{... | collective-permute-start | bytes 122888 | tf_op jit(solution)/shard_map/ppermute | solution.py:311
  17.7 5.3 %collective-permute-start.7 = (bf16[80,256]{1,0:T(8,128)(2,1)S(1)}, bf16[80,256]{1,0:T(8,128)(2,1)S(1)}, u32[]{:S(2)}, u32[]{:S(2)}) collective-permute-start(bf16[80,256]{1,0:T(8,128)(2,1)S(1)} %get-tuple-element.45), channel_id=1, source_target_pairs={{0,8},{4,12},{8,0},{12,4},{16,24},{20,28},{24,16},{28,20},{1,9},{5... | collective-permute-start | bytes 122888 | tf_op jit(solution)/shard_map/ppermute | solution.py:311
  19.5 11.8 %collective-permute-start.13 = (bf16[256,512]{1,0:T(8,128)(2,1)S(1)}, bf16[256,512]{1,0:T(8,128)(2,1)S(1)}, u32[]{:S(2)}, u32[]{:S(2)}) collective-permute-start(bf16[256,512]{1,0:T(8,128)(2,1)S(1)} %pick_even.1), channel_id=1, source_target_pairs={{0,4},{8,12},{16,20},{24,28},{4,0},{12,8},{20,16},{28,24},{1,5},{9... | collective-permute-start | bytes 786440 | tf_op jit(solution)/shard_map/ppermute | solution.py:225
  23.2 11.0 %collective-permute-start.14 = (bf16[256,512]{1,0:T(8,128)(2,1)S(1)}, bf16[256,512]{1,0:T(8,128)(2,1)S(1)}, u32[]{:S(2)}, u32[]{:S(2)}) collective-permute-start(bf16[256,512]{1,0:T(8,128)(2,1)S(1)} %pick_odd.1), channel_id=1, source_target_pairs={{4,8},{12,16},{20,24},{8,4},{16,12},{24,20},{5,9},{13,17},{21,25},... | collective-permute-start | bytes 786440 | tf_op jit(solution)/shard_map/ppermute | solution.py:225
  25.3 3.7 %collective-permute-start.12 = (bf16[64,256]{1,0:T(8,128)(2,1)S(1)}, bf16[64,256]{1,0:T(8,128)(2,1)S(1)}, u32[]{:S(2)}, u32[]{:S(2)}) collective-permute-start(bf16[64,256]{1,0:T(8,128)(2,1)S(1)} %add_convert_fusion.2.field0), channel_id=1, source_target_pairs={{0,3},{1,2},{2,1},{3,0},{4,7},{5,6},{6,5},{7,4},{8,11},{9,10},{10,... | collective-permute-start | bytes 98312 | tf_op jit(solution)/shard_map/ppermute | solution.py:208
  25.9 4.2 %collective-permute-start.11 = (bf16[64,256]{1,0:T(8,128)(2,1)S(1)}, bf16[64,256]{1,0:T(8,128)(2,1)S(1)}, u32[]{:S(2)}, u32[]{:S(2)}) collective-permute-start(bf16[64,256]{1,0:T(8,128)(2,1)S(1)} %add_convert_fusion.2.field0), channel_id=1, source_target_pairs={{0,2},{1,3},{2,0},{3,1},{4,6},{5,7},{6,4},{7,5},{8,10},{9,11},{10,... | collective-permute-start | bytes 98312 | tf_op jit(solution)/shard_map/ppermute | solution.py:208
  27.0 3.1 %collective-permute-start.10 = (bf16[64,256]{1,0:T(8,128)(2,1)S(1)}, bf16[64,256]{1,0:T(8,128)(2,1)S(1)}, u32[]{:S(2)}, u32[]{:S(2)}) collective-permute-start(bf16[64,256]{1,0:T(8,128)(2,1)S(1)} %add_convert_fusion.2.field0), channel_id=1, source_target_pairs={{0,1},{1,0},{2,3},{3,2},{4,5},{5,4},{6,7},{7,6},{8,9},{9,8},{10,11... | collective-permute-start | bytes 98312 | tf_op jit(solution)/shard_map/ppermute | solution.py:208

commit v2 on v1

--- a/solution.py
+++ b/solution.py
@@ -162,7 +162,7 @@
 
 
 def near_kernel(
-    x_ref, mate_ref, across_ref, corner_ref, edge_ref, tiles_ref, w_ref, field0, field1, field2,
+    x_ref, mate_ref, across_ref, corner_ref, tiles_ref, w_ref, field0, field1, field2,
     field3, cols_ref, count_ref, acc_ref, field_ref
 ):
     pos = lax.axis_index("level")
@@ -170,11 +170,13 @@
         field_ref[part_of(pos ^ turn)] = part_ref[...]
     field = jnp.concatenate([field_ref[part] for part in range(GROUP)], axis=0)
     odd = pos & 1
-    inner = jnp.logical_or(pos == 1, pos == 2)
     acc = dot(x_ref[...], tiles_ref[0, 0]) + dot(mate_ref[...], tiles_ref[0, 2 - odd])
-    beside = jnp.where(inner, corner_ref[...], edge_ref[...])
-    acc = acc + dot(beside, tiles_ref[0, 1 + odd])
     acc_ref[...] = acc + dot_t(field, w_ref[...])
+
+    @pl.when(is_inner(pos))
+    def _():
+        acc_ref[...] += dot(corner_ref[...], tiles_ref[0, 1 + odd])
+
     col = cols_ref[0, SLOT]
     turn = lax.rem(col, GROUP) ^ pos
     here = jnp.logical_and(count_ref[0] > SLOT, col // GROUP == 1)
@@ -184,20 +186,37 @@
             acc_ref[...] += dot(block[...], tiles_ref[0, SLOT])
 
 
-def finish_kernel(acc_ref, even_ref, odd_ref, tiles_ref, cols_ref, count_ref, out_ref):
+def finish_kernel(
+    acc_ref, even_ref, odd_ref, edge_ref, tiles_ref, cols_ref, count_ref, out_ref, total_ref
+):
     side = lax.axis_index("leaf") & 1
+    pos = lax.axis_index("level")
     group = cols_ref[0, SLOT] // GROUP
     live = jnp.logical_and(count_ref[0] > SLOT, group != 1)
     from_even = (group == 0) == (side == 1)
 
+    outer = jnp.logical_not(is_inner(pos))
+
+    @pl.when(outer)
+    def _():
+        total_ref[...] = acc_ref[...] + dot(edge_ref[...], tiles_ref[0, 1 + (pos & 1)])
+
+    @pl.when(jnp.logical_not(outer))
+    def _():
+        total_ref[...] = acc_ref[...]
+
     @pl.when(jnp.logical_not(live))
     def _():
-        out_ref[...] = acc_ref[...].astype(BF16)
+        out_ref[...] = total_ref[...].astype(BF16)
 
     for here, block in ((from_even, even_ref), (jnp.logical_not(from_even), odd_ref)):
         @pl.when(jnp.logical_and(live, here))
         def _(block=block):
-            out_ref[...] = (acc_ref[...] + dot(block[...], tiles_ref[0, SLOT])).astype(BF16)
+            out_ref[...] = (total_ref[...] + dot(block[...], tiles_ref[0, SLOT])).astype(BF16)
+
+
+def is_inner(pos):
+    return jnp.logical_and(pos > 0, pos < GROUP - 1)
 
 
 def part_of(pos):
@@ -283,14 +302,12 @@
     )
     chip_sum = (keep.astype(F32) + turned(send, 1).astype(F32)).astype(BF16)
     came_half = turned(chip_sum[rows + TAIL :], 2)
+    mate = turned(points_x, 1)
+    mate, came_half = lax.optimization_barrier((mate, came_half))
     coef = (chip_sum[: rows + TAIL].astype(F32) + came_half.astype(F32)).astype(BF16)
-    sent, coef = lax.optimization_barrier((points_x, coef))
-    joints = [(GROUP * g - 1, GROUP * g) for g in range(1, leaf_count)]
-    edge = lax.ppermute(sent, ("leaf", "level"), joints + [(b, a) for a, b in joints])
     beside = swapped(coef, 0)
 
     across = turned(points_x, 2)
-    mate = turned(points_x, 1)
 
     active = min(coupling.shape[0], leaf_count.bit_length())
     pairs = leaf_count // 2
@@ -303,7 +320,7 @@
     )
     across, pushes = lax.optimization_barrier((across, pushes))
     corner = turned(across, 1)
-    edge, mate, corner, pushes[0] = lax.optimization_barrier((edge, mate, corner, pushes[0]))
+    corner, pushes[0] = lax.optimization_barrier((corner, pushes[0]))
     held = [own_x, mate, across, corner]
     came = {}
     for turn, push in zip(turns, pushes):
@@ -327,16 +344,18 @@
     (to_odd,) = call(
         partial(pick_odd_kernel, rows, pairs, len(named)), "pick_odd", named + held, [], [block]
     )
-    field, to_odd = lax.optimization_barrier((field, to_odd))
+    sent, field, to_odd = lax.optimization_barrier((points_x, field, to_odd))
+    joints = [(GROUP * g - 1, GROUP * g) for g in range(1, leaf_count)]
+    edge = lax.ppermute(sent, ("leaf", "level"), joints + [(b, a) for a, b in joints])
     fields = [field] + [turned(field, turn) for turn in range(1, GROUP)]
     from_odd = neighbours(to_odd, 1)
     (acc,) = call(
-        near_kernel, "near", held + [edge, near_tiles, w] + fields, [near_cols, near_count],
+        near_kernel, "near", held + [near_tiles, w] + fields, [near_cols, near_count],
         [((vectors, points), F32)], [pltpu.VMEM((GROUP, rows, rank), BF16)],
     )
     (out,) = call(
-        finish_kernel, "finish", [acc, from_even, from_odd, near_tiles], [near_cols, near_count],
-        [block],
+        finish_kernel, "finish", [acc, from_even, from_odd, edge, near_tiles],
+        [near_cols, near_count], [block], [pltpu.VMEM((vectors, points), F32)],
     )
     return out
 

time: 35.7 us -> 41.4 us (1.16)
  the two profiles are of different devices: /device:TPU:6 before, /device:TPU:0 now
where the time goes in v2:
time: 41.4 us; the launch traced here: 41.2 us
  starting transfers between devices  19.7 us (48%)
  waiting for transfers between devices  13.5 us (33%)
  Pallas kernels  7.11 us (17%)
  between operations  0.77 us (2%)
    ppermute x8, starting transfers between devices, turned(): return lax.ppermute(value, 'level', [(i, i ^ turn) for i in range(GROUP)])  9.62 us
    ppermute x8, waiting for transfers between devices, turned(): return lax.ppermute(value, 'level', [(i, i ^ turn) for i in range(GROUP)])  9.31 us
    pallas_call x6, Pallas kernels, call(): pl.pallas_call(kernel, out_shape=shapes, in_specs=[pl.BlockSpec(memory_sp...  7.11 us
    ppermute x3, starting transfers between devices, per_device(): lax.ppermute(push, 'leaf', [(i, i ^ 2 * turn) for i in range(leaf_count)])  4.66 us
    ppermute x2, starting transfers between devices, neighbours(): return lax.ppermute(value, 'leaf', route + [(b, a) for a, b in route])  2.52 us
    ppermute x3, waiting for transfers between devices, per_device(): lax.ppermute(push, 'leaf', [(i, i ^ 2 * turn) for i in range(leaf_count)])  2.25 us
    ppermute x1, starting transfers between devices, swapped(): lax.ppermute(value, 'leaf', [(i, i ^ 1 << distance) for i in range(count)])  2.24 us
    ppermute x1, waiting for transfers between devices, swapped(): lax.ppermute(value, 'leaf', [(i, i ^ 1 << distance) for i in range(count)])  1.98 us
  transfers between devices with their start and end apart: 15, of which 6 were waited for; matrix products, arithmetic and copies ran while one was open for 0% of the time, Pallas kernels for 9%

profile of v2, /device:TPU:0, one launch (start us, length us, event | category | flops | bytes accessed | tf_op | source)
XLA Modules:
  0.0 41.2 jit_solution(5426949881470881831)
XLA Ops:
  0.0 1.8 %up.1 = (bf16[160,256]{1,0:T(8,128)(2,1)S(1)}, bf16[160,256]{1,0:T(8,128)(2,1)S(1)}, bf16[512,256]{1,0:T(8,128)(2,1)S(1)}, bf16[256,512]{1,0:T(8,128)(2,1)S(1)},...) custom-call(bf16[256,512]{1,0:T(8,128)(2,1)} %x_hbm.1, bf16[1,512,256]{2,1,0:T(8,128)(2,1)} %basis_hbm.1, ...), custom_call_target="tpu_custom_call" | custom-call | tf_op jit(solution)/shard_map/up/pallas_call | solution.py:28
  1.9 0.5 %collective-permute-start.1 = (bf16[160,256]{1,0:T(8,128)(2,1)S(1)}, bf16[160,256]{1,0:T(8,128)(2,1)S(1)}, u32[]{:S(2)}, u32[]{:S(2)}) collective-permute-start(bf16[160,256]{1,0:T(8,128)(2,1)S(1)} %get-tuple-element.30), channel_id=1, source_target_pairs={{0,1},{1,0},{2,3},{3,2},{4,5},{5,4},{6,7},{7,6},{8,9},{9,8},{10,11... | collective-permute-start | bytes 245768 | tf_op jit(solution)/shard_map/ppermute | solution.py:227
  2.4 0.1 collective-permute-start
  2.5 0.8 %collective-permute-done.1 = bf16[160,256]{1,0:T(8,128)(2,1)S(1)} collective-permute-done((bf16[160,256]{1,0:T(8,128)(2,1)S(1)}, bf16[160,256]{1,0:T(8,128)(2,1)S(1)}, u32[]{:S(2)}, u32[]{:S(2)}) %collective-permute-start.1) | collective-permute-done | bytes 81952 | tf_op jit(solution)/shard_map/ppermute | solution.py:227
  3.3 2.9 %collective-permute-start.2 = (bf16[80,256]{1,0:T(8,128)(2,1)S(1)}, bf16[80,256]{1,0:T(8,128)(2,1)S(1)}, u32[]{:S(2)}, u32[]{:S(2)}) collective-permute-start(bf16[80,256]{1,0:T(8,128)(2,1)S(1)} %slice.20), channel_id=1, source_target_pairs={{0,2},{1,3},{2,0},{3,1},{4,6},{5,7},{6,4},{7,5},{8,10},{9,11},{10,... | collective-permute-start | bytes 122888 | tf_op jit(solution)/shard_map/ppermute | solution.py:227
  6.2 0.1 collective-permute-start.3
  6.3 1.9 %collective-permute-done.2 = bf16[80,256]{1,0:T(8,128)(2,1)S(1)} collective-permute-done((bf16[80,256]{1,0:T(8,128)(2,1)S(1)}, bf16[80,256]{1,0:T(8,128)(2,1)S(1)}, u32[]{:S(2)}, u32[]{:S(2)}) %collective-permute-start.2) | collective-permute-done | bytes 40992 | tf_op jit(solution)/shard_map/ppermute | solution.py:227
  8.2 0.0 collective-permute-done.refs_3_.mate_ref.refs_1_
  8.2 2.2 %collective-permute-start.4 = (bf16[80,256]{1,0:T(8,128)(2,1)S(1)}, bf16[80,256]{1,0:T(8,128)(2,1)S(1)}, u32[]{:S(2)}, u32[]{:S(2)}) collective-permute-start(bf16[80,256]{1,0:T(8,128)(2,1)S(1)} %add_convert_fusion.1.own_ref), channel_id=1, source_target_pairs={{0,4},{4,0},{8,12},{12,8},{16,20},{20,16},{24,28},{28,24},{1,5},{5... | collective-permute-start | bytes 122888 | tf_op jit(solution)/shard_map/ppermute | solution.py:238
  10.5 2.0 %collective-permute-done.4.mate_ref.named_ref = bf16[80,256]{1,0:T(8,128)(2,1)S(1)} collective-permute-done((bf16[80,256]{1,0:T(8,128)(2,1)S(1)}, bf16[80,256]{1,0:T(8,128)(2,1)S(1)}, u32[]{:S(2)}, u32[]{:S(2)}) %collective-permute-start.4) | collective-permute-done | bytes 40992 | tf_op jit(solution)/shard_map/ppermute | solution.py:238
  12.5 2.3 %push.1 = (bf16[80,256]{1,0:T(8,128)(2,1)S(1)}, bf16[80,256]{1,0:T(8,128)(2,1)S(1)}, bf16[80,256]{1,0:T(8,128)(2,1)S(1)}, bf16[64,256]{1,0:T(8,128)(2,1)}) custom-call(bf16[80,256]{1,0:T(8,128)(2,1)S(1)} %add_convert_fusion.1.own_ref, bf16[80,256]{1,0:T(8,128)(2,1)S(1)} %collective-permute-done.4.mate_ref.named_ref, ...), custom_call_target="tpu_custom_call" | custom-call | tf_op jit(solution)/shard_map/push/pallas_call | solution.py:28
  14.7 0.0 collective-permute-done.3.refs_4_.across_ref.refs_2_
  14.7 0.0 collective-permute-start.5
  14.7 4.0 %collective-permute-start.7 = (bf16[80,256]{1,0:T(8,128)(2,1)S(1)}, bf16[80,256]{1,0:T(8,128)(2,1)S(1)}, u32[]{:S(2)}, u32[]{:S(2)}) collective-permute-start(bf16[80,256]{1,0:T(8,128)(2,1)S(1)} %get-tuple-element.43), channel_id=1, source_target_pairs={{0,24},{4,28},{8,16},{12,20},{16,8},{20,12},{24,0},{28,4},{1,25},{... | collective-permute-start | bytes 122888 | tf_op jit(solution)/shard_map/ppermute | solution.py:328
  18.8 0.0 collective-permute-start.8
  18.8 0.0 collective-permute-done.5.refs_5_.corner_ref.refs_3_
  18.8 0.6 %collective-permute-start.6 = (bf16[80,256]{1,0:T(8,128)(2,1)S(1)}, bf16[80,256]{1,0:T(8,128)(2,1)S(1)}, u32[]{:S(2)}, u32[]{:S(2)}) collective-permute-start(bf16[80,256]{1,0:T(8,128)(2,1)S(1)} %get-tuple-element.42), channel_id=1, source_target_pairs={{0,8},{4,12},{8,0},{12,4},{16,24},{20,28},{24,16},{28,20},{1,9},{5... | collective-permute-start | bytes 122888 | tf_op jit(solution)/shard_map/ppermute | solution.py:328
  19.4 0.2 pick_even.1
  19.6 1.8 %collective-permute-start.12 = (bf16[256,512]{1,0:T(8,128)(2,1)S(1)}, bf16[256,512]{1,0:T(8,128)(2,1)S(1)}, u32[]{:S(2)}, u32[]{:S(2)}) collective-permute-start(bf16[256,512]{1,0:T(8,128)(2,1)S(1)} %pick_even.1), channel_id=1, source_target_pairs={{0,4},{8,12},{16,20},{24,28},{4,0},{12,8},{20,16},{28,24},{1,5},{9... | collective-permute-start | bytes 786440 | tf_op jit(solution)/shard_map/ppermute | solution.py:244
  21.4 0.0 collective-permute-done.7.refs_1_
  21.4 2.2 %collective-permute-done.8 = bf16[80,256]{1,0:T(8,128)(2,1)S(1)} collective-permute-done((bf16[80,256]{1,0:T(8,128)(2,1)S(1)}, bf16[80,256]{1,0:T(8,128)(2,1)S(1)}, u32[]{:S(2)}, u32[]{:S(2)}) %collective-permute-start.8) | collective-permute-done | bytes 40992 | tf_op jit(solution)/shard_map/ppermute | solution.py:328
  23.7 0.2 pick_odd.1
  23.9 0.7 %collective-permute-start.13 = (bf16[256,512]{1,0:T(8,128)(2,1)S(1)}, bf16[256,512]{1,0:T(8,128)(2,1)S(1)}, u32[]{:S(2)}, u32[]{:S(2)}) collective-permute-start(bf16[256,512]{1,0:T(8,128)(2,1)S(1)} %pick_odd.1), channel_id=1, source_target_pairs={{4,8},{12,16},{20,24},{8,4},{16,12},{24,20},{5,9},{13,17},{21,25},... | collective-permute-start | bytes 786440 | tf_op jit(solution)/shard_map/ppermute | solution.py:244
  24.6 0.7 %collective-permute-start.14 = (bf16[256,512]{1,0:T(8,128)(2,1)S(1)}, bf16[256,512]{1,0:T(8,128)(2,1)S(1)}, u32[]{:S(2)}, u32[]{:S(2)}) collective-permute-start(bf16[256,512]{1,0:T(8,128)(2,1)S(1)} %copy-done.3), channel_id=1, source_target_pairs={{3,4},{7,8},{11,12},{15,16},{19,20},{23,24},{27,28},{4,3},{8,7},{1... | collective-permute-start | bytes 786440 | tf_op jit(solution)/shard_map/ppermute | solution.py:349
  25.2 6.0 %collective-permute-start.11 = (bf16[64,256]{1,0:T(8,128)(2,1)S(1)}, bf16[64,256]{1,0:T(8,128)(2,1)S(1)}, u32[]{:S(2)}, u32[]{:S(2)}) collective-permute-start(bf16[64,256]{1,0:T(8,128)(2,1)S(1)} %add_convert_fusion.2.field0), channel_id=1, source_target_pairs={{0,3},{1,2},{2,1},{3,0},{4,7},{5,6},{6,5},{7,4},{8,11},{9,10},{10,... | collective-permute-start | bytes 98312 | tf_op jit(solution)/shard_map/ppermute | solution.py:227
  31.3 6.0 %collective-permute-done.11.field3 = bf16[64,256]{1,0:T(8,128)(2,1)S(1)} collective-permute-done((bf16[64,256]{1,0:T(8,128)(2,1)S(1)}, bf16[64,256]{1,0:T(8,128)(2,1)S(1)}, u32[]{:S(2)}, u32[]{:S(2)}) %collective-permute-start.11) | collective-permute-done | bytes 32800 | tf_op jit(solution)/shard_map/ppermute | solution.py:227
  37.9 0.0 collective-permute-done.10.field2
  37.9 0.5 %collective-permute-done.9.field1 = bf16[64,256]{1,0:T(8,128)(2,1)S(1)} collective-permute-done((bf16[64,256]{1,0:T(8,128)(2,1)S(1)}, bf16[64,256]{1,0:T(8,128)(2,1)S(1)}, u32[]{:S(2)}, u32[]{:S(2)}) %collective-permute-start.9) | collective-permute-done | bytes 32800 | tf_op jit(solution)/shard_map/ppermute | solution.py:227
  38.5 1.1 %near.1.acc_ref = f32[256,512]{1,0:T(8,128)S(1)} custom-call(bf16[256,512]{1,0:T(8,128)(2,1)S(1)} %get-tuple-element.28.refs_2_.x_ref.refs_0_, bf16[256,512]{1,0:T(8,128)(2,1)S(1)} %collective-permute-done.refs_3_.mate_ref.refs_1_, bf16[256,512]{1,0:T(8,128)(2,1)S(1)} %collective-permute-done.3.refs_4_.across_ref.refs_2_, ...), custom_call_target="tpu_custom_call" | custom-call | tf_op jit(solution)/shard_map/near/pallas_call | solution.py:28
  39.6 0.0 collective-permute-done.12.even_ref
  39.6 0.0 collective-permute-done.14.edge_ref
  39.6 1.6 %finish.1 = bf16[256,512]{1,0:T(8,128)(2,1)} custom-call(f32[256,512]{1,0:T(8,128)S(1)} %near.1.acc_ref, bf16[256,512]{1,0:T(8,128)(2,1)S(1)} %collective-permute-done.12.even_ref, bf16[256,512]{1,0:T(8,128)(2,1)S(1)} %collective-permute-done.13.odd_ref, bf16[256,512]{1,0:T(8,128)(2,1)S(1)} %collective-permute-done.14.edge_ref, ...), custom_call_target="tpu_custom_call" | custom-call | tf_op jit(solution)/shard_map/finish/pallas_call | solution.py:28
  (16 shorter events, 0.1 us)
Async XLA Ops:
  0.0 2.4 %copy-start.3 = (bf16[256,512]{1,0:T(8,128)(2,1)S(1)}, bf16[256,512]{1,0:T(8,128)(2,1)}, u32[]{:S(2)}) copy-start(bf16[256,512]{1,0:T(8,128)(2,1)} %x_hbm.1) | copy-start | bytes 786436
  0.0 12.5 %copy-start.1 = (s32[6,8,2]{1,2,0:T(2,128)S(1)}, s32[6,8,2]{1,2,0:T(2,128)}, u32[]{:S(2)}) copy-start(s32[6,8,2]{1,2,0:T(2,128)} %param.15) | copy-start | bytes 1156
  1.9 1.4 %collective-permute-start.1 = (bf16[160,256]{1,0:T(8,128)(2,1)S(1)}, bf16[160,256]{1,0:T(8,128)(2,1)S(1)}, u32[]{:S(2)}, u32[]{:S(2)}) collective-permute-start(bf16[160,256]{1,0:T(8,128)(2,1)S(1)} %get-tuple-element.30), channel_id=1, source_target_pairs={{0,1},{1,0},{2,3},{3,2},{4,5},{5,4},{6,7},{7,6},{8,9},{9,8},{10,11... | collective-permute-start | bytes 245768 | tf_op jit(solution)/shard_map/ppermute | solution.py:227
  2.4 5.9 %collective-permute-start = (bf16[256,512]{1,0:T(8,128)(2,1)S(1)}, bf16[256,512]{1,0:T(8,128)(2,1)S(1)}, u32[]{:S(2)}, u32[]{:S(2)}) collective-permute-start(bf16[256,512]{1,0:T(8,128)(2,1)S(1)} %copy-done.3), channel_id=1, source_target_pairs={{0,1},{1,0},{2,3},{3,2},{4,5},{5,4},{6,7},{7,6},{8,9},{9,8},{10,11... | collective-permute-start | bytes 786440 | tf_op jit(solution)/shard_map/ppermute | solution.py:227
  3.3 35.2 %copy-start = (bf16[1,4,512,512]{3,2,1,0:T(8,128)(2,1)S(1)}, bf16[1,4,512,512]{3,2,1,0:T(8,128)(2,1)}, u32[]{:S(2)}) copy-start(bf16[1,4,512,512]{3,2,1,0:T(8,128)(2,1)} %tiles_ref.3) | copy-start | bytes 6291460
  3.3 35.2 %copy-start.2 = (s32[1,4]{1,0:T(1,128)S(1)}, s32[1,4]{1,0:T(1,128)}, u32[]{:S(2)}) copy-start(s32[1,4]{1,0:T(1,128)} %cols_ref.3) | copy-start | bytes 52
  3.3 4.9 %collective-permute-start.2 = (bf16[80,256]{1,0:T(8,128)(2,1)S(1)}, bf16[80,256]{1,0:T(8,128)(2,1)S(1)}, u32[]{:S(2)}, u32[]{:S(2)}) collective-permute-start(bf16[80,256]{1,0:T(8,128)(2,1)S(1)} %slice.20), channel_id=1, source_target_pairs={{0,2},{1,3},{2,0},{3,1},{4,6},{5,7},{6,4},{7,5},{8,10},{9,11},{10,... | collective-permute-start | bytes 122888 | tf_op jit(solution)/shard_map/ppermute | solution.py:227
  6.2 8.5 %collective-permute-start.3 = (bf16[256,512]{1,0:T(8,128)(2,1)S(1)}, bf16[256,512]{1,0:T(8,128)(2,1)S(1)}, u32[]{:S(2)}, u32[]{:S(2)}) collective-permute-start(bf16[256,512]{1,0:T(8,128)(2,1)S(1)} %copy-done.3), channel_id=1, source_target_pairs={{0,2},{1,3},{2,0},{3,1},{4,6},{5,7},{6,4},{7,5},{8,10},{9,11},{10,... | collective-permute-start | bytes 786440 | tf_op jit(solution)/shard_map/ppermute | solution.py:227
  8.2 4.2 %collective-permute-start.4 = (bf16[80,256]{1,0:T(8,128)(2,1)S(1)}, bf16[80,256]{1,0:T(8,128)(2,1)S(1)}, u32[]{:S(2)}, u32[]{:S(2)}) collective-permute-start(bf16[80,256]{1,0:T(8,128)(2,1)S(1)} %add_convert_fusion.1.own_ref), channel_id=1, source_target_pairs={{0,4},{4,0},{8,12},{12,8},{16,20},{20,16},{24,28},{28,24},{1,5},{5... | collective-permute-start | bytes 122888 | tf_op jit(solution)/shard_map/ppermute | solution.py:238
  14.7 4.0 %collective-permute-start.5 = (bf16[256,512]{1,0:T(8,128)(2,1)S(1)}, bf16[256,512]{1,0:T(8,128)(2,1)S(1)}, u32[]{:S(2)}, u32[]{:S(2)}) collective-permute-start(bf16[256,512]{1,0:T(8,128)(2,1)S(1)} %collective-permute-done.3.refs_4_.across_ref.refs_2_), channel_id=1, source_target_pairs={{0,1},{1,0},{2,3},{3,2},{4,5},{5,4},{6,7},{7,6},{8,9},{9,8},{10,11... | collective-permute-start | bytes 786440 | tf_op jit(solution)/shard_map/ppermute | solution.py:227
  14.7 6.7 %collective-permute-start.7 = (bf16[80,256]{1,0:T(8,128)(2,1)S(1)}, bf16[80,256]{1,0:T(8,128)(2,1)S(1)}, u32[]{:S(2)}, u32[]{:S(2)}) collective-permute-start(bf16[80,256]{1,0:T(8,128)(2,1)S(1)} %get-tuple-element.43), channel_id=1, source_target_pairs={{0,24},{4,28},{8,16},{12,20},{16,8},{20,12},{24,0},{28,4},{1,25},{... | collective-permute-start | bytes 122888 | tf_op jit(solution)/shard_map/ppermute | solution.py:328
  18.8 4.9 %collective-permute-start.8 = (bf16[80,256]{1,0:T(8,128)(2,1)S(1)}, bf16[80,256]{1,0:T(8,128)(2,1)S(1)}, u32[]{:S(2)}, u32[]{:S(2)}) collective-permute-start(bf16[80,256]{1,0:T(8,128)(2,1)S(1)} %get-tuple-element.44), channel_id=1, source_target_pairs={{0,16},{4,20},{8,24},{12,28},{16,0},{20,4},{24,8},{28,12},{1,17},{... | collective-permute-start | bytes 122888 | tf_op jit(solution)/shard_map/ppermute | solution.py:328
  18.8 4.9 %collective-permute-start.6 = (bf16[80,256]{1,0:T(8,128)(2,1)S(1)}, bf16[80,256]{1,0:T(8,128)(2,1)S(1)}, u32[]{:S(2)}, u32[]{:S(2)}) collective-permute-start(bf16[80,256]{1,0:T(8,128)(2,1)S(1)} %get-tuple-element.42), channel_id=1, source_target_pairs={{0,8},{4,12},{8,0},{12,4},{16,24},{20,28},{24,16},{28,20},{1,9},{5... | collective-permute-start | bytes 122888 | tf_op jit(solution)/shard_map/ppermute | solution.py:328
  19.6 20.0 %collective-permute-start.12 = (bf16[256,512]{1,0:T(8,128)(2,1)S(1)}, bf16[256,512]{1,0:T(8,128)(2,1)S(1)}, u32[]{:S(2)}, u32[]{:S(2)}) collective-permute-start(bf16[256,512]{1,0:T(8,128)(2,1)S(1)} %pick_even.1), channel_id=1, source_target_pairs={{0,4},{8,12},{16,20},{24,28},{4,0},{12,8},{20,16},{28,24},{1,5},{9... | collective-permute-start | bytes 786440 | tf_op jit(solution)/shard_map/ppermute | solution.py:244
  23.9 15.7 %collective-permute-start.13 = (bf16[256,512]{1,0:T(8,128)(2,1)S(1)}, bf16[256,512]{1,0:T(8,128)(2,1)S(1)}, u32[]{:S(2)}, u32[]{:S(2)}) collective-permute-start(bf16[256,512]{1,0:T(8,128)(2,1)S(1)} %pick_odd.1), channel_id=1, source_target_pairs={{4,8},{12,16},{20,24},{8,4},{16,12},{24,20},{5,9},{13,17},{21,25},... | collective-permute-start | bytes 786440 | tf_op jit(solution)/shard_map/ppermute | solution.py:244
  24.6 15.1 %collective-permute-start.14 = (bf16[256,512]{1,0:T(8,128)(2,1)S(1)}, bf16[256,512]{1,0:T(8,128)(2,1)S(1)}, u32[]{:S(2)}, u32[]{:S(2)}) collective-permute-start(bf16[256,512]{1,0:T(8,128)(2,1)S(1)} %copy-done.3), channel_id=1, source_target_pairs={{3,4},{7,8},{11,12},{15,16},{19,20},{23,24},{27,28},{4,3},{8,7},{1... | collective-permute-start | bytes 786440 | tf_op jit(solution)/shard_map/ppermute | solution.py:349
  25.2 12.0 %collective-permute-start.11 = (bf16[64,256]{1,0:T(8,128)(2,1)S(1)}, bf16[64,256]{1,0:T(8,128)(2,1)S(1)}, u32[]{:S(2)}, u32[]{:S(2)}) collective-permute-start(bf16[64,256]{1,0:T(8,128)(2,1)S(1)} %add_convert_fusion.2.field0), channel_id=1, source_target_pairs={{0,3},{1,2},{2,1},{3,0},{4,7},{5,6},{6,5},{7,4},{8,11},{9,10},{10,... | collective-permute-start | bytes 98312 | tf_op jit(solution)/shard_map/ppermute | solution.py:227
  31.3 6.7 %collective-permute-start.10 = (bf16[64,256]{1,0:T(8,128)(2,1)S(1)}, bf16[64,256]{1,0:T(8,128)(2,1)S(1)}, u32[]{:S(2)}, u32[]{:S(2)}) collective-permute-start(bf16[64,256]{1,0:T(8,128)(2,1)S(1)} %add_convert_fusion.2.field0), channel_id=1, source_target_pairs={{0,2},{1,3},{2,0},{3,1},{4,6},{5,7},{6,4},{7,5},{8,10},{9,11},{10,... | collective-permute-start | bytes 98312 | tf_op jit(solution)/shard_map/ppermute | solution.py:227
  37.3 1.2 %collective-permute-start.9 = (bf16[64,256]{1,0:T(8,128)(2,1)S(1)}, bf16[64,256]{1,0:T(8,128)(2,1)S(1)}, u32[]{:S(2)}, u32[]{:S(2)}) collective-permute-start(bf16[64,256]{1,0:T(8,128)(2,1)S(1)} %add_convert_fusion.2.field0), channel_id=1, source_target_pairs={{0,1},{1,0},{2,3},{3,2},{4,5},{5,4},{6,7},{7,6},{8,9},{9,8},{10,11... | collective-permute-start | bytes 98312 | tf_op jit(solution)/shard_map/ppermute | solution.py:227

commit v3 on v1

--- a/solution.py
+++ b/solution.py
@@ -75,43 +75,37 @@
     copies[3].wait()
 
 
-def push_kernel(
-    turns, pairs, clusters, own_ref, mate_ref, coupling_ref, transfer_ref, mask_ref, *refs
-):
-    *push_refs, pair_ref, both_ref = refs
+def fold_kernel(turns, pairs, clusters, coupling_ref, transfer_ref, mask_ref, *fold_refs):
     leaf_pos = lax.axis_index("leaf")
     pair, side = leaf_pos >> 1, leaf_pos & 1
-    rows = both_ref.shape[1]
-    both_ref[side] = own_ref[:rows]
-    both_ref[1 - side] = mate_ref[:rows]
-    total = dot(both_ref[0], transfer_ref[0]) + dot(both_ref[1], transfer_ref[1])
-    pair_ref[...] = total.astype(BF16)
-
-    def term(lev, coef, gap, source, target):
-        pick = abs(gap) - 2
-        matrix = coupling_ref[lev, pick]
-        switch = mask_ref[lev, pick, source if gap > 0 else target].astype(F32)
-        return switch * (dot_t(coef, matrix) if gap > 0 else dot(coef, matrix))
-
-    def fill(push_ref, distance, to_side):
-        target_pair = pair + distance
-        total = None
+
+    def switch(lev, gap, source, target):
+        return mask_ref[lev, abs(gap) - 2, source if gap > 0 else target].astype(F32)
+
+    def fill(fold_ref, distance, to_side):
+        other = pair + distance
+        through = None
         if abs(distance) in (2, 3) and clusters[1]:
-            coupled = term(1, pair_ref[...], distance, pair, target_pair).astype(BF16)
-            total = dot_t(coupled, transfer_ref[to_side])
+            matrix = coupling_ref[1, abs(distance) - 2]
+            on = switch(1, distance, pair, other)
+            if distance > 0:
+                through = dot(transfer_ref[to_side], matrix)
+            else:
+                through = dot_t(matrix, transfer_ref[to_side])
+            through = (on * through).astype(BF16)
         for from_side in (0, 1):
+            total = jnp.zeros(fold_ref.shape[1:], F32)
+            if through is not None:
+                product = dot_t if distance > 0 else dot
+                total = product(transfer_ref[from_side], through)
             gap = 2 * distance + to_side - from_side
             if abs(gap) in (2, 3) and clusters[0]:
-                more = term(
-                    0, both_ref[from_side], gap, 2 * pair + from_side, 2 * target_pair + to_side
-                )
-                total = more if total is None else total + more
-        if total is None:
-            total = jnp.zeros(pair_ref.shape, F32)
-        push_ref[:rows] = total.astype(BF16)
-
-    for turn, push_ref in zip(turns, push_refs):
-        push_ref[rows:] = mate_ref[rows:]
+                matrix = coupling_ref[0, abs(gap) - 2].astype(F32)
+                on = switch(0, gap, 2 * pair + from_side, 2 * other + to_side)
+                total = total + on * (matrix.T if gap > 0 else matrix)
+            fold_ref[from_side] = total.astype(BF16)
+
+    for turn, fold_ref in zip(turns, fold_refs):
         for distance in reached(turn, pairs):
             if pairs == 4:
                 inside = (pair ^ turn) == pair + distance
@@ -119,8 +113,17 @@
                 inside = jnp.logical_and(pair + distance >= 0, pair + distance < pairs)
             for to_side in (0, 1):
                 @pl.when(jnp.logical_and(inside, side == to_side))
-                def _(push_ref=push_ref, distance=distance, to_side=to_side):
-                    fill(push_ref, distance, to_side)
+                def _(fold_ref=fold_ref, distance=distance, to_side=to_side):
+                    fill(fold_ref, distance, to_side)
+
+
+def push_kernel(rows, count, own_ref, mate_ref, *refs):
+    fold_refs, push_refs = refs[:count], refs[count:]
+    side = lax.axis_index("leaf") & 1
+    for fold_ref, push_ref in zip(fold_refs, push_refs):
+        total = dot(own_ref[:rows], fold_ref[side]) + dot(mate_ref[:rows], fold_ref[1 - side])
+        push_ref[:rows] = total.astype(BF16)
+        push_ref[rows:] = mate_ref[rows:]
 
 
 def reached(turn, pairs):
@@ -230,12 +233,14 @@
     leaf_pos = lax.axis_index("leaf")
     couplings = []
     levels = range(2, min(coupling.shape[0], leaf_count.bit_length()))
-    for lev in levels:
+    for lev in range(1, levels.stop):
         other = swapped(coef, lev - 1)
         is_upper = (leaf_pos >> lev - 1 & 1) == 1
         total = dot(jnp.where(is_upper, other, coef), transfer[0])
         total = total + dot(jnp.where(is_upper, coef, other), transfer[1])
         coef = total.astype(BF16)
+        if lev not in levels:
+            continue
         cluster = leaf_pos >> lev
         coupled = jnp.zeros(coef.shape, F32)
         for pick, offset in enumerate((2, 3)):
@@ -283,6 +288,16 @@
     )
     chip_sum = (keep.astype(F32) + turned(send, 1).astype(F32)).astype(BF16)
     came_half = turned(chip_sum[rows + TAIL :], 2)
+    mate = turned(points_x, 1)
+    active = min(coupling.shape[0], leaf_count.bit_length())
+    pairs = leaf_count // 2
+    turns = [2, 1, 3] if pairs == 4 else [2, 1, 3, -1, -2, -3]
+    clusters = [lev < active and (leaf_count >> lev) > 2 for lev in (0, 1)]
+    folds = call(
+        partial(fold_kernel, turns, pairs, clusters), "fold", [coupling_in, transfer_in],
+        [couple_mask.transpose(0, 2, 1)], [((2, rank, rank), BF16)] * len(turns),
+    )
+    mate, came_half, folds = lax.optimization_barrier((mate, came_half, folds))
     coef = (chip_sum[: rows + TAIL].astype(F32) + came_half.astype(F32)).astype(BF16)
     sent, coef = lax.optimization_barrier((points_x, coef))
     joints = [(GROUP * g - 1, GROUP * g) for g in range(1, leaf_count)]
@@ -290,20 +305,15 @@
     beside = swapped(coef, 0)
 
     across = turned(points_x, 2)
-    mate = turned(points_x, 1)
-
-    active = min(coupling.shape[0], leaf_count.bit_length())
-    pairs = leaf_count // 2
-    turns = [1, 3, 2] if pairs == 4 else [1, 2, 3, -1, -2, -3]
-    clusters = [lev < active and (leaf_count >> lev) > 2 for lev in (0, 1)]
-    *pushes, pair_coef = call(
-        partial(push_kernel, turns, pairs, clusters), "push",
-        [coef, beside, coupling_in, transfer_in], [couple_mask.transpose(0, 2, 1)],
-        [tailed] * len(turns) + [part], [pltpu.VMEM((2, rows, rank), BF16)],
-    )
+
+    pushes = call(
+        partial(push_kernel, rows, len(turns)), "push", [coef, beside, *folds], [],
+        [tailed] * len(turns),
+    )
+    pushes = list(pushes)
     across, pushes = lax.optimization_barrier((across, pushes))
     corner = turned(across, 1)
-    edge, mate, corner, pushes[0] = lax.optimization_barrier((edge, mate, corner, pushes[0]))
+    edge, corner, pushes[0] = lax.optimization_barrier((edge, corner, pushes[0]))
     held = [own_x, mate, across, corner]
     came = {}
     for turn, push in zip(turns, pushes):
@@ -313,12 +323,11 @@
             )
         else:
             came[turn] = shifted(push, 2 * turn)
-    came = dict(zip(came, lax.optimization_barrier(list(came.values()))))
-    field = came[1][:rows].astype(F32)
+    field = came[turns[0]][:rows].astype(F32)
     for turn in turns[1:]:
         field = field + came[turn][:rows].astype(F32)
     if active > 2 and (leaf_count >> 2) > 2:
-        field = field + upper_field(pair_coef, coupling, transfer, couple_mask)
+        field = field + upper_field(coef[:rows], coupling, transfer, couple_mask)
     field = field.astype(BF16)
 
     (to_even,) = call(partial(pick_even_kernel, rows), "pick_even", [beside] + held, [], [block])

time: 35.7 us -> 34.8 us (0.975)
  the two profiles are of different devices: /device:TPU:6 before, /device:TPU:8 now
where the time goes in v3:
time: 34.8 us; the launch traced here: 34.6 us
  starting transfers between devices  16.8 us (48%)
  waiting for transfers between devices  10.7 us (31%)
  Pallas kernels  6.22 us (18%)
  between operations  0.81 us (2%)
    ppermute x3, starting transfers between devices, per_device(): lax.ppermute(push, 'leaf', [(i, i ^ 2 * turn) for i in range(leaf_count)])  6.64 us
    pallas_call x7, Pallas kernels, call(): pl.pallas_call(kernel, out_shape=shapes, in_specs=[pl.BlockSpec(memory_sp...  6.22 us
    ppermute x8, waiting for transfers between devices, turned(): return lax.ppermute(value, 'level', [(i, i ^ turn) for i in range(GROUP)])  4.64 us
    ppermute x8, starting transfers between devices, turned(): return lax.ppermute(value, 'level', [(i, i ^ turn) for i in range(GROUP)])  4.59 us
    ppermute x2, starting transfers between devices, neighbours(): return lax.ppermute(value, 'leaf', route + [(b, a) for a, b in route])  2.1 us
    ppermute x2, waiting for transfers between devices, neighbours(): return lax.ppermute(value, 'leaf', route + [(b, a) for a, b in route])  2.07 us
    ppermute x1, starting transfers between devices, per_device(): lax.ppermute(sent, ('leaf', 'level'), joints + [(b, a) for a, b in joints])  1.91 us
    ppermute x3, waiting for transfers between devices, per_device(): lax.ppermute(push, 'leaf', [(i, i ^ 2 * turn) for i in range(leaf_count)])  1.88 us
  transfers between devices with their start and end apart: 15, of which 9 were waited for; matrix products, arithmetic and copies ran while one was open for 0% of the time, Pallas kernels for 9%

profile of v3, /device:TPU:8, one launch (start us, length us, event | category | flops | bytes accessed | tf_op | source)
XLA Modules:
  0.0 34.6 jit_solution(3253310620492988701)
XLA Ops:
  0.0 1.8 %up.1 = (bf16[160,256]{1,0:T(8,128)(2,1)S(1)}, bf16[160,256]{1,0:T(8,128)(2,1)S(1)}, bf16[512,256]{1,0:T(8,128)(2,1)S(1)}, bf16[256,512]{1,0:T(8,128)(2,1)S(1)},...) custom-call(bf16[256,512]{1,0:T(8,128)(2,1)} %x_hbm.1, bf16[1,512,256]{2,1,0:T(8,128)(2,1)} %basis_hbm.1, ...), custom_call_target="tpu_custom_call" | custom-call | tf_op jit(solution)/shard_map/up/pallas_call | solution.py:28
  1.9 0.1 collective-permute-start.1
  1.9 0.5 %collective-permute-start = (bf16[256,512]{1,0:T(8,128)(2,1)S(1)}, bf16[256,512]{1,0:T(8,128)(2,1)S(1)}, u32[]{:S(2)}, u32[]{:S(2)}) collective-permute-start(bf16[256,512]{1,0:T(8,128)(2,1)S(1)} %copy-done.3), channel_id=1, source_target_pairs={{0,1},{1,0},{2,3},{3,2},{4,5},{5,4},{6,7},{7,6},{8,9},{9,8},{10,11... | collective-permute-start | bytes 786440 | tf_op jit(solution)/shard_map/ppermute | solution.py:211
  2.4 0.8 %collective-permute-done.1 = bf16[160,256]{1,0:T(8,128)(2,1)S(1)} collective-permute-done((bf16[160,256]{1,0:T(8,128)(2,1)S(1)}, bf16[160,256]{1,0:T(8,128)(2,1)S(1)}, u32[]{:S(2)}, u32[]{:S(2)}) %collective-permute-start.1) | collective-permute-done | bytes 81952 | tf_op jit(solution)/shard_map/ppermute | solution.py:211
  3.2 1.6 %collective-permute-start.2 = (bf16[80,256]{1,0:T(8,128)(2,1)S(1)}, bf16[80,256]{1,0:T(8,128)(2,1)S(1)}, u32[]{:S(2)}, u32[]{:S(2)}) collective-permute-start(bf16[80,256]{1,0:T(8,128)(2,1)S(1)} %slice.20), channel_id=1, source_target_pairs={{0,2},{1,3},{2,0},{3,1},{4,6},{5,7},{6,4},{7,5},{8,10},{9,11},{10,... | collective-permute-start | bytes 122888 | tf_op jit(solution)/shard_map/ppermute | solution.py:211
  4.8 0.5 %collective-permute-start.3 = (bf16[256,512]{1,0:T(8,128)(2,1)S(1)}, bf16[256,512]{1,0:T(8,128)(2,1)S(1)}, u32[]{:S(2)}, u32[]{:S(2)}) collective-permute-start(bf16[256,512]{1,0:T(8,128)(2,1)S(1)} %copy-done.3), channel_id=1, source_target_pairs={{0,2},{1,3},{2,0},{3,1},{4,6},{5,7},{6,4},{7,5},{8,10},{9,11},{10,... | collective-permute-start | bytes 786440 | tf_op jit(solution)/shard_map/ppermute | solution.py:211
  5.3 1.3 %fold.1 = (bf16[2,256,256]{2,1,0:T(8,128)(2,1)S(1)}, bf16[2,256,256]{2,1,0:T(8,128)(2,1)S(1)}, bf16[2,256,256]{2,1,0:T(8,128)(2,1)S(1)}) custom-call(bf16[2,2,256,256]{3,2,1,0:T(8,128)(2,1)S(1)} %get-tuple-element.36.coupling_ref, bf16[2,256,256]{2,1,0:T(8,128)(2,1)S(1)} %get-tuple-element.37.transfer_ref, s32[6,2,8]{2,1,0:T(2,128)S(1)} %bitcast.1), custom_call_target="tpu_custom_call" | custom-call | tf_op jit(solution)/shard_map/fold/pallas_call | solution.py:28
  6.6 0.0 copy-start
  6.7 0.0 copy-start.2
  6.7 0.8 %collective-permute-done.2 = bf16[80,256]{1,0:T(8,128)(2,1)S(1)} collective-permute-done((bf16[80,256]{1,0:T(8,128)(2,1)S(1)}, bf16[80,256]{1,0:T(8,128)(2,1)S(1)}, u32[]{:S(2)}, u32[]{:S(2)}) %collective-permute-start.2) | collective-permute-done | bytes 40992 | tf_op jit(solution)/shard_map/ppermute | solution.py:211
  7.5 1.6 %collective-permute-start.4 = (bf16[80,256]{1,0:T(8,128)(2,1)S(1)}, bf16[80,256]{1,0:T(8,128)(2,1)S(1)}, u32[]{:S(2)}, u32[]{:S(2)}) collective-permute-start(bf16[80,256]{1,0:T(8,128)(2,1)S(1)} %add_convert_fusion.1.own_ref), channel_id=1, source_target_pairs={{0,4},{4,0},{8,12},{12,8},{16,20},{20,16},{24,28},{28,24},{1,5},{5... | collective-permute-start | bytes 122888 | tf_op jit(solution)/shard_map/ppermute | solution.py:222
  9.0 1.9 %collective-permute-start.5 = (bf16[256,512]{1,0:T(8,128)(2,1)S(1)}, bf16[256,512]{1,0:T(8,128)(2,1)S(1)}, u32[]{:S(2)}, u32[]{:S(2)}) collective-permute-start(bf16[256,512]{1,0:T(8,128)(2,1)S(1)} %copy-done.3), channel_id=1, source_target_pairs={{3,4},{7,8},{11,12},{15,16},{19,20},{23,24},{27,28},{4,3},{8,7},{1... | collective-permute-start | bytes 786440 | tf_op jit(solution)/shard_map/ppermute | solution.py:304
  11.0 0.6 %collective-permute-done.4.mate_ref.named_ref = bf16[80,256]{1,0:T(8,128)(2,1)S(1)} collective-permute-done((bf16[80,256]{1,0:T(8,128)(2,1)S(1)}, bf16[80,256]{1,0:T(8,128)(2,1)S(1)}, u32[]{:S(2)}, u32[]{:S(2)}) %collective-permute-start.4) | collective-permute-done | bytes 40992 | tf_op jit(solution)/shard_map/ppermute | solution.py:222
  11.5 0.3 push.1
  11.8 1.1 %collective-permute-done.3.refs_4_.across_ref.refs_2_ = bf16[256,512]{1,0:T(8,128)(2,1)S(1)} collective-permute-done((bf16[256,512]{1,0:T(8,128)(2,1)S(1)}, bf16[256,512]{1,0:T(8,128)(2,1)S(1)}, u32[]{:S(2)}, u32[]{:S(2)}) %collective-permute-start.3) | collective-permute-done | bytes 262176 | tf_op jit(solution)/shard_map/ppermute | solution.py:211
  12.9 1.6 %collective-permute-start.9 = (bf16[80,256]{1,0:T(8,128)(2,1)S(1)}, bf16[80,256]{1,0:T(8,128)(2,1)S(1)}, u32[]{:S(2)}, u32[]{:S(2)}) collective-permute-start(bf16[80,256]{1,0:T(8,128)(2,1)S(1)} %get-tuple-element.58), channel_id=1, source_target_pairs={{0,24},{4,28},{8,16},{12,20},{16,8},{20,12},{24,0},{28,4},{1,25},{... | collective-permute-start | bytes 122888 | tf_op jit(solution)/shard_map/ppermute | solution.py:321
  14.5 2.5 %collective-permute-start.8 = (bf16[80,256]{1,0:T(8,128)(2,1)S(1)}, bf16[80,256]{1,0:T(8,128)(2,1)S(1)}, u32[]{:S(2)}, u32[]{:S(2)}) collective-permute-start(bf16[80,256]{1,0:T(8,128)(2,1)S(1)} %get-tuple-element.57), channel_id=1, source_target_pairs={{0,8},{4,12},{8,0},{12,4},{16,24},{20,28},{24,16},{28,20},{1,9},{5... | collective-permute-start | bytes 122888 | tf_op jit(solution)/shard_map/ppermute | solution.py:321
  17.0 1.5 %collective-permute-done.5.edge_ref = bf16[256,512]{1,0:T(8,128)(2,1)S(1)} collective-permute-done((bf16[256,512]{1,0:T(8,128)(2,1)S(1)}, bf16[256,512]{1,0:T(8,128)(2,1)S(1)}, u32[]{:S(2)}, u32[]{:S(2)}) %collective-permute-start.5) | collective-permute-done | bytes 262176 | tf_op jit(solution)/shard_map/ppermute | solution.py:304
  18.5 2.6 %collective-permute-start.7 = (bf16[80,256]{1,0:T(8,128)(2,1)S(1)}, bf16[80,256]{1,0:T(8,128)(2,1)S(1)}, u32[]{:S(2)}, u32[]{:S(2)}) collective-permute-start(bf16[80,256]{1,0:T(8,128)(2,1)S(1)} %get-tuple-element.56), channel_id=1, source_target_pairs={{0,16},{4,20},{8,24},{12,28},{16,0},{20,4},{24,8},{28,12},{1,17},{... | collective-permute-start | bytes 122888 | tf_op jit(solution)/shard_map/ppermute | solution.py:321
  21.1 0.2 pick_even.1
  21.3 0.1 collective-permute-start.13
  21.4 0.2 pick_odd.1
  21.5 1.9 %collective-permute-done.7 = bf16[80,256]{1,0:T(8,128)(2,1)S(1)} collective-permute-done((bf16[80,256]{1,0:T(8,128)(2,1)S(1)}, bf16[80,256]{1,0:T(8,128)(2,1)S(1)}, u32[]{:S(2)}, u32[]{:S(2)}) %collective-permute-start.7) | collective-permute-done | bytes 40992 | tf_op jit(solution)/shard_map/ppermute | solution.py:321
  23.4 2.0 %collective-permute-start.14 = (bf16[256,512]{1,0:T(8,128)(2,1)S(1)}, bf16[256,512]{1,0:T(8,128)(2,1)S(1)}, u32[]{:S(2)}, u32[]{:S(2)}) collective-permute-start(bf16[256,512]{1,0:T(8,128)(2,1)S(1)} %pick_odd.1), channel_id=1, source_target_pairs={{4,8},{12,16},{20,24},{8,4},{16,12},{24,20},{5,9},{13,17},{21,25},... | collective-permute-start | bytes 786440 | tf_op jit(solution)/shard_map/ppermute | solution.py:228
  25.5 0.1 collective-permute-start.10
  25.6 0.8 %collective-permute-start.11 = (bf16[64,256]{1,0:T(8,128)(2,1)S(1)}, bf16[64,256]{1,0:T(8,128)(2,1)S(1)}, u32[]{:S(2)}, u32[]{:S(2)}) collective-permute-start(bf16[64,256]{1,0:T(8,128)(2,1)S(1)} %add_convert_fusion.2.field0), channel_id=1, source_target_pairs={{0,2},{1,3},{2,0},{3,1},{4,6},{5,7},{6,4},{7,5},{8,10},{9,11},{10,... | collective-permute-start | bytes 98312 | tf_op jit(solution)/shard_map/ppermute | solution.py:211
  26.4 1.1 %collective-permute-start.12 = (bf16[64,256]{1,0:T(8,128)(2,1)S(1)}, bf16[64,256]{1,0:T(8,128)(2,1)S(1)}, u32[]{:S(2)}, u32[]{:S(2)}) collective-permute-start(bf16[64,256]{1,0:T(8,128)(2,1)S(1)} %add_convert_fusion.2.field0), channel_id=1, source_target_pairs={{0,3},{1,2},{2,1},{3,0},{4,7},{5,6},{6,5},{7,4},{8,11},{9,10},{10,... | collective-permute-start | bytes 98312 | tf_op jit(solution)/shard_map/ppermute | solution.py:211
  28.1 1.6 %collective-permute-done.11.field2 = bf16[64,256]{1,0:T(8,128)(2,1)S(1)} collective-permute-done((bf16[64,256]{1,0:T(8,128)(2,1)S(1)}, bf16[64,256]{1,0:T(8,128)(2,1)S(1)}, u32[]{:S(2)}, u32[]{:S(2)}) %collective-permute-start.11) | collective-permute-done | bytes 32800 | tf_op jit(solution)/shard_map/ppermute | solution.py:211
  29.7 0.3 collective-permute-done.12.field3
  30.0 1.2 %near.1.acc_ref = f32[256,512]{1,0:T(8,128)S(1)} custom-call(bf16[256,512]{1,0:T(8,128)(2,1)S(1)} %get-tuple-element.33.refs_2_.x_ref.refs_0_, bf16[256,512]{1,0:T(8,128)(2,1)S(1)} %collective-permute-done.refs_3_.mate_ref.refs_1_, bf16[256,512]{1,0:T(8,128)(2,1)S(1)} %collective-permute-done.3.refs_4_.across_ref.refs_2_, ...), custom_call_target="tpu_custom_call" | custom-call | tf_op jit(solution)/shard_map/near/pallas_call | solution.py:28
  31.3 2.1 %collective-permute-done.13.even_ref = bf16[256,512]{1,0:T(8,128)(2,1)S(1)} collective-permute-done((bf16[256,512]{1,0:T(8,128)(2,1)S(1)}, bf16[256,512]{1,0:T(8,128)(2,1)S(1)}, u32[]{:S(2)}, u32[]{:S(2)}) %collective-permute-start.13) | collective-permute-done | bytes 262176 | tf_op jit(solution)/shard_map/ppermute | solution.py:228
  33.3 1.3 %finish.1 = bf16[256,512]{1,0:T(8,128)(2,1)} custom-call(f32[256,512]{1,0:T(8,128)S(1)} %near.1.acc_ref, bf16[256,512]{1,0:T(8,128)(2,1)S(1)} %collective-permute-done.13.even_ref, bf16[256,512]{1,0:T(8,128)(2,1)S(1)} %collective-permute-done.14.odd_ref, bf16[1,4,512,512]{3,2,1,0:T(8,128)(2,1)S(1)} %copy-done, s32[1,4]{1,0:T(1,128)S(1)} %copy-done.2, ...), custom_call_target="tpu_custom_call" | custom-call | tf_op jit(solution)/shard_map/finish/pallas_call | solution.py:28
  (17 shorter events, 0.1 us)
Async XLA Ops:
  0.0 1.9 %copy-start.3 = (bf16[256,512]{1,0:T(8,128)(2,1)S(1)}, bf16[256,512]{1,0:T(8,128)(2,1)}, u32[]{:S(2)}) copy-start(bf16[256,512]{1,0:T(8,128)(2,1)} %x_hbm.1) | copy-start | bytes 786436
  0.0 5.3 %copy-start.1 = (s32[6,8,2]{1,2,0:T(2,128)S(1)}, s32[6,8,2]{1,2,0:T(2,128)}, u32[]{:S(2)}) copy-start(s32[6,8,2]{1,2,0:T(2,128)} %param.15) | copy-start | bytes 1156
  1.9 1.3 %collective-permute-start.1 = (bf16[160,256]{1,0:T(8,128)(2,1)S(1)}, bf16[160,256]{1,0:T(8,128)(2,1)S(1)}, u32[]{:S(2)}, u32[]{:S(2)}) collective-permute-start(bf16[160,256]{1,0:T(8,128)(2,1)S(1)} %get-tuple-element.35), channel_id=1, source_target_pairs={{0,1},{1,0},{2,3},{3,2},{4,5},{5,4},{6,7},{7,6},{8,9},{9,8},{10,11... | collective-permute-start | bytes 245768 | tf_op jit(solution)/shard_map/ppermute | solution.py:211
  1.9 5.5 %collective-permute-start = (bf16[256,512]{1,0:T(8,128)(2,1)S(1)}, bf16[256,512]{1,0:T(8,128)(2,1)S(1)}, u32[]{:S(2)}, u32[]{:S(2)}) collective-permute-start(bf16[256,512]{1,0:T(8,128)(2,1)S(1)} %copy-done.3), channel_id=1, source_target_pairs={{0,1},{1,0},{2,3},{3,2},{4,5},{5,4},{6,7},{7,6},{8,9},{9,8},{10,11... | collective-permute-start | bytes 786440 | tf_op jit(solution)/shard_map/ppermute | solution.py:211
  3.2 4.2 %collective-permute-start.2 = (bf16[80,256]{1,0:T(8,128)(2,1)S(1)}, bf16[80,256]{1,0:T(8,128)(2,1)S(1)}, u32[]{:S(2)}, u32[]{:S(2)}) collective-permute-start(bf16[80,256]{1,0:T(8,128)(2,1)S(1)} %slice.20), channel_id=1, source_target_pairs={{0,2},{1,3},{2,0},{3,1},{4,6},{5,7},{6,4},{7,5},{8,10},{9,11},{10,... | collective-permute-start | bytes 122888 | tf_op jit(solution)/shard_map/ppermute | solution.py:211
  4.8 8.1 %collective-permute-start.3 = (bf16[256,512]{1,0:T(8,128)(2,1)S(1)}, bf16[256,512]{1,0:T(8,128)(2,1)S(1)}, u32[]{:S(2)}, u32[]{:S(2)}) collective-permute-start(bf16[256,512]{1,0:T(8,128)(2,1)S(1)} %copy-done.3), channel_id=1, source_target_pairs={{0,2},{1,3},{2,0},{3,1},{4,6},{5,7},{6,4},{7,5},{8,10},{9,11},{10,... | collective-permute-start | bytes 786440 | tf_op jit(solution)/shard_map/ppermute | solution.py:211
  6.6 23.4 %copy-start = (bf16[1,4,512,512]{3,2,1,0:T(8,128)(2,1)S(1)}, bf16[1,4,512,512]{3,2,1,0:T(8,128)(2,1)}, u32[]{:S(2)}) copy-start(bf16[1,4,512,512]{3,2,1,0:T(8,128)(2,1)} %tiles_ref.3) | copy-start | bytes 6291460
  6.7 23.4 %copy-start.2 = (s32[1,4]{1,0:T(1,128)S(1)}, s32[1,4]{1,0:T(1,128)}, u32[]{:S(2)}) copy-start(s32[1,4]{1,0:T(1,128)} %cols_ref.3) | copy-start | bytes 52
  7.5 4.1 %collective-permute-start.4 = (bf16[80,256]{1,0:T(8,128)(2,1)S(1)}, bf16[80,256]{1,0:T(8,128)(2,1)S(1)}, u32[]{:S(2)}, u32[]{:S(2)}) collective-permute-start(bf16[80,256]{1,0:T(8,128)(2,1)S(1)} %add_convert_fusion.1.own_ref), channel_id=1, source_target_pairs={{0,4},{4,0},{8,12},{12,8},{16,20},{20,16},{24,28},{28,24},{1,5},{5... | collective-permute-start | bytes 122888 | tf_op jit(solution)/shard_map/ppermute | solution.py:222
  9.0 9.5 %collective-permute-start.5 = (bf16[256,512]{1,0:T(8,128)(2,1)S(1)}, bf16[256,512]{1,0:T(8,128)(2,1)S(1)}, u32[]{:S(2)}, u32[]{:S(2)}) collective-permute-start(bf16[256,512]{1,0:T(8,128)(2,1)S(1)} %copy-done.3), channel_id=1, source_target_pairs={{3,4},{7,8},{11,12},{15,16},{19,20},{23,24},{27,28},{4,3},{8,7},{1... | collective-permute-start | bytes 786440 | tf_op jit(solution)/shard_map/ppermute | solution.py:304
  12.9 5.6 %collective-permute-start.6 = (bf16[256,512]{1,0:T(8,128)(2,1)S(1)}, bf16[256,512]{1,0:T(8,128)(2,1)S(1)}, u32[]{:S(2)}, u32[]{:S(2)}) collective-permute-start(bf16[256,512]{1,0:T(8,128)(2,1)S(1)} %collective-permute-done.3.refs_4_.across_ref.refs_2_), channel_id=1, source_target_pairs={{0,1},{1,0},{2,3},{3,2},{4,5},{5,4},{6,7},{7,6},{8,9},{9,8},{10,11... | collective-permute-start | bytes 786440 | tf_op jit(solution)/shard_map/ppermute | solution.py:211
  12.9 8.4 %collective-permute-start.9 = (bf16[80,256]{1,0:T(8,128)(2,1)S(1)}, bf16[80,256]{1,0:T(8,128)(2,1)S(1)}, u32[]{:S(2)}, u32[]{:S(2)}) collective-permute-start(bf16[80,256]{1,0:T(8,128)(2,1)S(1)} %get-tuple-element.58), channel_id=1, source_target_pairs={{0,24},{4,28},{8,16},{12,20},{16,8},{20,12},{24,0},{28,4},{1,25},{... | collective-permute-start | bytes 122888 | tf_op jit(solution)/shard_map/ppermute | solution.py:321
  14.5 6.9 %collective-permute-start.8 = (bf16[80,256]{1,0:T(8,128)(2,1)S(1)}, bf16[80,256]{1,0:T(8,128)(2,1)S(1)}, u32[]{:S(2)}, u32[]{:S(2)}) collective-permute-start(bf16[80,256]{1,0:T(8,128)(2,1)S(1)} %get-tuple-element.57), channel_id=1, source_target_pairs={{0,8},{4,12},{8,0},{12,4},{16,24},{20,28},{24,16},{28,20},{1,9},{5... | collective-permute-start | bytes 122888 | tf_op jit(solution)/shard_map/ppermute | solution.py:321
  18.5 4.9 %collective-permute-start.7 = (bf16[80,256]{1,0:T(8,128)(2,1)S(1)}, bf16[80,256]{1,0:T(8,128)(2,1)S(1)}, u32[]{:S(2)}, u32[]{:S(2)}) collective-permute-start(bf16[80,256]{1,0:T(8,128)(2,1)S(1)} %get-tuple-element.56), channel_id=1, source_target_pairs={{0,16},{4,20},{8,24},{12,28},{16,0},{20,4},{24,8},{28,12},{1,17},{... | collective-permute-start | bytes 122888 | tf_op jit(solution)/shard_map/ppermute | solution.py:321
  21.3 12.1 %collective-permute-start.13 = (bf16[256,512]{1,0:T(8,128)(2,1)S(1)}, bf16[256,512]{1,0:T(8,128)(2,1)S(1)}, u32[]{:S(2)}, u32[]{:S(2)}) collective-permute-start(bf16[256,512]{1,0:T(8,128)(2,1)S(1)} %pick_even.1), channel_id=1, source_target_pairs={{0,4},{8,12},{16,20},{24,28},{4,0},{12,8},{20,16},{28,24},{1,5},{9... | collective-permute-start | bytes 786440 | tf_op jit(solution)/shard_map/ppermute | solution.py:228
  23.4 9.9 %collective-permute-start.14 = (bf16[256,512]{1,0:T(8,128)(2,1)S(1)}, bf16[256,512]{1,0:T(8,128)(2,1)S(1)}, u32[]{:S(2)}, u32[]{:S(2)}) collective-permute-start(bf16[256,512]{1,0:T(8,128)(2,1)S(1)} %pick_odd.1), channel_id=1, source_target_pairs={{4,8},{12,16},{20,24},{8,4},{16,12},{24,20},{5,9},{13,17},{21,25},... | collective-permute-start | bytes 786440 | tf_op jit(solution)/shard_map/ppermute | solution.py:228
  25.5 2.6 %collective-permute-start.10 = (bf16[64,256]{1,0:T(8,128)(2,1)S(1)}, bf16[64,256]{1,0:T(8,128)(2,1)S(1)}, u32[]{:S(2)}, u32[]{:S(2)}) collective-permute-start(bf16[64,256]{1,0:T(8,128)(2,1)S(1)} %add_convert_fusion.2.field0), channel_id=1, source_target_pairs={{0,1},{1,0},{2,3},{3,2},{4,5},{5,4},{6,7},{7,6},{8,9},{9,8},{10,11... | collective-permute-start | bytes 98312 | tf_op jit(solution)/shard_map/ppermute | solution.py:211
  25.6 4.2 %collective-permute-start.11 = (bf16[64,256]{1,0:T(8,128)(2,1)S(1)}, bf16[64,256]{1,0:T(8,128)(2,1)S(1)}, u32[]{:S(2)}, u32[]{:S(2)}) collective-permute-start(bf16[64,256]{1,0:T(8,128)(2,1)S(1)} %add_convert_fusion.2.field0), channel_id=1, source_target_pairs={{0,2},{1,3},{2,0},{3,1},{4,6},{5,7},{6,4},{7,5},{8,10},{9,11},{10,... | collective-permute-start | bytes 98312 | tf_op jit(solution)/shard_map/ppermute | solution.py:211
  26.4 3.7 %collective-permute-start.12 = (bf16[64,256]{1,0:T(8,128)(2,1)S(1)}, bf16[64,256]{1,0:T(8,128)(2,1)S(1)}, u32[]{:S(2)}, u32[]{:S(2)}) collective-permute-start(bf16[64,256]{1,0:T(8,128)(2,1)S(1)} %add_convert_fusion.2.field0), channel_id=1, source_target_pairs={{0,3},{1,2},{2,1},{3,0},{4,7},{5,6},{6,5},{7,4},{8,11},{9,10},{10,... | collective-permute-start | bytes 98312 | tf_op jit(solution)/shard_map/ppermute | solution.py:211

commit v4 on v3

--- a/solution.py
+++ b/solution.py
@@ -165,19 +165,14 @@
 
 
 def near_kernel(
-    x_ref, mate_ref, across_ref, corner_ref, edge_ref, tiles_ref, w_ref, field0, field1, field2,
-    field3, cols_ref, count_ref, acc_ref, field_ref
+    x_ref, mate_ref, across_ref, corner_ref, edge_ref, tiles_ref, cols_ref, count_ref, acc_ref
 ):
     pos = lax.axis_index("level")
-    for turn, part_ref in enumerate((field0, field1, field2, field3)):
-        field_ref[part_of(pos ^ turn)] = part_ref[...]
-    field = jnp.concatenate([field_ref[part] for part in range(GROUP)], axis=0)
     odd = pos & 1
     inner = jnp.logical_or(pos == 1, pos == 2)
     acc = dot(x_ref[...], tiles_ref[0, 0]) + dot(mate_ref[...], tiles_ref[0, 2 - odd])
     beside = jnp.where(inner, corner_ref[...], edge_ref[...])
-    acc = acc + dot(beside, tiles_ref[0, 1 + odd])
-    acc_ref[...] = acc + dot_t(field, w_ref[...])
+    acc_ref[...] = acc + dot(beside, tiles_ref[0, 1 + odd])
     col = cols_ref[0, SLOT]
     turn = lax.rem(col, GROUP) ^ pos
     here = jnp.logical_and(count_ref[0] > SLOT, col // GROUP == 1)
@@ -187,20 +182,32 @@
             acc_ref[...] += dot(block[...], tiles_ref[0, SLOT])
 
 
-def finish_kernel(acc_ref, even_ref, odd_ref, tiles_ref, cols_ref, count_ref, out_ref):
+def finish_kernel(
+    acc_ref, even_ref, odd_ref, tiles_ref, w_ref, field0, field1, field2, field3,
+    cols_ref, count_ref, out_ref, total_ref, field_ref
+):
+    pos = lax.axis_index("level")
     side = lax.axis_index("leaf") & 1
+    for turn, part_ref in enumerate((field0, field1, field2, field3)):
+        field_ref[part_of(pos ^ turn)] = part_ref[...]
+    field = jnp.concatenate([field_ref[part] for part in range(GROUP)], axis=0)
     group = cols_ref[0, SLOT] // GROUP
     live = jnp.logical_and(count_ref[0] > SLOT, group != 1)
     from_even = (group == 0) == (side == 1)
+    total = acc_ref[...] + dot_t(field, w_ref[...])
 
     @pl.when(jnp.logical_not(live))
     def _():
-        out_ref[...] = acc_ref[...].astype(BF16)
+        out_ref[...] = total.astype(BF16)
+
+    @pl.when(live)
+    def _():
+        total_ref[...] = total
 
     for here, block in ((from_even, even_ref), (jnp.logical_not(from_even), odd_ref)):
         @pl.when(jnp.logical_and(live, here))
         def _(block=block):
-            out_ref[...] = (acc_ref[...] + dot(block[...], tiles_ref[0, SLOT])).astype(BF16)
+            out_ref[...] = (total_ref[...] + dot(block[...], tiles_ref[0, SLOT])).astype(BF16)
 
 
 def part_of(pos):
@@ -336,16 +343,17 @@
     (to_odd,) = call(
         partial(pick_odd_kernel, rows, pairs, len(named)), "pick_odd", named + held, [], [block]
     )
-    field, to_odd = lax.optimization_barrier((field, to_odd))
+    (acc,) = call(
+        near_kernel, "near", held + [edge, near_tiles], [near_cols, near_count],
+        [((vectors, points), F32)],
+    )
+    field, to_odd, acc = lax.optimization_barrier((field, to_odd, acc))
     fields = [field] + [turned(field, turn) for turn in range(1, GROUP)]
     from_odd = neighbours(to_odd, 1)
-    (acc,) = call(
-        near_kernel, "near", held + [edge, near_tiles, w] + fields, [near_cols, near_count],
-        [((vectors, points), F32)], [pltpu.VMEM((GROUP, rows, rank), BF16)],
-    )
     (out,) = call(
-        finish_kernel, "finish", [acc, from_even, from_odd, near_tiles], [near_cols, near_count],
-        [block],
+        finish_kernel, "finish", [acc, from_even, from_odd, near_tiles, w] + fields,
+        [near_cols, near_count], [block],
+        [pltpu.VMEM((vectors, points), F32), pltpu.VMEM((GROUP, rows, rank), BF16)],
     )
     return out
 

time: 34.8 us -> 36.1 us (1.037)
  starting transfers between devices: 16.8 us -> 17.6 us
  waiting for transfers between devices: 10.7 us -> 11.1 us
    ppermute x3, waiting for transfers between devices: 1.88 us -> 0.01 us  [per_device(): lax.ppermute(push, 'leaf', [(i, i ^ 2 * turn) for i in range(leaf_count)])]
    ppermute x2, starting transfers between devices: 2.1 us -> 3.42 us  [neighbours(): return lax.ppermute(value, 'leaf', route + [(b, a) for a, b in route])]
    ppermute x1, waiting for transfers between devices: 1.53 us -> 2.53 us  [per_device(): lax.ppermute(sent, ('leaf', 'level'), joints + [(b, a) for a, b in joints])]
    ppermute x2, waiting for transfers between devices: 2.07 us -> 2.99 us  [neighbours(): return lax.ppermute(value, 'leaf', route + [(b, a) for a, b in route])]
    ppermute x3, starting transfers between devices: 6.64 us -> 6.09 us  [per_device(): lax.ppermute(push, 'leaf', [(i, i ^ 2 * turn) for i in range(leaf_count)])]
  transfers between devices with their start and end apart: 15 -> 15, of which waited for: 9 -> 7; matrix products, arithmetic and copies ran while one was open for 0% -> 0% of each run, Pallas kernels for 9% -> 8%
where the time goes in v4:
time: 36.1 us; the launch traced here: 36 us
  starting transfers between devices  17.6 us (49%)
  waiting for transfers between devices  11.1 us (31%)
  Pallas kernels  6.4 us (18%)
  between operations  0.83 us (2%)
    pallas_call x7, Pallas kernels, call(): pl.pallas_call(kernel, out_shape=shapes, in_specs=[pl.BlockSpec(memory_sp...  6.4 us
    ppermute x3, starting transfers between devices, per_device(): lax.ppermute(push, 'leaf', [(i, i ^ 2 * turn) for i in range(leaf_count)])  6.09 us
    ppermute x8, waiting for transfers between devices, turned(): return lax.ppermute(value, 'level', [(i, i ^ turn) for i in range(GROUP)])  5 us
    ppermute x8, starting transfers between devices, turned(): return lax.ppermute(value, 'level', [(i, i ^ turn) for i in range(GROUP)])  4.59 us
    ppermute x2, starting transfers between devices, neighbours(): return lax.ppermute(value, 'leaf', route + [(b, a) for a, b in route])  3.42 us
    ppermute x2, waiting for transfers between devices, neighbours(): return lax.ppermute(value, 'leaf', route + [(b, a) for a, b in route])  2.99 us
    ppermute x1, waiting for transfers between devices, per_device(): lax.ppermute(sent, ('leaf', 'level'), joints + [(b, a) for a, b in joints])  2.53 us
    ppermute x1, starting transfers between devices, per_device(): lax.ppermute(sent, ('leaf', 'level'), joints + [(b, a) for a, b in joints])  1.91 us
  transfers between devices with their start and end apart: 15, of which 7 were waited for; matrix products, arithmetic and copies ran while one was open for 0% of the time, Pallas kernels for 8%

profile of v4, /device:TPU:8, one launch (start us, length us, event | category | flops | bytes accessed | tf_op | source)
XLA Modules:
  0.0 36.0 jit_solution(17825778649902331691)
XLA Ops:
  0.0 1.8 %up.1 = (bf16[160,256]{1,0:T(8,128)(2,1)S(1)}, bf16[160,256]{1,0:T(8,128)(2,1)S(1)}, bf16[512,256]{1,0:T(8,128)(2,1)S(1)}, bf16[256,512]{1,0:T(8,128)(2,1)S(1)},...) custom-call(bf16[256,512]{1,0:T(8,128)(2,1)} %x_hbm.1, bf16[1,512,256]{2,1,0:T(8,128)(2,1)} %basis_hbm.1, ...), custom_call_target="tpu_custom_call" | custom-call | tf_op jit(solution)/shard_map/up/pallas_call | solution.py:28
  1.9 0.0 copy-start
  1.9 0.0 copy-start.2
  1.9 0.1 collective-permute-start
  2.0 0.5 %collective-permute-start.1 = (bf16[256,512]{1,0:T(8,128)(2,1)S(1)}, bf16[256,512]{1,0:T(8,128)(2,1)S(1)}, u32[]{:S(2)}, u32[]{:S(2)}) collective-permute-start(bf16[256,512]{1,0:T(8,128)(2,1)S(1)} %copy-done.3), channel_id=1, source_target_pairs={{0,1},{1,0},{2,3},{3,2},{4,5},{5,4},{6,7},{7,6},{8,9},{9,8},{10,11... | collective-permute-start | bytes 786440 | tf_op jit(solution)/shard_map/ppermute | solution.py:218
  2.5 0.8 %collective-permute-done = bf16[160,256]{1,0:T(8,128)(2,1)S(1)} collective-permute-done((bf16[160,256]{1,0:T(8,128)(2,1)S(1)}, bf16[160,256]{1,0:T(8,128)(2,1)S(1)}, u32[]{:S(2)}, u32[]{:S(2)}) %collective-permute-start) | collective-permute-done | bytes 81952 | tf_op jit(solution)/shard_map/ppermute | solution.py:218
  3.3 1.6 %collective-permute-start.2 = (bf16[80,256]{1,0:T(8,128)(2,1)S(1)}, bf16[80,256]{1,0:T(8,128)(2,1)S(1)}, u32[]{:S(2)}, u32[]{:S(2)}) collective-permute-start(bf16[80,256]{1,0:T(8,128)(2,1)S(1)} %slice.21), channel_id=1, source_target_pairs={{0,2},{1,3},{2,0},{3,1},{4,6},{5,7},{6,4},{7,5},{8,10},{9,11},{10,... | collective-permute-start | bytes 122888 | tf_op jit(solution)/shard_map/ppermute | solution.py:218
  4.8 0.5 %collective-permute-start.4 = (bf16[256,512]{1,0:T(8,128)(2,1)S(1)}, bf16[256,512]{1,0:T(8,128)(2,1)S(1)}, u32[]{:S(2)}, u32[]{:S(2)}) collective-permute-start(bf16[256,512]{1,0:T(8,128)(2,1)S(1)} %copy-done.3), channel_id=1, source_target_pairs={{0,2},{1,3},{2,0},{3,1},{4,6},{5,7},{6,4},{7,5},{8,10},{9,11},{10,... | collective-permute-start | bytes 786440 | tf_op jit(solution)/shard_map/ppermute | solution.py:218
  5.4 1.3 %fold.1 = (bf16[2,256,256]{2,1,0:T(8,128)(2,1)S(1)}, bf16[2,256,256]{2,1,0:T(8,128)(2,1)S(1)}, bf16[2,256,256]{2,1,0:T(8,128)(2,1)S(1)}) custom-call(bf16[2,2,256,256]{3,2,1,0:T(8,128)(2,1)S(1)} %get-tuple-element.36.coupling_ref, bf16[2,256,256]{2,1,0:T(8,128)(2,1)S(1)} %get-tuple-element.37.transfer_ref, s32[6,2,8]{2,1,0:T(2,128)S(1)} %bitcast.1), custom_call_target="tpu_custom_call" | custom-call | tf_op jit(solution)/shard_map/fold/pallas_call | solution.py:28
  6.7 0.8 %collective-permute-done.2 = bf16[80,256]{1,0:T(8,128)(2,1)S(1)} collective-permute-done((bf16[80,256]{1,0:T(8,128)(2,1)S(1)}, bf16[80,256]{1,0:T(8,128)(2,1)S(1)}, u32[]{:S(2)}, u32[]{:S(2)}) %collective-permute-start.2) | collective-permute-done | bytes 40992 | tf_op jit(solution)/shard_map/ppermute | solution.py:218
  7.5 0.0 collective-permute-done.1.refs_3_.mate_ref.refs_1_
  7.5 1.6 %collective-permute-start.5 = (bf16[80,256]{1,0:T(8,128)(2,1)S(1)}, bf16[80,256]{1,0:T(8,128)(2,1)S(1)}, u32[]{:S(2)}, u32[]{:S(2)}) collective-permute-start(bf16[80,256]{1,0:T(8,128)(2,1)S(1)} %add_convert_fusion.1.own_ref), channel_id=1, source_target_pairs={{0,4},{4,0},{8,12},{12,8},{16,20},{20,16},{24,28},{28,24},{1,5},{5... | collective-permute-start | bytes 122888 | tf_op jit(solution)/shard_map/ppermute | solution.py:229
  9.1 1.9 %collective-permute-start.3 = (bf16[256,512]{1,0:T(8,128)(2,1)S(1)}, bf16[256,512]{1,0:T(8,128)(2,1)S(1)}, u32[]{:S(2)}, u32[]{:S(2)}) collective-permute-start(bf16[256,512]{1,0:T(8,128)(2,1)S(1)} %copy-done.3), channel_id=1, source_target_pairs={{3,4},{7,8},{11,12},{15,16},{19,20},{23,24},{27,28},{4,3},{8,7},{1... | collective-permute-start | bytes 786440 | tf_op jit(solution)/shard_map/ppermute | solution.py:311
  11.0 0.6 %collective-permute-done.5.mate_ref.named_ref = bf16[80,256]{1,0:T(8,128)(2,1)S(1)} collective-permute-done((bf16[80,256]{1,0:T(8,128)(2,1)S(1)}, bf16[80,256]{1,0:T(8,128)(2,1)S(1)}, u32[]{:S(2)}, u32[]{:S(2)}) %collective-permute-start.5) | collective-permute-done | bytes 40992 | tf_op jit(solution)/shard_map/ppermute | solution.py:229
  11.5 0.3 push.1
  11.8 1.1 %collective-permute-done.4.refs_4_.across_ref.refs_2_ = bf16[256,512]{1,0:T(8,128)(2,1)S(1)} collective-permute-done((bf16[256,512]{1,0:T(8,128)(2,1)S(1)}, bf16[256,512]{1,0:T(8,128)(2,1)S(1)}, u32[]{:S(2)}, u32[]{:S(2)}) %collective-permute-start.4) | collective-permute-done | bytes 262176 | tf_op jit(solution)/shard_map/ppermute | solution.py:218
  12.9 0.0 collective-permute-start.6
  12.9 0.4 %collective-permute-start.8 = (bf16[80,256]{1,0:T(8,128)(2,1)S(1)}, bf16[80,256]{1,0:T(8,128)(2,1)S(1)}, u32[]{:S(2)}, u32[]{:S(2)}) collective-permute-start(bf16[80,256]{1,0:T(8,128)(2,1)S(1)} %get-tuple-element.53), channel_id=1, source_target_pairs={{0,8},{4,12},{8,0},{12,4},{16,24},{20,28},{24,16},{28,20},{1,9},{5... | collective-permute-start | bytes 122888 | tf_op jit(solution)/shard_map/ppermute | solution.py:328
  13.4 2.7 %collective-permute-start.9 = (bf16[80,256]{1,0:T(8,128)(2,1)S(1)}, bf16[80,256]{1,0:T(8,128)(2,1)S(1)}, u32[]{:S(2)}, u32[]{:S(2)}) collective-permute-start(bf16[80,256]{1,0:T(8,128)(2,1)S(1)} %get-tuple-element.54), channel_id=1, source_target_pairs={{0,24},{4,28},{8,16},{12,20},{16,8},{20,12},{24,0},{28,4},{1,25},{... | collective-permute-start | bytes 122888 | tf_op jit(solution)/shard_map/ppermute | solution.py:328
  16.1 2.5 %collective-permute-done.3.edge_ref = bf16[256,512]{1,0:T(8,128)(2,1)S(1)} collective-permute-done((bf16[256,512]{1,0:T(8,128)(2,1)S(1)}, bf16[256,512]{1,0:T(8,128)(2,1)S(1)}, u32[]{:S(2)}, u32[]{:S(2)}) %collective-permute-start.3) | collective-permute-done | bytes 262176 | tf_op jit(solution)/shard_map/ppermute | solution.py:311
  18.6 2.9 %collective-permute-start.7 = (bf16[80,256]{1,0:T(8,128)(2,1)S(1)}, bf16[80,256]{1,0:T(8,128)(2,1)S(1)}, u32[]{:S(2)}, u32[]{:S(2)}) collective-permute-start(bf16[80,256]{1,0:T(8,128)(2,1)S(1)} %get-tuple-element.52), channel_id=1, source_target_pairs={{0,16},{4,20},{8,24},{12,28},{16,0},{20,4},{24,8},{28,12},{1,17},{... | collective-permute-start | bytes 122888 | tf_op jit(solution)/shard_map/ppermute | solution.py:328
  22.2 0.2 pick_even.1
  22.4 0.1 collective-permute-start.10
  22.5 1.1 %near.1.acc_ref = f32[256,512]{1,0:T(8,128)S(1)} custom-call(bf16[256,512]{1,0:T(8,128)(2,1)S(1)} %get-tuple-element.55.refs_2_.x_ref.refs_0_, bf16[256,512]{1,0:T(8,128)(2,1)S(1)} %collective-permute-done.1.refs_3_.mate_ref.refs_1_, bf16[256,512]{1,0:T(8,128)(2,1)S(1)} %collective-permute-done.4.refs_4_.across_ref.refs_2_, ...), custom_call_target="tpu_custom_call" | custom-call | tf_op jit(solution)/shard_map/near/pallas_call | solution.py:28
  23.7 0.2 pick_odd.1
  23.9 3.3 %collective-permute-start.11 = (bf16[256,512]{1,0:T(8,128)(2,1)S(1)}, bf16[256,512]{1,0:T(8,128)(2,1)S(1)}, u32[]{:S(2)}, u32[]{:S(2)}) collective-permute-start(bf16[256,512]{1,0:T(8,128)(2,1)S(1)} %pick_odd.1), channel_id=1, source_target_pairs={{4,8},{12,16},{20,24},{8,4},{16,12},{24,20},{5,9},{13,17},{21,25},... | collective-permute-start | bytes 786440 | tf_op jit(solution)/shard_map/ppermute | solution.py:235
  27.2 0.1 collective-permute-start.12
  27.3 0.1 collective-permute-start.13
  27.4 1.7 %collective-permute-start.14 = (bf16[64,256]{1,0:T(8,128)(2,1)S(1)}, bf16[64,256]{1,0:T(8,128)(2,1)S(1)}, u32[]{:S(2)}, u32[]{:S(2)}) collective-permute-start(bf16[64,256]{1,0:T(8,128)(2,1)S(1)} %add_convert_fusion.2.field0), channel_id=1, source_target_pairs={{0,3},{1,2},{2,1},{3,0},{4,7},{5,6},{6,5},{7,4},{8,11},{9,10},{10,... | collective-permute-start | bytes 98312 | tf_op jit(solution)/shard_map/ppermute | solution.py:218
  29.2 2.3 %collective-permute-done.13.field2 = bf16[64,256]{1,0:T(8,128)(2,1)S(1)} collective-permute-done((bf16[64,256]{1,0:T(8,128)(2,1)S(1)}, bf16[64,256]{1,0:T(8,128)(2,1)S(1)}, u32[]{:S(2)}, u32[]{:S(2)}) %collective-permute-start.13) | collective-permute-done | bytes 32800 | tf_op jit(solution)/shard_map/ppermute | solution.py:218
  31.5 3.0 %collective-permute-done.10.even_ref = bf16[256,512]{1,0:T(8,128)(2,1)S(1)} collective-permute-done((bf16[256,512]{1,0:T(8,128)(2,1)S(1)}, bf16[256,512]{1,0:T(8,128)(2,1)S(1)}, u32[]{:S(2)}, u32[]{:S(2)}) %collective-permute-start.10) | collective-permute-done | bytes 262176 | tf_op jit(solution)/shard_map/ppermute | solution.py:235
  34.5 1.5 %finish.1 = bf16[256,512]{1,0:T(8,128)(2,1)} custom-call(f32[256,512]{1,0:T(8,128)S(1)} %near.1.acc_ref, bf16[256,512]{1,0:T(8,128)(2,1)S(1)} %collective-permute-done.10.even_ref, bf16[256,512]{1,0:T(8,128)(2,1)S(1)} %collective-permute-done.11.odd_ref, bf16[1,4,512,512]{3,2,1,0:T(8,128)(2,1)S(1)} %copy-done, bf16[512,256]{1,0:T(8,128)(2,1)S(1)} %get-tuple-element.61.w_ref, ...), custom_call_target="tpu_custom_call" | custom-call | tf_op jit(solution)/shard_map/finish/pallas_call | solution.py:28
  (17 shorter events, 0.1 us)
Async XLA Ops:
  0.0 2.0 %copy-start.3 = (bf16[256,512]{1,0:T(8,128)(2,1)S(1)}, bf16[256,512]{1,0:T(8,128)(2,1)}, u32[]{:S(2)}) copy-start(bf16[256,512]{1,0:T(8,128)(2,1)} %x_hbm.1) | copy-start | bytes 786436
  0.0 5.4 %copy-start.1 = (s32[6,8,2]{1,2,0:T(2,128)S(1)}, s32[6,8,2]{1,2,0:T(2,128)}, u32[]{:S(2)}) copy-start(s32[6,8,2]{1,2,0:T(2,128)} %param.15) | copy-start | bytes 1156
  1.9 20.6 %copy-start = (bf16[1,4,512,512]{3,2,1,0:T(8,128)(2,1)S(1)}, bf16[1,4,512,512]{3,2,1,0:T(8,128)(2,1)}, u32[]{:S(2)}) copy-start(bf16[1,4,512,512]{3,2,1,0:T(8,128)(2,1)} %tiles_ref.3) | copy-start | bytes 6291460
  1.9 20.6 %copy-start.2 = (s32[1,4]{1,0:T(1,128)S(1)}, s32[1,4]{1,0:T(1,128)}, u32[]{:S(2)}) copy-start(s32[1,4]{1,0:T(1,128)} %cols_ref.3) | copy-start | bytes 52
  1.9 1.3 %collective-permute-start = (bf16[160,256]{1,0:T(8,128)(2,1)S(1)}, bf16[160,256]{1,0:T(8,128)(2,1)S(1)}, u32[]{:S(2)}, u32[]{:S(2)}) collective-permute-start(bf16[160,256]{1,0:T(8,128)(2,1)S(1)} %get-tuple-element.35), channel_id=1, source_target_pairs={{0,1},{1,0},{2,3},{3,2},{4,5},{5,4},{6,7},{7,6},{8,9},{9,8},{10,11... | collective-permute-start | bytes 245768 | tf_op jit(solution)/shard_map/ppermute | solution.py:218
  2.0 5.5 %collective-permute-start.1 = (bf16[256,512]{1,0:T(8,128)(2,1)S(1)}, bf16[256,512]{1,0:T(8,128)(2,1)S(1)}, u32[]{:S(2)}, u32[]{:S(2)}) collective-permute-start(bf16[256,512]{1,0:T(8,128)(2,1)S(1)} %copy-done.3), channel_id=1, source_target_pairs={{0,1},{1,0},{2,3},{3,2},{4,5},{5,4},{6,7},{7,6},{8,9},{9,8},{10,11... | collective-permute-start | bytes 786440 | tf_op jit(solution)/shard_map/ppermute | solution.py:218
  3.3 4.2 %collective-permute-start.2 = (bf16[80,256]{1,0:T(8,128)(2,1)S(1)}, bf16[80,256]{1,0:T(8,128)(2,1)S(1)}, u32[]{:S(2)}, u32[]{:S(2)}) collective-permute-start(bf16[80,256]{1,0:T(8,128)(2,1)S(1)} %slice.21), channel_id=1, source_target_pairs={{0,2},{1,3},{2,0},{3,1},{4,6},{5,7},{6,4},{7,5},{8,10},{9,11},{10,... | collective-permute-start | bytes 122888 | tf_op jit(solution)/shard_map/ppermute | solution.py:218
  4.8 8.1 %collective-permute-start.4 = (bf16[256,512]{1,0:T(8,128)(2,1)S(1)}, bf16[256,512]{1,0:T(8,128)(2,1)S(1)}, u32[]{:S(2)}, u32[]{:S(2)}) collective-permute-start(bf16[256,512]{1,0:T(8,128)(2,1)S(1)} %copy-done.3), channel_id=1, source_target_pairs={{0,2},{1,3},{2,0},{3,1},{4,6},{5,7},{6,4},{7,5},{8,10},{9,11},{10,... | collective-permute-start | bytes 786440 | tf_op jit(solution)/shard_map/ppermute | solution.py:218
  7.5 4.1 %collective-permute-start.5 = (bf16[80,256]{1,0:T(8,128)(2,1)S(1)}, bf16[80,256]{1,0:T(8,128)(2,1)S(1)}, u32[]{:S(2)}, u32[]{:S(2)}) collective-permute-start(bf16[80,256]{1,0:T(8,128)(2,1)S(1)} %add_convert_fusion.1.own_ref), channel_id=1, source_target_pairs={{0,4},{4,0},{8,12},{12,8},{16,20},{20,16},{24,28},{28,24},{1,5},{5... | collective-permute-start | bytes 122888 | tf_op jit(solution)/shard_map/ppermute | solution.py:229
  9.1 9.6 %collective-permute-start.3 = (bf16[256,512]{1,0:T(8,128)(2,1)S(1)}, bf16[256,512]{1,0:T(8,128)(2,1)S(1)}, u32[]{:S(2)}, u32[]{:S(2)}) collective-permute-start(bf16[256,512]{1,0:T(8,128)(2,1)S(1)} %copy-done.3), channel_id=1, source_target_pairs={{3,4},{7,8},{11,12},{15,16},{19,20},{23,24},{27,28},{4,3},{8,7},{1... | collective-permute-start | bytes 786440 | tf_op jit(solution)/shard_map/ppermute | solution.py:311
  12.9 5.7 %collective-permute-start.6 = (bf16[256,512]{1,0:T(8,128)(2,1)S(1)}, bf16[256,512]{1,0:T(8,128)(2,1)S(1)}, u32[]{:S(2)}, u32[]{:S(2)}) collective-permute-start(bf16[256,512]{1,0:T(8,128)(2,1)S(1)} %collective-permute-done.4.refs_4_.across_ref.refs_2_), channel_id=1, source_target_pairs={{0,1},{1,0},{2,3},{3,2},{4,5},{5,4},{6,7},{7,6},{8,9},{9,8},{10,11... | collective-permute-start | bytes 786440 | tf_op jit(solution)/shard_map/ppermute | solution.py:218
  12.9 10.7 %collective-permute-start.8 = (bf16[80,256]{1,0:T(8,128)(2,1)S(1)}, bf16[80,256]{1,0:T(8,128)(2,1)S(1)}, u32[]{:S(2)}, u32[]{:S(2)}) collective-permute-start(bf16[80,256]{1,0:T(8,128)(2,1)S(1)} %get-tuple-element.53), channel_id=1, source_target_pairs={{0,8},{4,12},{8,0},{12,4},{16,24},{20,28},{24,16},{28,20},{1,9},{5... | collective-permute-start | bytes 122888 | tf_op jit(solution)/shard_map/ppermute | solution.py:328
  13.4 10.3 %collective-permute-start.9 = (bf16[80,256]{1,0:T(8,128)(2,1)S(1)}, bf16[80,256]{1,0:T(8,128)(2,1)S(1)}, u32[]{:S(2)}, u32[]{:S(2)}) collective-permute-start(bf16[80,256]{1,0:T(8,128)(2,1)S(1)} %get-tuple-element.54), channel_id=1, source_target_pairs={{0,24},{4,28},{8,16},{12,20},{16,8},{20,12},{24,0},{28,4},{1,25},{... | collective-permute-start | bytes 122888 | tf_op jit(solution)/shard_map/ppermute | solution.py:328
  18.6 5.2 %collective-permute-start.7 = (bf16[80,256]{1,0:T(8,128)(2,1)S(1)}, bf16[80,256]{1,0:T(8,128)(2,1)S(1)}, u32[]{:S(2)}, u32[]{:S(2)}) collective-permute-start(bf16[80,256]{1,0:T(8,128)(2,1)S(1)} %get-tuple-element.52), channel_id=1, source_target_pairs={{0,16},{4,20},{8,24},{12,28},{16,0},{20,4},{24,8},{28,12},{1,17},{... | collective-permute-start | bytes 122888 | tf_op jit(solution)/shard_map/ppermute | solution.py:328
  22.4 12.1 %collective-permute-start.10 = (bf16[256,512]{1,0:T(8,128)(2,1)S(1)}, bf16[256,512]{1,0:T(8,128)(2,1)S(1)}, u32[]{:S(2)}, u32[]{:S(2)}) collective-permute-start(bf16[256,512]{1,0:T(8,128)(2,1)S(1)} %pick_even.1), channel_id=1, source_target_pairs={{0,4},{8,12},{16,20},{24,28},{4,0},{12,8},{20,16},{28,24},{1,5},{9... | collective-permute-start | bytes 786440 | tf_op jit(solution)/shard_map/ppermute | solution.py:235
  23.9 10.6 %collective-permute-start.11 = (bf16[256,512]{1,0:T(8,128)(2,1)S(1)}, bf16[256,512]{1,0:T(8,128)(2,1)S(1)}, u32[]{:S(2)}, u32[]{:S(2)}) collective-permute-start(bf16[256,512]{1,0:T(8,128)(2,1)S(1)} %pick_odd.1), channel_id=1, source_target_pairs={{4,8},{12,16},{20,24},{8,4},{16,12},{24,20},{5,9},{13,17},{21,25},... | collective-permute-start | bytes 786440 | tf_op jit(solution)/shard_map/ppermute | solution.py:235
  27.2 1.9 %collective-permute-start.12 = (bf16[64,256]{1,0:T(8,128)(2,1)S(1)}, bf16[64,256]{1,0:T(8,128)(2,1)S(1)}, u32[]{:S(2)}, u32[]{:S(2)}) collective-permute-start(bf16[64,256]{1,0:T(8,128)(2,1)S(1)} %add_convert_fusion.2.field0), channel_id=1, source_target_pairs={{0,1},{1,0},{2,3},{3,2},{4,5},{5,4},{6,7},{7,6},{8,9},{9,8},{10,11... | collective-permute-start | bytes 98312 | tf_op jit(solution)/shard_map/ppermute | solution.py:218
  27.3 4.2 %collective-permute-start.13 = (bf16[64,256]{1,0:T(8,128)(2,1)S(1)}, bf16[64,256]{1,0:T(8,128)(2,1)S(1)}, u32[]{:S(2)}, u32[]{:S(2)}) collective-permute-start(bf16[64,256]{1,0:T(8,128)(2,1)S(1)} %add_convert_fusion.2.field0), channel_id=1, source_target_pairs={{0,2},{1,3},{2,0},{3,1},{4,6},{5,7},{6,4},{7,5},{8,10},{9,11},{10,... | collective-permute-start | bytes 98312 | tf_op jit(solution)/shard_map/ppermute | solution.py:218
  27.4 4.0 %collective-permute-start.14 = (bf16[64,256]{1,0:T(8,128)(2,1)S(1)}, bf16[64,256]{1,0:T(8,128)(2,1)S(1)}, u32[]{:S(2)}, u32[]{:S(2)}) collective-permute-start(bf16[64,256]{1,0:T(8,128)(2,1)S(1)} %add_convert_fusion.2.field0), channel_id=1, source_target_pairs={{0,3},{1,2},{2,1},{3,0},{4,7},{5,6},{6,5},{7,4},{8,11},{9,10},{10,... | collective-permute-start | bytes 98312 | tf_op jit(solution)/shard_map/ppermute | solution.py:218

commit v5 on v4

--- a/solution.py
+++ b/solution.py
@@ -165,49 +165,39 @@
 
 
 def near_kernel(
-    x_ref, mate_ref, across_ref, corner_ref, edge_ref, tiles_ref, cols_ref, count_ref, acc_ref
+    x_ref, mate_ref, across_ref, corner_ref, edge_ref, even_ref, odd_ref, tiles_ref,
+    cols_ref, count_ref, acc_ref
 ):
     pos = lax.axis_index("level")
+    side = lax.axis_index("leaf") & 1
     odd = pos & 1
     inner = jnp.logical_or(pos == 1, pos == 2)
     acc = dot(x_ref[...], tiles_ref[0, 0]) + dot(mate_ref[...], tiles_ref[0, 2 - odd])
     beside = jnp.where(inner, corner_ref[...], edge_ref[...])
     acc_ref[...] = acc + dot(beside, tiles_ref[0, 1 + odd])
     col = cols_ref[0, SLOT]
-    turn = lax.rem(col, GROUP) ^ pos
-    here = jnp.logical_and(count_ref[0] > SLOT, col // GROUP == 1)
-    for at, block in enumerate((x_ref, mate_ref, across_ref, corner_ref)):
-        @pl.when(jnp.logical_and(here, turn == at))
+    group, turn = col // GROUP, lax.rem(col, GROUP) ^ pos
+    live = count_ref[0] > SLOT
+    from_even = (group == 0) == (side == 1)
+    sources = [
+        (jnp.logical_and(group == 1, turn == at), block)
+        for at, block in enumerate((x_ref, mate_ref, across_ref, corner_ref))
+    ] + [
+        (jnp.logical_and(group != 1, from_even), even_ref),
+        (jnp.logical_and(group != 1, jnp.logical_not(from_even)), odd_ref),
+    ]
+    for here, block in sources:
+        @pl.when(jnp.logical_and(live, here))
         def _(block=block):
             acc_ref[...] += dot(block[...], tiles_ref[0, SLOT])
 
 
-def finish_kernel(
-    acc_ref, even_ref, odd_ref, tiles_ref, w_ref, field0, field1, field2, field3,
-    cols_ref, count_ref, out_ref, total_ref, field_ref
-):
+def finish_kernel(acc_ref, w_ref, field0, field1, field2, field3, out_ref, field_ref):
     pos = lax.axis_index("level")
-    side = lax.axis_index("leaf") & 1
     for turn, part_ref in enumerate((field0, field1, field2, field3)):
         field_ref[part_of(pos ^ turn)] = part_ref[...]
     field = jnp.concatenate([field_ref[part] for part in range(GROUP)], axis=0)
-    group = cols_ref[0, SLOT] // GROUP
-    live = jnp.logical_and(count_ref[0] > SLOT, group != 1)
-    from_even = (group == 0) == (side == 1)
-    total = acc_ref[...] + dot_t(field, w_ref[...])
-
-    @pl.when(jnp.logical_not(live))
-    def _():
-        out_ref[...] = total.astype(BF16)
-
-    @pl.when(live)
-    def _():
-        total_ref[...] = total
-
-    for here, block in ((from_even, even_ref), (jnp.logical_not(from_even), odd_ref)):
-        @pl.when(jnp.logical_and(live, here))
-        def _(block=block):
-            out_ref[...] = (total_ref[...] + dot(block[...], tiles_ref[0, SLOT])).astype(BF16)
+    out_ref[...] = (acc_ref[...] + dot_t(field, w_ref[...])).astype(BF16)
 
 
 def part_of(pos):
@@ -343,17 +333,16 @@
     (to_odd,) = call(
         partial(pick_odd_kernel, rows, pairs, len(named)), "pick_odd", named + held, [], [block]
     )
-    (acc,) = call(
-        near_kernel, "near", held + [edge, near_tiles], [near_cols, near_count],
-        [((vectors, points), F32)],
-    )
-    field, to_odd, acc = lax.optimization_barrier((field, to_odd, acc))
+
     fields = [field] + [turned(field, turn) for turn in range(1, GROUP)]
     from_odd = neighbours(to_odd, 1)
+    (acc,) = call(
+        near_kernel, "near", held + [edge, from_even, from_odd, near_tiles],
+        [near_cols, near_count], [((vectors, points), F32)],
+    )
     (out,) = call(
-        finish_kernel, "finish", [acc, from_even, from_odd, near_tiles, w] + fields,
-        [near_cols, near_count], [block],
-        [pltpu.VMEM((vectors, points), F32), pltpu.VMEM((GROUP, rows, rank), BF16)],
+        finish_kernel, "finish", [acc, w] + fields, [], [block],
+        [pltpu.VMEM((GROUP, rows, rank), BF16)],
     )
     return out
 

time: 36.1 us -> 35 us (0.970)
  the two profiles are of different devices: /device:TPU:8 before, /device:TPU:0 now
where the time goes in v5:
time: 35 us; the launch traced here: 34.8 us
  starting transfers between devices  17.4 us (50%)
  waiting for transfers between devices  10 us (29%)
  Pallas kernels  6.5 us (19%)
  between operations  0.81 us (2%)
    ppermute x3, starting transfers between devices, per_device(): lax.ppermute(push, 'leaf', [(i, i ^ 2 * turn) for i in range(leaf_count)])  8.21 us
    pallas_call x7, Pallas kernels, call(): pl.pallas_call(kernel, out_shape=shapes, in_specs=[pl.BlockSpec(memory_sp...  6.5 us
    ppermute x8, starting transfers between devices, turned(): return lax.ppermute(value, 'level', [(i, i ^ turn) for i in range(GROUP)])  5.52 us
    ppermute x2, waiting for transfers between devices, neighbours(): return lax.ppermute(value, 'leaf', route + [(b, a) for a, b in route])  5.19 us
    ppermute x8, waiting for transfers between devices, turned(): return lax.ppermute(value, 'level', [(i, i ^ turn) for i in range(GROUP)])  2.63 us
    ppermute x1, starting transfers between devices, swapped(): lax.ppermute(value, 'leaf', [(i, i ^ 1 << distance) for i in range(count)])  2.24 us
    ppermute x1, waiting for transfers between devices, swapped(): lax.ppermute(value, 'leaf', [(i, i ^ 1 << distance) for i in range(count)])  1.31 us
    ppermute x3, waiting for transfers between devices, per_device(): lax.ppermute(push, 'leaf', [(i, i ^ 2 * turn) for i in range(leaf_count)])  0.86 us
  transfers between devices with their start and end apart: 15, of which 6 were waited for; matrix products, arithmetic and copies ran while one was open for 0% of the time, Pallas kernels for 11%

profile of v5, /device:TPU:0, one launch (start us, length us, event | category | flops | bytes accessed | tf_op | source)
XLA Modules:
  0.0 34.8 jit_solution(16123895510373282015)
XLA Ops:
  0.0 1.8 %up.1 = (bf16[160,256]{1,0:T(8,128)(2,1)S(1)}, bf16[160,256]{1,0:T(8,128)(2,1)S(1)}, bf16[512,256]{1,0:T(8,128)(2,1)S(1)}, bf16[256,512]{1,0:T(8,128)(2,1)S(1)},...) custom-call(bf16[256,512]{1,0:T(8,128)(2,1)} %x_hbm.1, bf16[1,512,256]{2,1,0:T(8,128)(2,1)} %basis_hbm.1, ...), custom_call_target="tpu_custom_call" | custom-call | tf_op jit(solution)/shard_map/up/pallas_call | solution.py:28
  1.9 0.5 %collective-permute-start.1 = (bf16[160,256]{1,0:T(8,128)(2,1)S(1)}, bf16[160,256]{1,0:T(8,128)(2,1)S(1)}, u32[]{:S(2)}, u32[]{:S(2)}) collective-permute-start(bf16[160,256]{1,0:T(8,128)(2,1)S(1)} %get-tuple-element.33), channel_id=1, source_target_pairs={{0,1},{1,0},{2,3},{3,2},{4,5},{5,4},{6,7},{7,6},{8,9},{9,8},{10,11... | collective-permute-start | bytes 245768 | tf_op jit(solution)/shard_map/ppermute | solution.py:208
  2.4 0.1 collective-permute-start
  2.5 0.8 %collective-permute-done.1 = bf16[160,256]{1,0:T(8,128)(2,1)S(1)} collective-permute-done((bf16[160,256]{1,0:T(8,128)(2,1)S(1)}, bf16[160,256]{1,0:T(8,128)(2,1)S(1)}, u32[]{:S(2)}, u32[]{:S(2)}) %collective-permute-start.1) | collective-permute-done | bytes 81952 | tf_op jit(solution)/shard_map/ppermute | solution.py:208
  3.3 2.9 %collective-permute-start.2 = (bf16[80,256]{1,0:T(8,128)(2,1)S(1)}, bf16[80,256]{1,0:T(8,128)(2,1)S(1)}, u32[]{:S(2)}, u32[]{:S(2)}) collective-permute-start(bf16[80,256]{1,0:T(8,128)(2,1)S(1)} %slice.20), channel_id=1, source_target_pairs={{0,2},{1,3},{2,0},{3,1},{4,6},{5,7},{6,4},{7,5},{8,10},{9,11},{10,... | collective-permute-start | bytes 122888 | tf_op jit(solution)/shard_map/ppermute | solution.py:208
  6.2 0.1 collective-permute-start.3
  6.3 1.7 %fold.1 = (bf16[2,256,256]{2,1,0:T(8,128)(2,1)S(1)}, bf16[2,256,256]{2,1,0:T(8,128)(2,1)S(1)}, bf16[2,256,256]{2,1,0:T(8,128)(2,1)S(1)}) custom-call(bf16[2,2,256,256]{3,2,1,0:T(8,128)(2,1)S(1)} %get-tuple-element.34.coupling_ref, bf16[2,256,256]{2,1,0:T(8,128)(2,1)S(1)} %get-tuple-element.35.transfer_ref, s32[6,2,8]{2,1,0:T(2,128)S(1)} %bitcast.1), custom_call_target="tpu_custom_call" | custom-call | tf_op jit(solution)/shard_map/fold/pallas_call | solution.py:28
  8.0 0.0 copy-start
  8.0 0.0 copy-start.2
  8.0 0.2 collective-permute-done.2
  8.2 0.0 collective-permute-done.refs_1_.refs_3_.mate_ref
  8.2 2.2 %collective-permute-start.4 = (bf16[80,256]{1,0:T(8,128)(2,1)S(1)}, bf16[80,256]{1,0:T(8,128)(2,1)S(1)}, u32[]{:S(2)}, u32[]{:S(2)}) collective-permute-start(bf16[80,256]{1,0:T(8,128)(2,1)S(1)} %add_convert_fusion.1.own_ref), channel_id=1, source_target_pairs={{0,4},{4,0},{8,12},{12,8},{16,20},{20,16},{24,28},{28,24},{1,5},{5... | collective-permute-start | bytes 122888 | tf_op jit(solution)/shard_map/ppermute | solution.py:219
  10.5 0.7 %collective-permute-start.5 = (bf16[256,512]{1,0:T(8,128)(2,1)S(1)}, bf16[256,512]{1,0:T(8,128)(2,1)S(1)}, u32[]{:S(2)}, u32[]{:S(2)}) collective-permute-start(bf16[256,512]{1,0:T(8,128)(2,1)S(1)} %copy-done.3), channel_id=1, source_target_pairs={{3,4},{7,8},{11,12},{15,16},{19,20},{23,24},{27,28},{4,3},{8,7},{1... | collective-permute-start | bytes 786440 | tf_op jit(solution)/shard_map/ppermute | solution.py:301
  11.2 1.3 %collective-permute-done.4.mate_ref.named_ref = bf16[80,256]{1,0:T(8,128)(2,1)S(1)} collective-permute-done((bf16[80,256]{1,0:T(8,128)(2,1)S(1)}, bf16[80,256]{1,0:T(8,128)(2,1)S(1)}, u32[]{:S(2)}, u32[]{:S(2)}) %collective-permute-start.4) | collective-permute-done | bytes 40992 | tf_op jit(solution)/shard_map/ppermute | solution.py:219
  12.5 0.3 push.1
  12.7 1.6 %collective-permute-done.3.refs_2_.refs_4_.across_ref = bf16[256,512]{1,0:T(8,128)(2,1)S(1)} collective-permute-done((bf16[256,512]{1,0:T(8,128)(2,1)S(1)}, bf16[256,512]{1,0:T(8,128)(2,1)S(1)}, u32[]{:S(2)}, u32[]{:S(2)}) %collective-permute-start.3) | collective-permute-done | bytes 262176 | tf_op jit(solution)/shard_map/ppermute | solution.py:208
  14.3 0.0 collective-permute-start.6
  14.3 1.6 %collective-permute-start.8 = (bf16[80,256]{1,0:T(8,128)(2,1)S(1)}, bf16[80,256]{1,0:T(8,128)(2,1)S(1)}, u32[]{:S(2)}, u32[]{:S(2)}) collective-permute-start(bf16[80,256]{1,0:T(8,128)(2,1)S(1)} %get-tuple-element.53), channel_id=1, source_target_pairs={{0,8},{4,12},{8,0},{12,4},{16,24},{20,28},{24,16},{28,20},{1,9},{5... | collective-permute-start | bytes 122888 | tf_op jit(solution)/shard_map/ppermute | solution.py:318
  16.0 2.5 %collective-permute-start.9 = (bf16[80,256]{1,0:T(8,128)(2,1)S(1)}, bf16[80,256]{1,0:T(8,128)(2,1)S(1)}, u32[]{:S(2)}, u32[]{:S(2)}) collective-permute-start(bf16[80,256]{1,0:T(8,128)(2,1)S(1)} %get-tuple-element.54), channel_id=1, source_target_pairs={{0,24},{4,28},{8,16},{12,20},{16,8},{20,12},{24,0},{28,4},{1,25},{... | collective-permute-start | bytes 122888 | tf_op jit(solution)/shard_map/ppermute | solution.py:318
  18.4 0.0 collective-permute-done.5.edge_ref
  18.4 4.1 %collective-permute-start.11 = (bf16[80,256]{1,0:T(8,128)(2,1)S(1)}, bf16[80,256]{1,0:T(8,128)(2,1)S(1)}, u32[]{:S(2)}, u32[]{:S(2)}) collective-permute-start(bf16[80,256]{1,0:T(8,128)(2,1)S(1)} %get-tuple-element.56), channel_id=1, source_target_pairs={{0,16},{4,20},{8,24},{12,28},{16,0},{20,4},{24,8},{28,12},{1,17},{... | collective-permute-start | bytes 122888 | tf_op jit(solution)/shard_map/ppermute | solution.py:318
  22.6 0.2 pick_even.1
  22.7 0.1 collective-permute-start.7
  22.8 0.2 pick_odd.1
  23.0 0.7 %collective-permute-start.10 = (bf16[256,512]{1,0:T(8,128)(2,1)S(1)}, bf16[256,512]{1,0:T(8,128)(2,1)S(1)}, u32[]{:S(2)}, u32[]{:S(2)}) collective-permute-start(bf16[256,512]{1,0:T(8,128)(2,1)S(1)} %pick_odd.1), channel_id=1, source_target_pairs={{4,8},{12,16},{20,24},{8,4},{16,12},{24,20},{5,9},{13,17},{21,25},... | collective-permute-start | bytes 786440 | tf_op jit(solution)/shard_map/ppermute | solution.py:225
  23.7 0.9 %collective-permute-done.11 = bf16[80,256]{1,0:T(8,128)(2,1)S(1)} collective-permute-done((bf16[80,256]{1,0:T(8,128)(2,1)S(1)}, bf16[80,256]{1,0:T(8,128)(2,1)S(1)}, u32[]{:S(2)}, u32[]{:S(2)}) %collective-permute-start.11) | collective-permute-done | bytes 40992 | tf_op jit(solution)/shard_map/ppermute | solution.py:318
  24.6 0.1 collective-permute-start.12
  24.6 0.8 %collective-permute-start.13 = (bf16[64,256]{1,0:T(8,128)(2,1)S(1)}, bf16[64,256]{1,0:T(8,128)(2,1)S(1)}, u32[]{:S(2)}, u32[]{:S(2)}) collective-permute-start(bf16[64,256]{1,0:T(8,128)(2,1)S(1)} %add_convert_fusion.2.field0), channel_id=1, source_target_pairs={{0,2},{1,3},{2,0},{3,1},{4,6},{5,7},{6,4},{7,5},{8,10},{9,11},{10,... | collective-permute-start | bytes 98312 | tf_op jit(solution)/shard_map/ppermute | solution.py:208
  25.5 1.0 %collective-permute-start.14 = (bf16[64,256]{1,0:T(8,128)(2,1)S(1)}, bf16[64,256]{1,0:T(8,128)(2,1)S(1)}, u32[]{:S(2)}, u32[]{:S(2)}) collective-permute-start(bf16[64,256]{1,0:T(8,128)(2,1)S(1)} %add_convert_fusion.2.field0), channel_id=1, source_target_pairs={{0,3},{1,2},{2,1},{3,0},{4,7},{5,6},{6,5},{7,4},{8,11},{9,10},{10,... | collective-permute-start | bytes 98312 | tf_op jit(solution)/shard_map/ppermute | solution.py:208
  27.1 5.2 %collective-permute-done.7.even_ref = bf16[256,512]{1,0:T(8,128)(2,1)S(1)} collective-permute-done((bf16[256,512]{1,0:T(8,128)(2,1)S(1)}, bf16[256,512]{1,0:T(8,128)(2,1)S(1)}, u32[]{:S(2)}, u32[]{:S(2)}) %collective-permute-start.7) | collective-permute-done | bytes 262176 | tf_op jit(solution)/shard_map/ppermute | solution.py:225
  32.3 1.4 %near.1.acc_ref = f32[256,512]{1,0:T(8,128)S(1)} custom-call(bf16[256,512]{1,0:T(8,128)(2,1)S(1)} %get-tuple-element.31.refs_0_.refs_2_.x_ref, bf16[256,512]{1,0:T(8,128)(2,1)S(1)} %collective-permute-done.refs_1_.refs_3_.mate_ref, bf16[256,512]{1,0:T(8,128)(2,1)S(1)} %collective-permute-done.3.refs_2_.refs_4_.across_ref, ...), custom_call_target="tpu_custom_call" | custom-call | tf_op jit(solution)/shard_map/near/pallas_call | solution.py:28
  33.8 1.0 %finish.1 = bf16[256,512]{1,0:T(8,128)(2,1)} custom-call(f32[256,512]{1,0:T(8,128)S(1)} %near.1.acc_ref, bf16[512,256]{1,0:T(8,128)(2,1)S(1)} %get-tuple-element.55.w_ref, bf16[64,256]{1,0:T(8,128)(2,1)S(1)} %add_convert_fusion.2.field0, bf16[64,256]{1,0:T(8,128)(2,1)S(1)} %collective-permute-done.12.field1, ...), custom_call_target="tpu_custom_call" | custom-call | tf_op jit(solution)/shard_map/finish/pallas_call | solution.py:28
  (17 shorter events, 0.1 us)
Async XLA Ops:
  0.0 2.4 %copy-start.3 = (bf16[256,512]{1,0:T(8,128)(2,1)S(1)}, bf16[256,512]{1,0:T(8,128)(2,1)}, u32[]{:S(2)}) copy-start(bf16[256,512]{1,0:T(8,128)(2,1)} %x_hbm.1) | copy-start | bytes 786436
  0.0 6.3 %copy-start.1 = (s32[6,8,2]{1,2,0:T(2,128)S(1)}, s32[6,8,2]{1,2,0:T(2,128)}, u32[]{:S(2)}) copy-start(s32[6,8,2]{1,2,0:T(2,128)} %param.15) | copy-start | bytes 1156
  1.9 1.4 %collective-permute-start.1 = (bf16[160,256]{1,0:T(8,128)(2,1)S(1)}, bf16[160,256]{1,0:T(8,128)(2,1)S(1)}, u32[]{:S(2)}, u32[]{:S(2)}) collective-permute-start(bf16[160,256]{1,0:T(8,128)(2,1)S(1)} %get-tuple-element.33), channel_id=1, source_target_pairs={{0,1},{1,0},{2,3},{3,2},{4,5},{5,4},{6,7},{7,6},{8,9},{9,8},{10,11... | collective-permute-start | bytes 245768 | tf_op jit(solution)/shard_map/ppermute | solution.py:208
  2.4 5.8 %collective-permute-start = (bf16[256,512]{1,0:T(8,128)(2,1)S(1)}, bf16[256,512]{1,0:T(8,128)(2,1)S(1)}, u32[]{:S(2)}, u32[]{:S(2)}) collective-permute-start(bf16[256,512]{1,0:T(8,128)(2,1)S(1)} %copy-done.3), channel_id=1, source_target_pairs={{0,1},{1,0},{2,3},{3,2},{4,5},{5,4},{6,7},{7,6},{8,9},{9,8},{10,11... | collective-permute-start | bytes 786440 | tf_op jit(solution)/shard_map/ppermute | solution.py:208
  3.3 4.9 %collective-permute-start.2 = (bf16[80,256]{1,0:T(8,128)(2,1)S(1)}, bf16[80,256]{1,0:T(8,128)(2,1)S(1)}, u32[]{:S(2)}, u32[]{:S(2)}) collective-permute-start(bf16[80,256]{1,0:T(8,128)(2,1)S(1)} %slice.20), channel_id=1, source_target_pairs={{0,2},{1,3},{2,0},{3,1},{4,6},{5,7},{6,4},{7,5},{8,10},{9,11},{10,... | collective-permute-start | bytes 122888 | tf_op jit(solution)/shard_map/ppermute | solution.py:208
  6.2 8.1 %collective-permute-start.3 = (bf16[256,512]{1,0:T(8,128)(2,1)S(1)}, bf16[256,512]{1,0:T(8,128)(2,1)S(1)}, u32[]{:S(2)}, u32[]{:S(2)}) collective-permute-start(bf16[256,512]{1,0:T(8,128)(2,1)S(1)} %copy-done.3), channel_id=1, source_target_pairs={{0,2},{1,3},{2,0},{3,1},{4,6},{5,7},{6,4},{7,5},{8,10},{9,11},{10,... | collective-permute-start | bytes 786440 | tf_op jit(solution)/shard_map/ppermute | solution.py:208
  8.0 24.3 %copy-start = (bf16[1,4,512,512]{3,2,1,0:T(8,128)(2,1)S(1)}, bf16[1,4,512,512]{3,2,1,0:T(8,128)(2,1)}, u32[]{:S(2)}) copy-start(bf16[1,4,512,512]{3,2,1,0:T(8,128)(2,1)} %tiles_ref.1) | copy-start | bytes 6291460
  8.0 24.3 %copy-start.2 = (s32[1,4]{1,0:T(1,128)S(1)}, s32[1,4]{1,0:T(1,128)}, u32[]{:S(2)}) copy-start(s32[1,4]{1,0:T(1,128)} %cols_ref.1) | copy-start | bytes 52
  8.2 4.2 %collective-permute-start.4 = (bf16[80,256]{1,0:T(8,128)(2,1)S(1)}, bf16[80,256]{1,0:T(8,128)(2,1)S(1)}, u32[]{:S(2)}, u32[]{:S(2)}) collective-permute-start(bf16[80,256]{1,0:T(8,128)(2,1)S(1)} %add_convert_fusion.1.own_ref), channel_id=1, source_target_pairs={{0,4},{4,0},{8,12},{12,8},{16,20},{20,16},{24,28},{28,24},{1,5},{5... | collective-permute-start | bytes 122888 | tf_op jit(solution)/shard_map/ppermute | solution.py:219
  10.5 7.9 %collective-permute-start.5 = (bf16[256,512]{1,0:T(8,128)(2,1)S(1)}, bf16[256,512]{1,0:T(8,128)(2,1)S(1)}, u32[]{:S(2)}, u32[]{:S(2)}) collective-permute-start(bf16[256,512]{1,0:T(8,128)(2,1)S(1)} %copy-done.3), channel_id=1, source_target_pairs={{3,4},{7,8},{11,12},{15,16},{19,20},{23,24},{27,28},{4,3},{8,7},{1... | collective-permute-start | bytes 786440 | tf_op jit(solution)/shard_map/ppermute | solution.py:301
  14.3 4.1 %collective-permute-start.6 = (bf16[256,512]{1,0:T(8,128)(2,1)S(1)}, bf16[256,512]{1,0:T(8,128)(2,1)S(1)}, u32[]{:S(2)}, u32[]{:S(2)}) collective-permute-start(bf16[256,512]{1,0:T(8,128)(2,1)S(1)} %collective-permute-done.3.refs_2_.refs_4_.across_ref), channel_id=1, source_target_pairs={{0,1},{1,0},{2,3},{3,2},{4,5},{5,4},{6,7},{7,6},{8,9},{9,8},{10,11... | collective-permute-start | bytes 786440 | tf_op jit(solution)/shard_map/ppermute | solution.py:208
  14.3 8.5 %collective-permute-start.8 = (bf16[80,256]{1,0:T(8,128)(2,1)S(1)}, bf16[80,256]{1,0:T(8,128)(2,1)S(1)}, u32[]{:S(2)}, u32[]{:S(2)}) collective-permute-start(bf16[80,256]{1,0:T(8,128)(2,1)S(1)} %get-tuple-element.53), channel_id=1, source_target_pairs={{0,8},{4,12},{8,0},{12,4},{16,24},{20,28},{24,16},{28,20},{1,9},{5... | collective-permute-start | bytes 122888 | tf_op jit(solution)/shard_map/ppermute | solution.py:318
  16.0 6.9 %collective-permute-start.9 = (bf16[80,256]{1,0:T(8,128)(2,1)S(1)}, bf16[80,256]{1,0:T(8,128)(2,1)S(1)}, u32[]{:S(2)}, u32[]{:S(2)}) collective-permute-start(bf16[80,256]{1,0:T(8,128)(2,1)S(1)} %get-tuple-element.54), channel_id=1, source_target_pairs={{0,24},{4,28},{8,16},{12,20},{16,8},{20,12},{24,0},{28,4},{1,25},{... | collective-permute-start | bytes 122888 | tf_op jit(solution)/shard_map/ppermute | solution.py:318
  18.4 6.1 %collective-permute-start.11 = (bf16[80,256]{1,0:T(8,128)(2,1)S(1)}, bf16[80,256]{1,0:T(8,128)(2,1)S(1)}, u32[]{:S(2)}, u32[]{:S(2)}) collective-permute-start(bf16[80,256]{1,0:T(8,128)(2,1)S(1)} %get-tuple-element.56), channel_id=1, source_target_pairs={{0,16},{4,20},{8,24},{12,28},{16,0},{20,4},{24,8},{28,12},{1,17},{... | collective-permute-start | bytes 122888 | tf_op jit(solution)/shard_map/ppermute | solution.py:318
  22.7 9.6 %collective-permute-start.7 = (bf16[256,512]{1,0:T(8,128)(2,1)S(1)}, bf16[256,512]{1,0:T(8,128)(2,1)S(1)}, u32[]{:S(2)}, u32[]{:S(2)}) collective-permute-start(bf16[256,512]{1,0:T(8,128)(2,1)S(1)} %pick_even.1), channel_id=1, source_target_pairs={{0,4},{8,12},{16,20},{24,28},{4,0},{12,8},{20,16},{28,24},{1,5},{9... | collective-permute-start | bytes 786440 | tf_op jit(solution)/shard_map/ppermute | solution.py:225
  23.0 9.3 %collective-permute-start.10 = (bf16[256,512]{1,0:T(8,128)(2,1)S(1)}, bf16[256,512]{1,0:T(8,128)(2,1)S(1)}, u32[]{:S(2)}, u32[]{:S(2)}) collective-permute-start(bf16[256,512]{1,0:T(8,128)(2,1)S(1)} %pick_odd.1), channel_id=1, source_target_pairs={{4,8},{12,16},{20,24},{8,4},{16,12},{24,20},{5,9},{13,17},{21,25},... | collective-permute-start | bytes 786440 | tf_op jit(solution)/shard_map/ppermute | solution.py:225
  24.6 9.2 %collective-permute-start.12 = (bf16[64,256]{1,0:T(8,128)(2,1)S(1)}, bf16[64,256]{1,0:T(8,128)(2,1)S(1)}, u32[]{:S(2)}, u32[]{:S(2)}) collective-permute-start(bf16[64,256]{1,0:T(8,128)(2,1)S(1)} %add_convert_fusion.2.field0), channel_id=1, source_target_pairs={{0,1},{1,0},{2,3},{3,2},{4,5},{5,4},{6,7},{7,6},{8,9},{9,8},{10,11... | collective-permute-start | bytes 98312 | tf_op jit(solution)/shard_map/ppermute | solution.py:208
  24.6 9.2 %collective-permute-start.13 = (bf16[64,256]{1,0:T(8,128)(2,1)S(1)}, bf16[64,256]{1,0:T(8,128)(2,1)S(1)}, u32[]{:S(2)}, u32[]{:S(2)}) collective-permute-start(bf16[64,256]{1,0:T(8,128)(2,1)S(1)} %add_convert_fusion.2.field0), channel_id=1, source_target_pairs={{0,2},{1,3},{2,0},{3,1},{4,6},{5,7},{6,4},{7,5},{8,10},{9,11},{10,... | collective-permute-start | bytes 98312 | tf_op jit(solution)/shard_map/ppermute | solution.py:208
  25.5 8.3 %collective-permute-start.14 = (bf16[64,256]{1,0:T(8,128)(2,1)S(1)}, bf16[64,256]{1,0:T(8,128)(2,1)S(1)}, u32[]{:S(2)}, u32[]{:S(2)}) collective-permute-start(bf16[64,256]{1,0:T(8,128)(2,1)S(1)} %add_convert_fusion.2.field0), channel_id=1, source_target_pairs={{0,3},{1,2},{2,1},{3,0},{4,7},{5,6},{6,5},{7,4},{8,11},{9,10},{10,... | collective-permute-start | bytes 98312 | tf_op jit(solution)/shard_map/ppermute | solution.py:208

commit v6 on v4

--- a/solution.py
+++ b/solution.py
@@ -347,7 +347,6 @@
         near_kernel, "near", held + [edge, near_tiles], [near_cols, near_count],
         [((vectors, points), F32)],
     )
-    field, to_odd, acc = lax.optimization_barrier((field, to_odd, acc))
     fields = [field] + [turned(field, turn) for turn in range(1, GROUP)]
     from_odd = neighbours(to_odd, 1)
     (out,) = call(

time: 36.1 us -> 34.2 us (0.947)
  the two profiles are of different devices: /device:TPU:8 before, /device:TPU:0 now
where the time goes in v6:
time: 34.2 us; the launch traced here: 33.9 us
  starting transfers between devices  17.4 us (51%)
  waiting for transfers between devices  8.81 us (26%)
  Pallas kernels  6.78 us (20%)
  between operations  0.81 us (2%)
    ppermute x3, starting transfers between devices, per_device(): lax.ppermute(push, 'leaf', [(i, i ^ 2 * turn) for i in range(leaf_count)])  8.22 us
    pallas_call x7, Pallas kernels, call(): pl.pallas_call(kernel, out_shape=shapes, in_specs=[pl.BlockSpec(memory_sp...  6.78 us
    ppermute x8, starting transfers between devices, turned(): return lax.ppermute(value, 'level', [(i, i ^ turn) for i in range(GROUP)])  5.52 us
    ppermute x8, waiting for transfers between devices, turned(): return lax.ppermute(value, 'level', [(i, i ^ turn) for i in range(GROUP)])  3.42 us
    ppermute x2, waiting for transfers between devices, neighbours(): return lax.ppermute(value, 'leaf', route + [(b, a) for a, b in route])  3.22 us
    ppermute x1, starting transfers between devices, swapped(): lax.ppermute(value, 'leaf', [(i, i ^ 1 << distance) for i in range(count)])  2.24 us
    ppermute x1, waiting for transfers between devices, swapped(): lax.ppermute(value, 'leaf', [(i, i ^ 1 << distance) for i in range(count)])  1.31 us
    ppermute x3, waiting for transfers between devices, per_device(): lax.ppermute(push, 'leaf', [(i, i ^ 2 * turn) for i in range(leaf_count)])  0.86 us
  transfers between devices with their start and end apart: 15, of which 8 were waited for; matrix products, arithmetic and copies ran while one was open for 0% of the time, Pallas kernels for 10%

profile of v6, /device:TPU:0, one launch (start us, length us, event | category | flops | bytes accessed | tf_op | source)
XLA Modules:
  0.0 33.9 jit_solution(996241770179151333)
XLA Ops:
  0.0 1.8 %up.1 = (bf16[160,256]{1,0:T(8,128)(2,1)S(1)}, bf16[160,256]{1,0:T(8,128)(2,1)S(1)}, bf16[512,256]{1,0:T(8,128)(2,1)S(1)}, bf16[256,512]{1,0:T(8,128)(2,1)S(1)},...) custom-call(bf16[256,512]{1,0:T(8,128)(2,1)} %x_hbm.1, bf16[1,512,256]{2,1,0:T(8,128)(2,1)} %basis_hbm.1, ...), custom_call_target="tpu_custom_call" | custom-call | tf_op jit(solution)/shard_map/up/pallas_call | solution.py:28
  1.9 0.5 %collective-permute-start.1 = (bf16[160,256]{1,0:T(8,128)(2,1)S(1)}, bf16[160,256]{1,0:T(8,128)(2,1)S(1)}, u32[]{:S(2)}, u32[]{:S(2)}) collective-permute-start(bf16[160,256]{1,0:T(8,128)(2,1)S(1)} %get-tuple-element.33), channel_id=1, source_target_pairs={{0,1},{1,0},{2,3},{3,2},{4,5},{5,4},{6,7},{7,6},{8,9},{9,8},{10,11... | collective-permute-start | bytes 245768 | tf_op jit(solution)/shard_map/ppermute | solution.py:218
  2.4 0.1 collective-permute-start
  2.5 0.8 %collective-permute-done.1 = bf16[160,256]{1,0:T(8,128)(2,1)S(1)} collective-permute-done((bf16[160,256]{1,0:T(8,128)(2,1)S(1)}, bf16[160,256]{1,0:T(8,128)(2,1)S(1)}, u32[]{:S(2)}, u32[]{:S(2)}) %collective-permute-start.1) | collective-permute-done | bytes 81952 | tf_op jit(solution)/shard_map/ppermute | solution.py:218
  3.3 2.9 %collective-permute-start.2 = (bf16[80,256]{1,0:T(8,128)(2,1)S(1)}, bf16[80,256]{1,0:T(8,128)(2,1)S(1)}, u32[]{:S(2)}, u32[]{:S(2)}) collective-permute-start(bf16[80,256]{1,0:T(8,128)(2,1)S(1)} %slice.20), channel_id=1, source_target_pairs={{0,2},{1,3},{2,0},{3,1},{4,6},{5,7},{6,4},{7,5},{8,10},{9,11},{10,... | collective-permute-start | bytes 122888 | tf_op jit(solution)/shard_map/ppermute | solution.py:218
  6.2 0.1 collective-permute-start.3
  6.3 1.7 %fold.1 = (bf16[2,256,256]{2,1,0:T(8,128)(2,1)S(1)}, bf16[2,256,256]{2,1,0:T(8,128)(2,1)S(1)}, bf16[2,256,256]{2,1,0:T(8,128)(2,1)S(1)}) custom-call(bf16[2,2,256,256]{3,2,1,0:T(8,128)(2,1)S(1)} %get-tuple-element.34.coupling_ref, bf16[2,256,256]{2,1,0:T(8,128)(2,1)S(1)} %get-tuple-element.35.transfer_ref, s32[6,2,8]{2,1,0:T(2,128)S(1)} %bitcast.1), custom_call_target="tpu_custom_call" | custom-call | tf_op jit(solution)/shard_map/fold/pallas_call | solution.py:28
  8.0 0.0 copy-start
  8.0 0.0 copy-start.2
  8.0 0.2 collective-permute-done.2
  8.2 0.0 collective-permute-done.mate_ref.refs_1_.refs_3_
  8.2 2.2 %collective-permute-start.4 = (bf16[80,256]{1,0:T(8,128)(2,1)S(1)}, bf16[80,256]{1,0:T(8,128)(2,1)S(1)}, u32[]{:S(2)}, u32[]{:S(2)}) collective-permute-start(bf16[80,256]{1,0:T(8,128)(2,1)S(1)} %add_convert_fusion.1.own_ref), channel_id=1, source_target_pairs={{0,4},{4,0},{8,12},{12,8},{16,20},{20,16},{24,28},{28,24},{1,5},{5... | collective-permute-start | bytes 122888 | tf_op jit(solution)/shard_map/ppermute | solution.py:229
  10.5 0.7 %collective-permute-start.5 = (bf16[256,512]{1,0:T(8,128)(2,1)S(1)}, bf16[256,512]{1,0:T(8,128)(2,1)S(1)}, u32[]{:S(2)}, u32[]{:S(2)}) collective-permute-start(bf16[256,512]{1,0:T(8,128)(2,1)S(1)} %copy-done.3), channel_id=1, source_target_pairs={{3,4},{7,8},{11,12},{15,16},{19,20},{23,24},{27,28},{4,3},{8,7},{1... | collective-permute-start | bytes 786440 | tf_op jit(solution)/shard_map/ppermute | solution.py:311
  11.2 1.3 %collective-permute-done.4.mate_ref.named_ref = bf16[80,256]{1,0:T(8,128)(2,1)S(1)} collective-permute-done((bf16[80,256]{1,0:T(8,128)(2,1)S(1)}, bf16[80,256]{1,0:T(8,128)(2,1)S(1)}, u32[]{:S(2)}, u32[]{:S(2)}) %collective-permute-start.4) | collective-permute-done | bytes 40992 | tf_op jit(solution)/shard_map/ppermute | solution.py:229
  12.5 0.3 push.1
  12.7 1.6 %collective-permute-done.3.across_ref.refs_2_.refs_4_ = bf16[256,512]{1,0:T(8,128)(2,1)S(1)} collective-permute-done((bf16[256,512]{1,0:T(8,128)(2,1)S(1)}, bf16[256,512]{1,0:T(8,128)(2,1)S(1)}, u32[]{:S(2)}, u32[]{:S(2)}) %collective-permute-start.3) | collective-permute-done | bytes 262176 | tf_op jit(solution)/shard_map/ppermute | solution.py:218
  14.3 1.6 %collective-permute-start.8 = (bf16[80,256]{1,0:T(8,128)(2,1)S(1)}, bf16[80,256]{1,0:T(8,128)(2,1)S(1)}, u32[]{:S(2)}, u32[]{:S(2)}) collective-permute-start(bf16[80,256]{1,0:T(8,128)(2,1)S(1)} %get-tuple-element.53), channel_id=1, source_target_pairs={{0,8},{4,12},{8,0},{12,4},{16,24},{20,28},{24,16},{28,20},{1,9},{5... | collective-permute-start | bytes 122888 | tf_op jit(solution)/shard_map/ppermute | solution.py:328
  15.9 2.5 %collective-permute-start.9 = (bf16[80,256]{1,0:T(8,128)(2,1)S(1)}, bf16[80,256]{1,0:T(8,128)(2,1)S(1)}, u32[]{:S(2)}, u32[]{:S(2)}) collective-permute-start(bf16[80,256]{1,0:T(8,128)(2,1)S(1)} %get-tuple-element.54), channel_id=1, source_target_pairs={{0,24},{4,28},{8,16},{12,20},{16,8},{20,12},{24,0},{28,4},{1,25},{... | collective-permute-start | bytes 122888 | tf_op jit(solution)/shard_map/ppermute | solution.py:328
  18.4 4.1 %collective-permute-start.11 = (bf16[80,256]{1,0:T(8,128)(2,1)S(1)}, bf16[80,256]{1,0:T(8,128)(2,1)S(1)}, u32[]{:S(2)}, u32[]{:S(2)}) collective-permute-start(bf16[80,256]{1,0:T(8,128)(2,1)S(1)} %get-tuple-element.56), channel_id=1, source_target_pairs={{0,16},{4,20},{8,24},{12,28},{16,0},{20,4},{24,8},{28,12},{1,17},{... | collective-permute-start | bytes 122888 | tf_op jit(solution)/shard_map/ppermute | solution.py:328
  22.6 0.2 pick_even.1
  22.7 0.1 collective-permute-start.7
  22.8 0.2 pick_odd.1
  23.0 0.7 %collective-permute-start.10 = (bf16[256,512]{1,0:T(8,128)(2,1)S(1)}, bf16[256,512]{1,0:T(8,128)(2,1)S(1)}, u32[]{:S(2)}, u32[]{:S(2)}) collective-permute-start(bf16[256,512]{1,0:T(8,128)(2,1)S(1)} %pick_odd.1), channel_id=1, source_target_pairs={{4,8},{12,16},{20,24},{8,4},{16,12},{24,20},{5,9},{13,17},{21,25},... | collective-permute-start | bytes 786440 | tf_op jit(solution)/shard_map/ppermute | solution.py:235
  23.7 0.9 %collective-permute-done.11 = bf16[80,256]{1,0:T(8,128)(2,1)S(1)} collective-permute-done((bf16[80,256]{1,0:T(8,128)(2,1)S(1)}, bf16[80,256]{1,0:T(8,128)(2,1)S(1)}, u32[]{:S(2)}, u32[]{:S(2)}) %collective-permute-start.11) | collective-permute-done | bytes 40992 | tf_op jit(solution)/shard_map/ppermute | solution.py:328
  24.6 0.1 collective-permute-start.12
  24.6 0.8 %collective-permute-start.13 = (bf16[64,256]{1,0:T(8,128)(2,1)S(1)}, bf16[64,256]{1,0:T(8,128)(2,1)S(1)}, u32[]{:S(2)}, u32[]{:S(2)}) collective-permute-start(bf16[64,256]{1,0:T(8,128)(2,1)S(1)} %add_convert_fusion.2.field0), channel_id=1, source_target_pairs={{0,2},{1,3},{2,0},{3,1},{4,6},{5,7},{6,4},{7,5},{8,10},{9,11},{10,... | collective-permute-start | bytes 98312 | tf_op jit(solution)/shard_map/ppermute | solution.py:218
  25.5 1.0 %collective-permute-start.14 = (bf16[64,256]{1,0:T(8,128)(2,1)S(1)}, bf16[64,256]{1,0:T(8,128)(2,1)S(1)}, u32[]{:S(2)}, u32[]{:S(2)}) collective-permute-start(bf16[64,256]{1,0:T(8,128)(2,1)S(1)} %add_convert_fusion.2.field0), channel_id=1, source_target_pairs={{0,3},{1,2},{2,1},{3,0},{4,7},{5,6},{6,5},{7,4},{8,11},{9,10},{10,... | collective-permute-start | bytes 98312 | tf_op jit(solution)/shard_map/ppermute | solution.py:218
  27.2 1.1 %near.1.acc_ref = f32[256,512]{1,0:T(8,128)S(1)} custom-call(bf16[256,512]{1,0:T(8,128)(2,1)S(1)} %get-tuple-element.31.x_ref.refs_0_.refs_2_, bf16[256,512]{1,0:T(8,128)(2,1)S(1)} %collective-permute-done.mate_ref.refs_1_.refs_3_, bf16[256,512]{1,0:T(8,128)(2,1)S(1)} %collective-permute-done.3.across_ref.refs_2_.refs_4_, ...), custom_call_target="tpu_custom_call" | custom-call | tf_op jit(solution)/shard_map/near/pallas_call | solution.py:28
  28.3 0.4 %collective-permute-done.13.field2 = bf16[64,256]{1,0:T(8,128)(2,1)S(1)} collective-permute-done((bf16[64,256]{1,0:T(8,128)(2,1)S(1)}, bf16[64,256]{1,0:T(8,128)(2,1)S(1)}, u32[]{:S(2)}, u32[]{:S(2)}) %collective-permute-start.13) | collective-permute-done | bytes 32800 | tf_op jit(solution)/shard_map/ppermute | solution.py:218
  28.8 0.4 %collective-permute-done.14.field3 = bf16[64,256]{1,0:T(8,128)(2,1)S(1)} collective-permute-done((bf16[64,256]{1,0:T(8,128)(2,1)S(1)}, bf16[64,256]{1,0:T(8,128)(2,1)S(1)}, u32[]{:S(2)}, u32[]{:S(2)}) %collective-permute-start.14) | collective-permute-done | bytes 32800 | tf_op jit(solution)/shard_map/ppermute | solution.py:218
  29.1 3.2 %collective-permute-done.7.even_ref = bf16[256,512]{1,0:T(8,128)(2,1)S(1)} collective-permute-done((bf16[256,512]{1,0:T(8,128)(2,1)S(1)}, bf16[256,512]{1,0:T(8,128)(2,1)S(1)}, u32[]{:S(2)}, u32[]{:S(2)}) %collective-permute-start.7) | collective-permute-done | bytes 262176 | tf_op jit(solution)/shard_map/ppermute | solution.py:235
  32.3 1.5 %finish.1 = bf16[256,512]{1,0:T(8,128)(2,1)} custom-call(f32[256,512]{1,0:T(8,128)S(1)} %near.1.acc_ref, bf16[256,512]{1,0:T(8,128)(2,1)S(1)} %collective-permute-done.7.even_ref, bf16[256,512]{1,0:T(8,128)(2,1)S(1)} %collective-permute-done.10.odd_ref, bf16[1,4,512,512]{3,2,1,0:T(8,128)(2,1)S(1)} %copy-done, bf16[512,256]{1,0:T(8,128)(2,1)S(1)} %get-tuple-element.55.w_ref, ...), custom_call_target="tpu_custom_call" | custom-call | tf_op jit(solution)/shard_map/finish/pallas_call | solution.py:28
  (17 shorter events, 0.1 us)
Async XLA Ops:
  0.0 2.4 %copy-start.3 = (bf16[256,512]{1,0:T(8,128)(2,1)S(1)}, bf16[256,512]{1,0:T(8,128)(2,1)}, u32[]{:S(2)}) copy-start(bf16[256,512]{1,0:T(8,128)(2,1)} %x_hbm.1) | copy-start | bytes 786436
  0.0 6.3 %copy-start.1 = (s32[6,8,2]{1,2,0:T(2,128)S(1)}, s32[6,8,2]{1,2,0:T(2,128)}, u32[]{:S(2)}) copy-start(s32[6,8,2]{1,2,0:T(2,128)} %param.15) | copy-start | bytes 1156
  1.9 1.4 %collective-permute-start.1 = (bf16[160,256]{1,0:T(8,128)(2,1)S(1)}, bf16[160,256]{1,0:T(8,128)(2,1)S(1)}, u32[]{:S(2)}, u32[]{:S(2)}) collective-permute-start(bf16[160,256]{1,0:T(8,128)(2,1)S(1)} %get-tuple-element.33), channel_id=1, source_target_pairs={{0,1},{1,0},{2,3},{3,2},{4,5},{5,4},{6,7},{7,6},{8,9},{9,8},{10,11... | collective-permute-start | bytes 245768 | tf_op jit(solution)/shard_map/ppermute | solution.py:218
  2.4 5.8 %collective-permute-start = (bf16[256,512]{1,0:T(8,128)(2,1)S(1)}, bf16[256,512]{1,0:T(8,128)(2,1)S(1)}, u32[]{:S(2)}, u32[]{:S(2)}) collective-permute-start(bf16[256,512]{1,0:T(8,128)(2,1)S(1)} %copy-done.3), channel_id=1, source_target_pairs={{0,1},{1,0},{2,3},{3,2},{4,5},{5,4},{6,7},{7,6},{8,9},{9,8},{10,11... | collective-permute-start | bytes 786440 | tf_op jit(solution)/shard_map/ppermute | solution.py:218
  3.3 4.9 %collective-permute-start.2 = (bf16[80,256]{1,0:T(8,128)(2,1)S(1)}, bf16[80,256]{1,0:T(8,128)(2,1)S(1)}, u32[]{:S(2)}, u32[]{:S(2)}) collective-permute-start(bf16[80,256]{1,0:T(8,128)(2,1)S(1)} %slice.20), channel_id=1, source_target_pairs={{0,2},{1,3},{2,0},{3,1},{4,6},{5,7},{6,4},{7,5},{8,10},{9,11},{10,... | collective-permute-start | bytes 122888 | tf_op jit(solution)/shard_map/ppermute | solution.py:218
  6.2 8.1 %collective-permute-start.3 = (bf16[256,512]{1,0:T(8,128)(2,1)S(1)}, bf16[256,512]{1,0:T(8,128)(2,1)S(1)}, u32[]{:S(2)}, u32[]{:S(2)}) collective-permute-start(bf16[256,512]{1,0:T(8,128)(2,1)S(1)} %copy-done.3), channel_id=1, source_target_pairs={{0,2},{1,3},{2,0},{3,1},{4,6},{5,7},{6,4},{7,5},{8,10},{9,11},{10,... | collective-permute-start | bytes 786440 | tf_op jit(solution)/shard_map/ppermute | solution.py:218
  8.0 19.1 %copy-start = (bf16[1,4,512,512]{3,2,1,0:T(8,128)(2,1)S(1)}, bf16[1,4,512,512]{3,2,1,0:T(8,128)(2,1)}, u32[]{:S(2)}) copy-start(bf16[1,4,512,512]{3,2,1,0:T(8,128)(2,1)} %tiles_ref.3) | copy-start | bytes 6291460
  8.0 19.1 %copy-start.2 = (s32[1,4]{1,0:T(1,128)S(1)}, s32[1,4]{1,0:T(1,128)}, u32[]{:S(2)}) copy-start(s32[1,4]{1,0:T(1,128)} %cols_ref.3) | copy-start | bytes 52
  8.2 4.2 %collective-permute-start.4 = (bf16[80,256]{1,0:T(8,128)(2,1)S(1)}, bf16[80,256]{1,0:T(8,128)(2,1)S(1)}, u32[]{:S(2)}, u32[]{:S(2)}) collective-permute-start(bf16[80,256]{1,0:T(8,128)(2,1)S(1)} %add_convert_fusion.1.own_ref), channel_id=1, source_target_pairs={{0,4},{4,0},{8,12},{12,8},{16,20},{20,16},{24,28},{28,24},{1,5},{5... | collective-permute-start | bytes 122888 | tf_op jit(solution)/shard_map/ppermute | solution.py:229
  10.5 7.9 %collective-permute-start.5 = (bf16[256,512]{1,0:T(8,128)(2,1)S(1)}, bf16[256,512]{1,0:T(8,128)(2,1)S(1)}, u32[]{:S(2)}, u32[]{:S(2)}) collective-permute-start(bf16[256,512]{1,0:T(8,128)(2,1)S(1)} %copy-done.3), channel_id=1, source_target_pairs={{3,4},{7,8},{11,12},{15,16},{19,20},{23,24},{27,28},{4,3},{8,7},{1... | collective-permute-start | bytes 786440 | tf_op jit(solution)/shard_map/ppermute | solution.py:311
  14.3 4.1 %collective-permute-start.6 = (bf16[256,512]{1,0:T(8,128)(2,1)S(1)}, bf16[256,512]{1,0:T(8,128)(2,1)S(1)}, u32[]{:S(2)}, u32[]{:S(2)}) collective-permute-start(bf16[256,512]{1,0:T(8,128)(2,1)S(1)} %collective-permute-done.3.across_ref.refs_2_.refs_4_), channel_id=1, source_target_pairs={{0,1},{1,0},{2,3},{3,2},{4,5},{5,4},{6,7},{7,6},{8,9},{9,8},{10,11... | collective-permute-start | bytes 786440 | tf_op jit(solution)/shard_map/ppermute | solution.py:218
  14.3 8.5 %collective-permute-start.8 = (bf16[80,256]{1,0:T(8,128)(2,1)S(1)}, bf16[80,256]{1,0:T(8,128)(2,1)S(1)}, u32[]{:S(2)}, u32[]{:S(2)}) collective-permute-start(bf16[80,256]{1,0:T(8,128)(2,1)S(1)} %get-tuple-element.53), channel_id=1, source_target_pairs={{0,8},{4,12},{8,0},{12,4},{16,24},{20,28},{24,16},{28,20},{1,9},{5... | collective-permute-start | bytes 122888 | tf_op jit(solution)/shard_map/ppermute | solution.py:328
  15.9 6.9 %collective-permute-start.9 = (bf16[80,256]{1,0:T(8,128)(2,1)S(1)}, bf16[80,256]{1,0:T(8,128)(2,1)S(1)}, u32[]{:S(2)}, u32[]{:S(2)}) collective-permute-start(bf16[80,256]{1,0:T(8,128)(2,1)S(1)} %get-tuple-element.54), channel_id=1, source_target_pairs={{0,24},{4,28},{8,16},{12,20},{16,8},{20,12},{24,0},{28,4},{1,25},{... | collective-permute-start | bytes 122888 | tf_op jit(solution)/shard_map/ppermute | solution.py:328
  18.4 6.1 %collective-permute-start.11 = (bf16[80,256]{1,0:T(8,128)(2,1)S(1)}, bf16[80,256]{1,0:T(8,128)(2,1)S(1)}, u32[]{:S(2)}, u32[]{:S(2)}) collective-permute-start(bf16[80,256]{1,0:T(8,128)(2,1)S(1)} %get-tuple-element.56), channel_id=1, source_target_pairs={{0,16},{4,20},{8,24},{12,28},{16,0},{20,4},{24,8},{28,12},{1,17},{... | collective-permute-start | bytes 122888 | tf_op jit(solution)/shard_map/ppermute | solution.py:328
  22.7 9.6 %collective-permute-start.7 = (bf16[256,512]{1,0:T(8,128)(2,1)S(1)}, bf16[256,512]{1,0:T(8,128)(2,1)S(1)}, u32[]{:S(2)}, u32[]{:S(2)}) collective-permute-start(bf16[256,512]{1,0:T(8,128)(2,1)S(1)} %pick_even.1), channel_id=1, source_target_pairs={{0,4},{8,12},{16,20},{24,28},{4,0},{12,8},{20,16},{28,24},{1,5},{9... | collective-permute-start | bytes 786440 | tf_op jit(solution)/shard_map/ppermute | solution.py:235
  23.0 9.3 %collective-permute-start.10 = (bf16[256,512]{1,0:T(8,128)(2,1)S(1)}, bf16[256,512]{1,0:T(8,128)(2,1)S(1)}, u32[]{:S(2)}, u32[]{:S(2)}) collective-permute-start(bf16[256,512]{1,0:T(8,128)(2,1)S(1)} %pick_odd.1), channel_id=1, source_target_pairs={{4,8},{12,16},{20,24},{8,4},{16,12},{24,20},{5,9},{13,17},{21,25},... | collective-permute-start | bytes 786440 | tf_op jit(solution)/shard_map/ppermute | solution.py:235
  24.6 3.8 %collective-permute-start.12 = (bf16[64,256]{1,0:T(8,128)(2,1)S(1)}, bf16[64,256]{1,0:T(8,128)(2,1)S(1)}, u32[]{:S(2)}, u32[]{:S(2)}) collective-permute-start(bf16[64,256]{1,0:T(8,128)(2,1)S(1)} %add_convert_fusion.2.field0), channel_id=1, source_target_pairs={{0,1},{1,0},{2,3},{3,2},{4,5},{5,4},{6,7},{7,6},{8,9},{9,8},{10,11... | collective-permute-start | bytes 98312 | tf_op jit(solution)/shard_map/ppermute | solution.py:218
  24.6 4.1 %collective-permute-start.13 = (bf16[64,256]{1,0:T(8,128)(2,1)S(1)}, bf16[64,256]{1,0:T(8,128)(2,1)S(1)}, u32[]{:S(2)}, u32[]{:S(2)}) collective-permute-start(bf16[64,256]{1,0:T(8,128)(2,1)S(1)} %add_convert_fusion.2.field0), channel_id=1, source_target_pairs={{0,2},{1,3},{2,0},{3,1},{4,6},{5,7},{6,4},{7,5},{8,10},{9,11},{10,... | collective-permute-start | bytes 98312 | tf_op jit(solution)/shard_map/ppermute | solution.py:218
  25.5 3.6 %collective-permute-start.14 = (bf16[64,256]{1,0:T(8,128)(2,1)S(1)}, bf16[64,256]{1,0:T(8,128)(2,1)S(1)}, u32[]{:S(2)}, u32[]{:S(2)}) collective-permute-start(bf16[64,256]{1,0:T(8,128)(2,1)S(1)} %add_convert_fusion.2.field0), channel_id=1, source_target_pairs={{0,3},{1,2},{2,1},{3,0},{4,7},{5,6},{6,5},{7,4},{8,11},{9,10},{10,... | collective-permute-start | bytes 98312 | tf_op jit(solution)/shard_map/ppermute | solution.py:218
